TPU v7x, 32 devices: a whole 2x2x4 slice. The times are simulated.
32 devices in a mesh: dp: 16 (over z, x, core), fsdp: 2 (over y).
Axes of the slice: x: 2, y: 2, z: 4, core: 2. Of those that a mesh axis runs over, the one named last changes fastest.
Arguments:
- tokens: bfloat16 [4096, 1024], P('dp'), may hold values from -8 to 8
- teacher: bfloat16 [32, 6144], P('dp'), may hold values from -8 to 8
- norm_gain: float32 [1024], replicated, may hold values from 0.25 to 1.75
- w_in: bfloat16 [1024, 4096], P(None, 'fsdp'), may hold values from -0.1875 to 0.1875
- b_in: float32 [4096], P('fsdp'), may hold values from -3 to 3
- w_out: bfloat16 [1024, 4096], P(None, 'fsdp'), may hold values from -0.09375 to 0.09375
- b_out: float32 [1024], replicated, may hold values from -3 to 3
- final_gain: float32 [1024], replicated, may hold values from 0.25 to 1.75
Outputs:
- loss_value: float32 [], replicated
- grad_in: bfloat16 [1024, 4096], P('dp', 'fsdp')
- grad_out: bfloat16 [1024, 4096], P('dp', 'fsdp')
All inputs are finite; a program needn't handle non-finite values.
Results may differ from a plain program's by a relative error of at most 0.008.
Values may be sent and summed in bfloat16 or wider, within the bound.
No kernel may reach another device: no remote copies, remote signals or barrier semaphores. Data moves between devices by JAX's collectives and lax.ppermute only.
A program may use at most 64 MiB of HBM per device.

v0:
```python
import jax
import jax.numpy as jnp
from jax import lax
from jax.experimental import pallas as pl
from jax.experimental.pallas import tpu as pltpu
from jax.sharding import PartitionSpec as P

loss_scale = 4096.0
lanes = 128
f32 = jnp.float32
bf16 = jnp.bfloat16


def gelu_tanh(values):
    inner = 0.7978845608 * (values + 0.044715 * values * values * values)
    return 0.5 * values * (1.0 + jnp.tanh(inner))


def gelu_slope(values):
    square = values * values
    tangent = jnp.tanh(0.7978845608 * (values + 0.044715 * values * square))
    return 0.5 * (1.0 + tangent) + 0.5 * values * (1.0 - tangent * tangent) * 0.7978845608 * (
        1.0 + 3.0 * 0.044715 * square
    )


def contract_last(left_side, right_side):
    return lax.dot_general(
        left_side, right_side, (((1,), (1,)), ((), ())), preferred_element_type=f32
    )


def fold_rows(values, width):
    count = values.shape[1] // width
    return jnp.concatenate(
        [
            values[i : i + 1, k * width : (k + 1) * width]
            for i in range(values.shape[0])
            for k in range(count)
        ],
        axis=0,
    )


def vmem_params(elements):
    return pltpu.CompilerParams(vmem_limit_bytes=min(56 * 2**20, 8 * elements + 8 * 2**20))


in_hbm = pl.BlockSpec(memory_space=pltpu.HBM)
in_any = pl.BlockSpec(memory_space=pl.ANY)


def hbm(value):
    return pltpu.with_memory_space_constraint(value, pltpu.HBM)


def near(value, keep):
    return pltpu.with_memory_space_constraint(value, pltpu.VMEM) if keep else value


def near_shape(shape, dtype, keep):
    return pltpu.VMEM(shape, dtype) if keep else jax.ShapeDtypeStruct(shape, dtype)


def normalize(values, gain):
    centered = values - jnp.mean(values, axis=-1, keepdims=True)
    inv_std = lax.rsqrt(jnp.mean(centered * centered, axis=-1, keepdims=True) + 1e-05)
    return (centered * inv_std * gain).astype(bf16)


def teacher_payload(first, teacher, copies, splits):
    images = teacher.shape[0]
    features = teacher.shape[1] // splits
    fold = features // 8

    def kernel(first_ref, teacher_ref, out_ref):
        start = 0
        if splits > 1:
            start = pl.multiple_of(first_ref[0] * features, features)
        folded = fold_rows(teacher_ref[:, pl.ds(start, features)].astype(f32), fold).astype(bf16)
        out_ref[...] = jnp.broadcast_to(folded[None], out_ref.shape)

    return pl.pallas_call(
        kernel,
        in_specs=[
            pl.BlockSpec(memory_space=pltpu.SMEM),
            pl.BlockSpec(memory_space=pltpu.VMEM),
        ],
        out_shape=pltpu.HBM((copies, images * 8, fold), bf16),
        compiler_params=vmem_params(copies * images * features),
        cost_estimate=pl.CostEstimate(
            flops=copies * images * features,
            bytes_accessed=2 * copies * images * features,
            transcendentals=0,
        ),
        name="teacher_payload",
    )(first, hbm(teacher))


def forward(first, tokens, norm_gain, w_in, b_in, w_out, b_out, copies, images):
    rows, width = tokens.shape
    hidden = w_in.shape[1]
    per_image = rows // images
    tile = min(512, hidden)
    steps = hidden // tile
    folds = width // lanes

    def kernel(
        first_ref, gain_ref, bias_ref, out_b_ref, tokens_any, in_any_ref, out_any_ref,
        pooled_ref, payload_ref, tokens_ref, in_ref, out_w_ref, sems,
    ):
        loads = [
            pltpu.make_async_copy(
                in_any_ref.at[:, pl.ds(j * tile, tile)], in_ref.at[j], sems.at[j]
            )
            for j in range(steps)
        ]
        loads.append(pltpu.make_async_copy(out_any_ref, out_w_ref, sems.at[steps]))
        loads.append(pltpu.make_async_copy(tokens_any, tokens_ref, sems.at[steps + 1]))
        loads[-1].start()
        for load in loads[:-1]:
            load.start()
        loads[-1].wait()
        values = tokens_ref[...].astype(f32)
        normed = normalize(values, gain_ref[...])
        token_mean = jnp.mean(values.reshape(images, per_image, width), axis=1)
        for j in range(steps):
            taken = slice(j * tile, (j + 1) * tile)
            loads[j].wait()
            pre_act = jnp.dot(normed, in_ref[j], preferred_element_type=f32) + bias_ref[:, taken]
            pooled_ref[:, taken] = jnp.mean(
                gelu_tanh(pre_act).reshape(images, per_image, tile), axis=1
            ).astype(bf16)
        loads[steps].wait()
        total = contract_last(pooled_ref[...], out_w_ref[...])
        total += jnp.where(first_ref[0] == 0, token_mean + out_b_ref[...], 0.0)
        folded = fold_rows(total, lanes).astype(bf16)
        payload_ref[...] = jnp.broadcast_to(folded[None], payload_ref.shape)

    whole = pl.BlockSpec(memory_space=pltpu.VMEM)
    payload = (copies, images * folds, lanes)
    return pl.pallas_call(
        kernel,
        in_specs=[pl.BlockSpec(memory_space=pltpu.SMEM)] + [whole] * 3 + [in_hbm] * 3,
        out_specs=[whole, whole],
        out_shape=[
            jax.ShapeDtypeStruct((images, hidden), bf16),
            pltpu.HBM(payload, bf16),
        ],
        scratch_shapes=[
            pltpu.VMEM((rows, width), bf16),
            pltpu.VMEM((steps, width, tile), bf16),
            pltpu.VMEM((width, hidden), bf16),
            pltpu.SemaphoreType.DMA((steps + 2,)),
        ],
        compiler_params=vmem_params(
            rows * width + width * hidden + copies * images * width
        ),
        cost_estimate=pl.CostEstimate(
            flops=2 * rows * width * hidden,
            bytes_accessed=4 * width * hidden,
            transcendentals=rows * hidden,
        ),
        name="forward",
    )(
        first, hbm(norm_gain[None]), hbm(b_in[None]), hbm(b_out[None]),
        hbm(tokens), hbm(w_in), hbm(w_out),
    )


def mate_slopes(share_index, blocks, norm_gain, w_in, b_in, share):
    rows, width = blocks[0].shape
    count = len(blocks)
    keep = rows <= 512

    def kernel(index_ref, *refs):
        token_refs = refs[:count]
        gain_ref, bias_ref, in_any_ref, slope_ref, turned_ref = refs[count : count + 5]
        held_ref, in_ref, sems = refs[count + 5 :]
        first_unit = pl.multiple_of(index_ref[0] * share, share)
        weight = pltpu.make_async_copy(
            in_any_ref.at[:, pl.ds(first_unit, share)], in_ref, sems.at[count]
        )
        loads = [
            pltpu.make_async_copy(token_refs[k], held_ref.at[k], sems.at[k]) for k in range(count)
        ]
        loads[0].start()
        weight.start()
        for load in loads[1:]:
            load.start()
        for k in range(count):
            taken = slice(k * rows, (k + 1) * rows)
            loads[k].wait()
            normed = normalize(held_ref[k].astype(f32), gain_ref[...])
            if k == 0:
                weight.wait()
            pre_act = jnp.dot(normed, in_ref[...], preferred_element_type=f32) + bias_ref[...]
            slope_ref[taken] = gelu_slope(pre_act).astype(bf16)
            turned_ref[:, taken] = normed.T

    return pl.pallas_call(
        kernel,
        grid_spec=pltpu.PrefetchScalarGridSpec(
            num_scalar_prefetch=1,
            grid=(1,),
            in_specs=[in_any] * count
            + [
                pl.BlockSpec((1, width), lambda j, s: (0, 0)),
                pl.BlockSpec((1, share), lambda j, s: (0, s[0])),
                in_hbm,
            ],
            out_specs=[
                pl.BlockSpec((count * rows, share), lambda j, s: (0, 0)),
                pl.BlockSpec((width, count * rows), lambda j, s: (0, 0)),
            ],
            scratch_shapes=[
                pltpu.VMEM((count, rows, width), bf16),
                pltpu.VMEM((width, share), bf16),
                pltpu.SemaphoreType.DMA((count + 1,)),
            ],
        ),
        out_shape=[
            near_shape((count * rows, share), bf16, keep),
            near_shape((width, count * rows), bf16, keep),
        ],
        compiler_params=vmem_params(count * rows * (width + share)),
        cost_estimate=pl.CostEstimate(
            flops=2 * rows * count * width * share,
            bytes_accessed=4 * rows * count * width,
            transcendentals=rows * count * share,
        ),
        name="mate_slopes",
    )(
        share_index,
        *[hbm(block) for block in blocks],
        hbm(norm_gain[None]),
        hbm(b_in[None]),
        hbm(w_in),
    )


def target_gram(arrived, images):
    senders, folded, fold = arrived.shape
    folds = senders * folded // images
    keep = images <= 64

    def kernel(arrived_ref, gram_ref, wide_ref):
        wide_ref[...] = arrived_ref[...].astype(f32).reshape(images, folds, fold)
        rows = jnp.concatenate([wide_ref[:, k, :].astype(bf16) for k in range(folds)], axis=1)
        gram_ref[...] = contract_last(rows, rows)

    return pl.pallas_call(
        kernel,
        out_shape=jax.ShapeDtypeStruct((images, images), f32),
        scratch_shapes=[pltpu.VMEM((images, folds, fold), f32)],
        compiler_params=vmem_params(images * folds * fold),
        cost_estimate=pl.CostEstimate(
            flops=2 * images * images * folds * fold,
            bytes_accessed=2 * images * folds * fold,
            transcendentals=0,
        ),
        name="target_gram",
    )(near(arrived, keep))


def unit_gram(parts):
    images = parts[0].shape[0]

    def kernel(*refs):
        gram_ref = refs[-1]
        gram = sum((ref[...] for ref in refs[1:-1]), refs[0][...])
        row = lax.broadcasted_iota(jnp.int32, gram.shape, 0)
        column = lax.broadcasted_iota(jnp.int32, gram.shape, 1)
        diagonal = jnp.where(row == column, gram, 0.0)
        down = lax.rsqrt(jnp.sum(diagonal, axis=1, keepdims=True) + 1e-06)
        across = lax.rsqrt(jnp.sum(diagonal, axis=0, keepdims=True) + 1e-06)
        gram_ref[...] = gram * down * across

    return pl.pallas_call(
        kernel,
        out_shape=jax.ShapeDtypeStruct((images, images), f32),
        compiler_params=vmem_params(4 * images * images),
        cost_estimate=pl.CostEstimate(
            flops=8 * images * images, bytes_accessed=8 * images * images, transcendentals=0
        ),
        name="unit_gram",
    )(*parts)


def backward(
    index, arrived, gram, final_gain, pooled, w_out, slopes, turns, mates, dp_size, per_image
):
    senders, folded, _ = arrived.shape
    width = w_out.shape[0]
    images = gram.shape[0]
    own_images, hidden = pooled.shape
    fsdp_size = senders // dp_size
    folds = width // lanes
    share = hidden // mates
    parts = len(turns)
    part_rows = [turned.shape[1] for turned in turns]
    mate_rows = sum(part_rows)
    out_rows = width // dp_size
    piece = min(share, 256)
    pieces = share // piece
    extra = own_images * hidden // piece
    group = max(1, 512 // out_rows)
    steps = dp_size // group
    in_rows = out_rows * pieces
    keep = images <= 64

    def kernel(index_ref, arrived_ref, gram_ref, gain_ref, pooled_ref, out_w_any, *refs):
        slope_refs, turned_refs, refs = refs[:parts], refs[parts : 2 * parts], refs[2 * parts :]
        loss_ref, dembed_ref, payload_any, wide_ref, hidden_ref = refs[:5]
        out_w_ref, payload_ref, sems = refs[5:]
        first_unit = pl.multiple_of(lax.rem(index_ref[0], mates) * share, share)
        load = pltpu.make_async_copy(
            out_w_any.at[:, pl.ds(first_unit, share)], out_w_ref, sems.at[steps]
        )
        load.start()
        embeds = arrived_ref[...].astype(f32).reshape(dp_size, fsdp_size, folded, lanes)
        wide_ref[...] = jnp.sum(embeds, axis=1).reshape(images, folds, lanes)
        embedding = jnp.concatenate([wide_ref[:, k, :] for k in range(folds)], axis=1)
        gain = gain_ref[...]
        centered = embedding - jnp.mean(embedding, axis=-1, keepdims=True)
        inv_std = lax.rsqrt(jnp.mean(centered * centered, axis=-1, keepdims=True) + 1e-05)
        normed = centered * inv_std
        scaled = normed * gain
        square = jnp.sum(scaled * scaled, axis=-1, keepdims=True) + 1e-06
        inv_norm = lax.rsqrt(square)
        unit = scaled * inv_norm
        student = unit.astype(bf16)
        resid = contract_last(student, student) - gram_ref[...]
        loss_ref[0, 0] = jnp.sum(resid * resid) / images
        dstudent = (loss_scale * 4.0 / images) * jnp.dot(
            resid.astype(bf16), student, preferred_element_type=f32
        )
        dunit = (dstudent - unit * jnp.sum(unit * dstudent, axis=-1, keepdims=True)) * inv_norm
        gain_grad = dunit * gain
        dembed = inv_std * (
            gain_grad
            - jnp.mean(gain_grad, axis=-1, keepdims=True)
            - normed * jnp.mean(gain_grad * normed, axis=-1, keepdims=True)
        )
        dembed_b = dembed.astype(bf16)
        dembed_ref[...] = dembed_b
        shape = (mates * own_images, images)
        row = lax.broadcasted_iota(jnp.int32, shape, 0)
        column = lax.broadcasted_iota(jnp.int32, shape, 1)
        owner = (row // own_images) ^ index_ref[0]
        pick = (owner * own_images + row % own_images == column).astype(f32).astype(bf16)
        mate_dembed = jnp.dot(pick, dembed_b, preferred_element_type=f32).astype(bf16)
        load.wait()
        dpooled = jnp.dot(mate_dembed, out_w_ref[...], preferred_element_type=f32) / per_image
        k = 0
        for part in range(parts):
            for j in range(part_rows[part] // per_image):
                rows = slice(k * per_image, (k + 1) * per_image)
                taken = slice(j * per_image, (j + 1) * per_image)
                hidden_ref[rows] = (
                    dpooled[k : k + 1] * slope_refs[part][taken].astype(f32)
                ).astype(bf16)
                k += 1
        folded_pooled = fold_rows(pooled_ref[...].astype(f32), piece).astype(bf16)
        stores = []
        for step in range(steps):
            taken = slice(step * group * out_rows, (step + 1) * group * out_rows)
            term, start = 0.0, 0
            for part in range(parts):
                rows = slice(start, start + part_rows[part])
                start += part_rows[part]
                term += jnp.dot(
                    turned_refs[part][taken], hidden_ref[rows], preferred_element_type=f32
                )
            term = term.astype(bf16)
            for d in range(group):
                for k in range(pieces):
                    payload_ref[step, d, k * out_rows : (k + 1) * out_rows] = term[
                        d * out_rows : (d + 1) * out_rows, k * piece : (k + 1) * piece
                    ]
                payload_ref[step, d, in_rows:] = folded_pooled
            stores.append(
                pltpu.make_async_copy(
                    payload_ref.at[step],
                    payload_any.at[pl.ds(step * group, group)],
                    sems.at[step],
                )
            )
            stores[-1].start()
        for store in stores:
            store.wait()

    whole = pl.BlockSpec(memory_space=pltpu.VMEM)
    smem = pl.BlockSpec(memory_space=pltpu.SMEM)
    return pl.pallas_call(
        kernel,
        in_specs=[smem, whole, whole, whole, whole, in_hbm] + [whole] * (2 * parts),
        out_specs=[smem, whole, in_hbm],
        out_shape=[
            jax.ShapeDtypeStruct((1, 1), f32),
            jax.ShapeDtypeStruct((images, width), bf16),
            pltpu.HBM((dp_size, in_rows + extra, piece), bf16),
        ],
        scratch_shapes=[
            pltpu.VMEM((images, folds, lanes), f32),
            pltpu.VMEM((mate_rows, share), bf16),
            pltpu.VMEM((width, share), bf16),
            pltpu.VMEM((steps, group, in_rows + extra, piece), bf16),
            pltpu.SemaphoreType.DMA((steps + 1,)),
        ],
        compiler_params=vmem_params(mate_rows * (width + share) // 2 + arrived.size),
        cost_estimate=pl.CostEstimate(
            flops=2 * mate_rows * width * share,
            bytes_accessed=2 * mate_rows * (width + share),
            transcendentals=0,
        ),
        name="backward",
    )(
        index, near(arrived, keep), gram, hbm(final_gain[None]), pooled, hbm(w_out),
        *[near(slope, keep) for slope in slopes], *[near(turned, keep) for turned in turns],
    )


def own_columns(index, dembed, out_rows):
    images, width = dembed.shape
    keep = images <= 64

    def kernel(index_ref, dembed_ref, columns_ref):
        row = lax.broadcasted_iota(jnp.int32, (out_rows, width), 0)
        column = lax.broadcasted_iota(jnp.int32, (out_rows, width), 1)
        pick = (row + index_ref[0] * out_rows == column).astype(f32).astype(bf16)
        columns_ref[...] = contract_last(pick, dembed_ref[...]).astype(bf16)

    return pl.pallas_call(
        kernel,
        in_specs=[
            pl.BlockSpec(memory_space=pltpu.SMEM),
            pl.BlockSpec(memory_space=pltpu.VMEM),
        ],
        out_shape=near_shape((out_rows, images), bf16, keep),
        compiler_params=vmem_params(images * width),
        cost_estimate=pl.CostEstimate(
            flops=2 * images * out_rows * width,
            bytes_accessed=2 * images * width,
            transcendentals=0,
        ),
        name="own_columns",
    )(index, dembed)


def finish(arrived, columns, mates, hidden):
    dp_size, _, piece = arrived.shape
    out_rows, images = columns.shape
    pieces = hidden // mates // piece
    in_rows = out_rows * pieces
    folds = hidden // piece
    keep = images <= 64

    def kernel(arrived_ref, columns_ref, in_ref, out_ref, wide_ref):
        wide_ref[...] = arrived_ref[:, in_rows:].astype(f32).reshape(images, folds, piece)
        rows = jnp.concatenate([wide_ref[:, k, :].astype(bf16) for k in range(folds)], axis=1)
        out_ref[...] = jnp.dot(columns_ref[...], rows, preferred_element_type=f32).astype(bf16)
        for q in range(mates):
            for k in range(pieces):
                taken = slice(k * out_rows, (k + 1) * out_rows)
                total = arrived_ref[q, taken].astype(f32)
                for s in range(q + mates, dp_size, mates):
                    total += arrived_ref[s, taken].astype(f32)
                start = (q * pieces + k) * piece
                in_ref[:, start : start + piece] = total.astype(bf16)

    return pl.pallas_call(
        kernel,
        out_shape=[jax.ShapeDtypeStruct((out_rows, hidden), bf16)] * 2,
        scratch_shapes=[pltpu.VMEM((images, folds, piece), f32)],
        compiler_params=vmem_params(arrived.size),
        cost_estimate=pl.CostEstimate(
            flops=2 * images * out_rows * hidden,
            bytes_accessed=2 * arrived.size,
            transcendentals=0,
        ),
        name="finish",
    )(near(arrived, keep), near(columns, keep))


def exchange(blocks, axes):
    return lax.all_to_all(blocks, axes, split_axis=0, concat_axis=0, tiled=True)


def mates_of(dp_size, hidden):
    mates = 4
    while dp_size % mates or hidden % (lanes * mates):
        mates //= 2
    return mates


def swap(value, axis, step):
    return lax.ppermute(value, axis, [(i, i ^ step) for i in range(lax.axis_size(axis))])


def after(value, other):
    return lax.optimization_barrier((value, other))[0]


def body(tokens, teacher, norm_gain, w_in, b_in, w_out, b_out, final_gain):
    dp_size = lax.axis_size("dp")
    fsdp_size = lax.axis_size("fsdp")
    images = teacher.shape[0] * dp_size
    per_image = tokens.shape[0] // teacher.shape[0]
    hidden = w_in.shape[1]
    mates = mates_of(dp_size, hidden)
    index = lax.axis_index("dp").astype(jnp.int32)[None]
    first = lax.axis_index("fsdp").astype(jnp.int32)[None]

    splits = fsdp_size if teacher.shape[1] % (fsdp_size * 8 * lanes) == 0 else 1

    blocks = {0: tokens}
    for bit in (2, 4, 1):
        if bit < mates:
            blocks[bit] = swap(tokens, "dp", bit)
    all_teacher = exchange(teacher_payload(first, teacher, dp_size, splits), "dp")
    pooled, embed_rows = forward(
        first, tokens, norm_gain, w_in, b_in, w_out, b_out, dp_size * fsdp_size, teacher.shape[0]
    )
    all_embed = exchange(embed_rows, ("dp", "fsdp"))
    gram = target_gram(after(all_teacher, [pooled] + [blocks[k] for k in (1,) if k in blocks]), images)
    for k, source, bit in ((6, 4, 2), (3, 2, 1), (5, 4, 1)):
        if k < mates:
            blocks[k] = swap(after(blocks[source], gram), "dp", bit)
    near_mates = [blocks[k] for k in range(min(mates, 6))]
    slope, turned = mate_slopes(index % mates, near_mates, norm_gain, w_in, b_in, hidden // mates)
    slopes, turns = [slope], [turned]
    if mates > 6:
        blocks[7] = swap(after(blocks[6], [slope, all_embed]), "dp", 1)
        far_mates = [blocks[6], blocks[7]]
        slope, turned = mate_slopes(
            index % mates, far_mates, norm_gain, w_in, b_in, hidden // mates
        )
        slopes, turns = slopes + [slope], turns + [turned]
    if splits == 1:
        grams = [gram]
    elif splits == 2:
        grams = [gram, after(swap(gram, "fsdp", 1), slopes[-1])]
    else:
        grams = [lax.psum(gram, "fsdp")]
    loss, dembed, parts = backward(
        index, all_embed, unit_gram(grams), final_gain, pooled, w_out, slopes, turns,
        mates, dp_size, per_image,
    )
    arrived = exchange(parts, "dp")
    columns = own_columns(index, dembed, dembed.shape[1] // dp_size)
    grad_in, grad_out = finish(arrived, columns, mates, hidden)
    return (loss[0, 0], grad_in, grad_out)


def solution(mesh):
    return jax.shard_map(
        body,
        mesh=mesh,
        in_specs=(
            P("dp", None),
            P("dp", None),
            P(),
            P(None, "fsdp"),
            P("fsdp"),
            P(None, "fsdp"),
            P(),
            P(),
        ),
        out_specs=(P(), P("dp", "fsdp"), P("dp", "fsdp")),
        check_vma=False,
    )
```

profile of v0, /device:TPU:11, one launch (start us, length us, event | category | flops | bytes accessed | tf_op | source)
XLA Modules:
  0.0 72.3 jit_solution(5080047969473648132)
XLA Ops:
  0.6 0.7 %collective-permute-start = (bf16[256,1024]{1,0:T(8,128)(2,1)}, bf16[256,1024]{1,0:T(8,128)(2,1)S(1)}, u32[]{:S(2)}, u32[]{:S(2)}) collective-permute-start(bf16[256,1024]{1,0:T(8,128)(2,1)} %refs_0_.1), channel_id=1, source_target_pairs={{0,2},{2,0},{4,6},{6,4},{8,10},{10,8},{12,14},{14,12},{16,18},{18,... | collective-permute-start | bytes 1572872 | tf_op jit(solution)/shard_map/ppermute | solution.py:498
  1.4 0.3 collective-permute-start.2
  1.6 1.4 %teacher_payload.1 = bf16[16,16,384]{2,1,0:T(8,128)(2,1)} custom-call(s32[1]{0:T(128)} %bitcast.1.first_ref, bf16[2,6144]{1,0:T(2,128)(2,1)} %teacher_ref.1), custom_call_target="tpu_custom_call" | custom-call | flops 98304 | bytes 196608 | tf_op jit(solution)/shard_map/teacher_payload/pallas_call | solution.py:83
  3.1 6.3 %all-to-all-start.1 = ((bf16[16,16,384]{2,1,0:T(8,128)(2,1)}), bf16[16,16,384]{2,1,0:T(8,128)(2,1)S(1)}, u32[]{:S(2)}, u32[]{:S(2)}) async-start(bf16[16,16,384]{2,1,0:T(8,128)(2,1)} %teacher_payload.1), calls=%async_computation.1 | async-start | bytes 393216 | tf_op jit(solution)/shard_map/all_to_all | solution.py:487
  9.3 6.4 %forward.1 = (bf16[2,2048]{1,0:T(2,128)(2,1)S(1)}, bf16[32,16,128]{2,1,0:T(8,128)(2,1)}) custom-call(s32[1]{0:T(128)} %bitcast.1.first_ref, f32[1,1024]{1,0:T(1,128)} %bitcast.9, f32[1,2048]{1,0:T(1,128)} %bitcast.7, f32[1,1024]{1,0:T(1,128)} %bitcast.11, bf16[256,1024]{1,0:T(8,128)(2,1)} %refs_0_.1, bf16[1024,2048]{1,0:T(8,128)(2,1)} %refs_6_.1, ...), custom_call_target="tpu_custom_call" | custom-call | flops 1073741824 | bytes 8388608 | tf_op jit(solution)/shard_map/forward/pallas_call | solution.py:142
  15.7 1.6 %all-to-all-done.1.arrived_ref = bf16[16,16,384]{2,1,0:T(8,128)(2,1)S(1)} async-done(((bf16[16,16,384]{2,1,0:T(8,128)(2,1)}), bf16[16,16,384]{2,1,0:T(8,128)(2,1)S(1)}, u32[]{:S(2)}, u32[]{:S(2)}) %all-to-all-start.1) | async-done | bytes 196640 | tf_op jit(solution)/shard_map/all_to_all | solution.py:487
  17.4 0.0 collective-permute-done.refs_1_
  17.4 0.0 copy-start
  17.4 0.5 target_gram.1.refs_0_
  17.9 0.0 collective-permute-done.2.refs_2_
  17.9 0.0 copy-start.1
  18.0 0.7 collective-permute-start.3
  18.7 5.8 %all-to-all-start = ((bf16[32,16,128]{2,1,0:T(8,128)(2,1)}), bf16[32,16,128]{2,1,0:T(8,128)(2,1)S(1)}, u32[]{:S(2)}, u32[]{:S(2)}) async-start(bf16[32,16,128]{2,1,0:T(8,128)(2,1)} %get-tuple-element.15), calls=%async_computation | async-start | bytes 262144 | tf_op jit(solution)/shard_map/all_to_all | solution.py:487
  24.5 1.2 %collective-permute-start.1 = (f32[32,32]{1,0:T(8,128)S(1)}, f32[32,32]{1,0:T(8,128)S(1)}, u32[]{:S(2)}, u32[]{:S(2)}) collective-permute-start(f32[32,32]{1,0:T(8,128)S(1)} %target_gram.1.refs_0_), channel_id=1, source_target_pairs={{0,1},{1,0},{2,3},{3,2},{4,5},{5,4},{6,7},{7,6},{8,9},{9,8},{10,11... | collective-permute-start | bytes 12296 | tf_op jit(solution)/shard_map/ppermute | solution.py:498
  25.7 0.0 copy-done
  25.7 0.0 copy-done.1
  25.7 0.0 collective-permute-done.3.refs_3_
  25.7 5.7 %mate_slopes.1 = (bf16[1024,512]{1,0:T(8,128)(2,1)S(1)}, bf16[1024,1024]{1,0:T(8,128)(2,1)S(1)}) custom-call(s32[1]{0:T(128)S(6)} %select_n.7.index_ref, bf16[256,1024]{1,0:T(8,128)(2,1)} %refs_0_.1, bf16[256,1024]{1,0:T(8,128)(2,1)} %copy-done, bf16[256,1024]{1,0:T(8,128)(2,1)} %copy-done.1, bf16[256,1024]{1,0:T(8,128)(2,1)} %collective-permute-done.3.refs_3_, ...), custom_call_target="tpu_custom_call" | custom-call | flops 1073741824 | bytes 4194304 | tf_op jit(solution)/shard_map/mate_slopes/pallas_call | solution.py:201
  31.4 0.0 collective-permute-done.1.refs_1_
  31.4 0.1 unit_gram.1.gram_ref
  31.5 0.0 all-to-all-done.arrived_ref
  31.5 5.3 %backward.1 = (f32[1,1]{1,0:T(1,128)}, bf16[32,1024]{1,0:T(8,128)(2,1)S(1)}, bf16[16,144,256]{2,1,0:T(8,128)(2,1)}) custom-call(s32[1]{0:T(128)} %bitcast.index_ref, bf16[32,16,128]{2,1,0:T(8,128)(2,1)S(1)} %all-to-all-done.arrived_ref, f32[32,32]{1,0:T(8,128)S(1)} %unit_gram.1.gram_ref, f32[1,1024]{1,0:T(1,128)} %bitcast.12, ...), custom_call_target="tpu_custom_call" | custom-call | flops 1073741824 | bytes 3145728 | tf_op jit(solution)/shard_map/backward/pallas_call | solution.py:395
  36.9 6.4 %all-to-all-start.2 = ((bf16[16,144,256]{2,1,0:T(8,128)(2,1)}), bf16[16,144,256]{2,1,0:T(8,128)(2,1)S(1)}, u32[]{:S(2)}, u32[]{:S(2)}) async-start(bf16[16,144,256]{2,1,0:T(8,128)(2,1)} %get-tuple-element.23), calls=%async_computation.2 | async-start | bytes 2359296 | tf_op jit(solution)/shard_map/all_to_all | solution.py:487
  43.3 0.2 own_columns.1.columns_ref
  43.5 27.6 %all-to-all-done.2.arrived_ref = bf16[16,144,256]{2,1,0:T(8,128)(2,1)S(1)} async-done(((bf16[16,144,256]{2,1,0:T(8,128)(2,1)}), bf16[16,144,256]{2,1,0:T(8,128)(2,1)S(1)}, u32[]{:S(2)}, u32[]{:S(2)}) %all-to-all-start.2) | async-done | bytes 1179680 | tf_op jit(solution)/shard_map/all_to_all | solution.py:487
  71.1 1.2 %finish.1 = (bf16[64,2048]{1,0:T(8,128)(2,1)}, bf16[64,2048]{1,0:T(8,128)(2,1)}) custom-call(bf16[16,144,256]{2,1,0:T(8,128)(2,1)S(1)} %all-to-all-done.2.arrived_ref, bf16[64,32]{1,0:T(8,128)(2,1)S(1)} %own_columns.1.columns_ref), custom_call_target="tpu_custom_call" | custom-call | flops 8388608 | bytes 1179648 | tf_op jit(solution)/shard_map/finish/pallas_call | solution.py:472
Async XLA Ops:
  0.6 16.8 %collective-permute-start = (bf16[256,1024]{1,0:T(8,128)(2,1)}, bf16[256,1024]{1,0:T(8,128)(2,1)S(1)}, u32[]{:S(2)}, u32[]{:S(2)}) collective-permute-start(bf16[256,1024]{1,0:T(8,128)(2,1)} %refs_0_.1), channel_id=1, source_target_pairs={{0,2},{2,0},{4,6},{6,4},{8,10},{10,8},{12,14},{14,12},{16,18},{18,... | collective-permute-start | bytes 1572872 | tf_op jit(solution)/shard_map/ppermute | solution.py:498
  1.4 16.6 %collective-permute-start.2 = (bf16[256,1024]{1,0:T(8,128)(2,1)}, bf16[256,1024]{1,0:T(8,128)(2,1)S(1)}, u32[]{:S(2)}, u32[]{:S(2)}) collective-permute-start(bf16[256,1024]{1,0:T(8,128)(2,1)} %refs_0_.1), channel_id=1, source_target_pairs={{0,4},{2,6},{4,0},{6,2},{8,12},{10,14},{12,8},{14,10},{16,20},{18,... | collective-permute-start | bytes 1572872 | tf_op jit(solution)/shard_map/ppermute | solution.py:498
  3.1 14.3 %all-to-all-start.1 = ((bf16[16,16,384]{2,1,0:T(8,128)(2,1)}), bf16[16,16,384]{2,1,0:T(8,128)(2,1)S(1)}, u32[]{:S(2)}, u32[]{:S(2)}) async-start(bf16[16,16,384]{2,1,0:T(8,128)(2,1)} %teacher_payload.1), calls=%async_computation.1 | async-start | bytes 393216 | tf_op jit(solution)/shard_map/all_to_all | solution.py:487
  17.4 8.3 %copy-start = (bf16[256,1024]{1,0:T(8,128)(2,1)}, bf16[256,1024]{1,0:T(8,128)(2,1)S(1)}, u32[]{:S(2)}) copy-start(bf16[256,1024]{1,0:T(8,128)(2,1)S(1)} %collective-permute-done.refs_1_) | copy-start | bytes 1572868
  17.9 7.8 %copy-start.1 = (bf16[256,1024]{1,0:T(8,128)(2,1)}, bf16[256,1024]{1,0:T(8,128)(2,1)S(1)}, u32[]{:S(2)}) copy-start(bf16[256,1024]{1,0:T(8,128)(2,1)S(1)} %collective-permute-done.2.refs_2_) | copy-start | bytes 1572868
  18.0 7.8 %collective-permute-start.3 = (bf16[256,1024]{1,0:T(8,128)(2,1)S(1)}, bf16[256,1024]{1,0:T(8,128)(2,1)}, u32[]{:S(2)}, u32[]{:S(2)}) collective-permute-start(bf16[256,1024]{1,0:T(8,128)(2,1)S(1)} %collective-permute-done.2.refs_2_), channel_id=1, source_target_pairs={{0,2},{2,0},{4,6},{6,4},{8,10},{10,8},{12,14},{14,12},{16,18},{18,... | collective-permute-start | bytes 1572872 | tf_op jit(solution)/shard_map/ppermute | solution.py:498
  18.7 12.9 %all-to-all-start = ((bf16[32,16,128]{2,1,0:T(8,128)(2,1)}), bf16[32,16,128]{2,1,0:T(8,128)(2,1)S(1)}, u32[]{:S(2)}, u32[]{:S(2)}) async-start(bf16[32,16,128]{2,1,0:T(8,128)(2,1)} %get-tuple-element.15), calls=%async_computation | async-start | bytes 262144 | tf_op jit(solution)/shard_map/all_to_all | solution.py:487
  24.5 7.0 %collective-permute-start.1 = (f32[32,32]{1,0:T(8,128)S(1)}, f32[32,32]{1,0:T(8,128)S(1)}, u32[]{:S(2)}, u32[]{:S(2)}) collective-permute-start(f32[32,32]{1,0:T(8,128)S(1)} %target_gram.1.refs_0_), channel_id=1, source_target_pairs={{0,1},{1,0},{2,3},{3,2},{4,5},{5,4},{6,7},{7,6},{8,9},{9,8},{10,11... | collective-permute-start | bytes 12296 | tf_op jit(solution)/shard_map/ppermute | solution.py:498
  36.9 34.2 %all-to-all-start.2 = ((bf16[16,144,256]{2,1,0:T(8,128)(2,1)}), bf16[16,144,256]{2,1,0:T(8,128)(2,1)S(1)}, u32[]{:S(2)}, u32[]{:S(2)}) async-start(bf16[16,144,256]{2,1,0:T(8,128)(2,1)} %get-tuple-element.23), calls=%async_computation.2 | async-start | bytes 2359296 | tf_op jit(solution)/shard_map/all_to_all | solution.py:487
where the time goes:
time: 72.8 us; the launch traced here: 72.3 us
  waiting for transfers between devices  29.2 us (40%)
  starting transfers between devices  21.4 us (29%)
  Pallas kernels  20.9 us (29%)
  between operations  0.74 us (1%)
    all_to_all x3, waiting for transfers between devices, exchange(): return lax.all_to_all(blocks, axes, split_axis=0, concat_axis=0, tiled=True)  29.2 us
    all_to_all x3, starting transfers between devices, exchange(): return lax.all_to_all(blocks, axes, split_axis=0, concat_axis=0, tiled=True)  18.4 us
    pallas_call x1, Pallas kernels, forward(): pl.pallas_call(kernel, in_specs=[pl.BlockSpec(memory_space=pltpu.SMEM)] +...  6.41 us
    pallas_call x1, Pallas kernels, mate_slopes(): pl.pallas_call(kernel, grid_spec=pltpu.PrefetchScalarGridSpec(num_scalar_...  5.69 us
    pallas_call x1, Pallas kernels, backward(): pl.pallas_call(kernel, in_specs=[smem, whole, whole, whole, whole, in_hbm...  5.34 us
    ppermute x4, starting transfers between devices, swap(): lax.ppermute(value, axis, [(i, i ^ step) for i in range(lax.axis_size(axi...  2.98 us
  transfers between devices with their start and end apart: 7, of which 2 were waited for; matrix products, arithmetic and copies ran while one was open for 0% of the time, Pallas kernels for 20%

commit v1 on v0

--- a/solution.py
+++ b/solution.py
@@ -304,18 +304,19 @@
     piece = min(share, 256)
     pieces = share // piece
     extra = own_images * hidden // piece
-    group = max(1, 512 // out_rows)
-    steps = dp_size // group
-    in_rows = out_rows * pieces
+    groups = dp_size // mates
+    group_rows = mates * out_rows
+    part_shape = (pieces * group_rows + extra, piece)
     keep = images <= 64
 
     def kernel(index_ref, arrived_ref, gram_ref, gain_ref, pooled_ref, out_w_any, *refs):
         slope_refs, turned_refs, refs = refs[:parts], refs[parts : 2 * parts], refs[2 * parts :]
-        loss_ref, dembed_ref, payload_any, wide_ref, hidden_ref = refs[:5]
-        out_w_ref, payload_ref, sems = refs[5:]
+        loss_ref, dembed_ref, refs = refs[0], refs[1], refs[2:]
+        part_refs, refs = refs[:groups], refs[groups:]
+        wide_ref, hidden_ref, out_w_ref, payload_ref, sems = refs
         first_unit = pl.multiple_of(lax.rem(index_ref[0], mates) * share, share)
         load = pltpu.make_async_copy(
-            out_w_any.at[:, pl.ds(first_unit, share)], out_w_ref, sems.at[steps]
+            out_w_any.at[:, pl.ds(first_unit, share)], out_w_ref, sems.at[0]
         )
         load.start()
         embeds = arrived_ref[...].astype(f32).reshape(dp_size, fsdp_size, folded, lanes)
@@ -363,29 +364,26 @@
                 k += 1
         folded_pooled = fold_rows(pooled_ref[...].astype(f32), piece).astype(bf16)
         stores = []
-        for step in range(steps):
-            taken = slice(step * group * out_rows, (step + 1) * group * out_rows)
+        for k in list(range(1, groups))[::-1] + [0]:
+            first_row = pl.multiple_of(
+                ((index_ref[0] // mates) ^ k) * group_rows, group_rows
+            )
             term, start = 0.0, 0
             for part in range(parts):
                 rows = slice(start, start + part_rows[part])
                 start += part_rows[part]
                 term += jnp.dot(
-                    turned_refs[part][taken], hidden_ref[rows], preferred_element_type=f32
+                    turned_refs[part][pl.ds(first_row, group_rows)],
+                    hidden_ref[rows],
+                    preferred_element_type=f32,
                 )
             term = term.astype(bf16)
-            for d in range(group):
-                for k in range(pieces):
-                    payload_ref[step, d, k * out_rows : (k + 1) * out_rows] = term[
-                        d * out_rows : (d + 1) * out_rows, k * piece : (k + 1) * piece
-                    ]
-                payload_ref[step, d, in_rows:] = folded_pooled
-            stores.append(
-                pltpu.make_async_copy(
-                    payload_ref.at[step],
-                    payload_any.at[pl.ds(step * group, group)],
-                    sems.at[step],
-                )
-            )
+            for j in range(pieces):
+                payload_ref[k, j * group_rows : (j + 1) * group_rows] = term[
+                    :, j * piece : (j + 1) * piece
+                ]
+            payload_ref[k, pieces * group_rows :] = folded_pooled
+            stores.append(pltpu.make_async_copy(payload_ref.at[k], part_refs[k], sems.at[k]))
             stores[-1].start()
         for store in stores:
             store.wait()
@@ -395,18 +393,19 @@
     return pl.pallas_call(
         kernel,
         in_specs=[smem, whole, whole, whole, whole, in_hbm] + [whole] * (2 * parts),
-        out_specs=[smem, whole, in_hbm],
+        out_specs=[smem, whole, in_any] + [in_hbm] * (groups - 1),
         out_shape=[
             jax.ShapeDtypeStruct((1, 1), f32),
             jax.ShapeDtypeStruct((images, width), bf16),
-            pltpu.HBM((dp_size, in_rows + extra, piece), bf16),
-        ],
+            near_shape(part_shape, bf16, keep),
+        ]
+        + [pltpu.HBM(part_shape, bf16)] * (groups - 1),
         scratch_shapes=[
             pltpu.VMEM((images, folds, lanes), f32),
             pltpu.VMEM((mate_rows, share), bf16),
             pltpu.VMEM((width, share), bf16),
-            pltpu.VMEM((steps, group, in_rows + extra, piece), bf16),
-            pltpu.SemaphoreType.DMA((steps + 1,)),
+            pltpu.VMEM((groups,) + part_shape, bf16),
+            pltpu.SemaphoreType.DMA((groups,)),
         ],
         compiler_params=vmem_params(mate_rows * (width + share) // 2 + arrived.size),
         cost_estimate=pl.CostEstimate(
@@ -448,39 +447,85 @@
     )(index, dembed)
 
 
-def finish(arrived, columns, mates, hidden):
-    dp_size, _, piece = arrived.shape
+def sum_groups(index, parts, mates, out_rows, extra):
+    groups = len(parts)
+    rows, piece = parts[0].shape
+    group_rows = mates * out_rows
+    pieces = (rows - extra) // group_rows
+    block = (pieces * out_rows + groups * extra, piece)
+
+    def kernel(index_ref, *refs):
+        part_refs, block_refs, total_ref = refs[:groups], refs[groups:-1], refs[-1]
+        total = part_refs[0][: rows - extra].astype(f32)
+        for part_ref in part_refs[1:]:
+            total += part_ref[: rows - extra].astype(f32)
+        total_ref[...] = total.astype(bf16)
+        for j in range(mates):
+            mate = lax.rem(index_ref[0], mates) ^ j
+            for k in range(pieces):
+                start = pl.multiple_of(k * group_rows + mate * out_rows, out_rows)
+                block_refs[j][k * out_rows : (k + 1) * out_rows] = total_ref[
+                    pl.ds(start, out_rows)
+                ]
+            for k in range(groups):
+                start = pieces * out_rows + k * extra
+                block_refs[j][start : start + extra] = part_refs[k][rows - extra :]
+
+    return pl.pallas_call(
+        kernel,
+        in_specs=[pl.BlockSpec(memory_space=pltpu.SMEM)]
+        + [pl.BlockSpec(memory_space=pltpu.VMEM)] * groups,
+        out_shape=[jax.ShapeDtypeStruct(block, bf16)] * mates,
+        scratch_shapes=[pltpu.VMEM((rows - extra, piece), bf16)],
+        compiler_params=vmem_params(groups * rows * piece),
+        cost_estimate=pl.CostEstimate(
+            flops=groups * rows * piece, bytes_accessed=4 * groups * rows * piece, transcendentals=0
+        ),
+        name="sum_groups",
+    )(index, *parts)
+
+
+def finish(index, blocks, columns, hidden, own_images):
+    mates = len(blocks)
+    rows, piece = blocks[0].shape
     out_rows, images = columns.shape
     pieces = hidden // mates // piece
     in_rows = out_rows * pieces
     folds = hidden // piece
-    keep = images <= 64
-
-    def kernel(arrived_ref, columns_ref, in_ref, out_ref, wide_ref):
-        wide_ref[...] = arrived_ref[:, in_rows:].astype(f32).reshape(images, folds, piece)
-        rows = jnp.concatenate([wide_ref[:, k, :].astype(bf16) for k in range(folds)], axis=1)
-        out_ref[...] = jnp.dot(columns_ref[...], rows, preferred_element_type=f32).astype(bf16)
-        for q in range(mates):
+    extra = own_images * folds
+    groups = (rows - in_rows) // extra
+
+    def kernel(index_ref, *refs):
+        block_refs, (columns_ref, in_ref, out_ref, wide_ref) = refs[:mates], refs[mates:]
+        for j in range(mates):
+            mate = lax.rem(index_ref[0], mates) ^ j
             for k in range(pieces):
-                taken = slice(k * out_rows, (k + 1) * out_rows)
-                total = arrived_ref[q, taken].astype(f32)
-                for s in range(q + mates, dp_size, mates):
-                    total += arrived_ref[s, taken].astype(f32)
-                start = (q * pieces + k) * piece
-                in_ref[:, start : start + piece] = total.astype(bf16)
-
-    return pl.pallas_call(
-        kernel,
+                start = pl.multiple_of((mate * pieces + k) * piece, piece)
+                in_ref[:, pl.ds(start, piece)] = block_refs[j][k * out_rows : (k + 1) * out_rows]
+            for k in range(groups):
+                sender = ((index_ref[0] // mates) ^ k) * mates + mate
+                start = in_rows + k * extra
+                taken = block_refs[j][start : start + extra].astype(f32)
+                wide_ref[pl.ds(sender * own_images, own_images)] = taken.reshape(
+                    own_images, folds, piece
+                )
+        pooled = jnp.concatenate([wide_ref[:, k, :].astype(bf16) for k in range(folds)], axis=1)
+        out_ref[...] = jnp.dot(columns_ref[...], pooled, preferred_element_type=f32).astype(bf16)
+
+    return pl.pallas_call(
+        kernel,
+        in_specs=[pl.BlockSpec(memory_space=pltpu.SMEM)]
+        + [pl.BlockSpec(memory_space=pltpu.VMEM)] * (mates + 1),
         out_shape=[jax.ShapeDtypeStruct((out_rows, hidden), bf16)] * 2,
         scratch_shapes=[pltpu.VMEM((images, folds, piece), f32)],
-        compiler_params=vmem_params(arrived.size),
+        compiler_params=vmem_params(2 * images * folds * piece + out_rows * hidden),
         cost_estimate=pl.CostEstimate(
             flops=2 * images * out_rows * hidden,
-            bytes_accessed=2 * arrived.size,
+            bytes_accessed=2 * mates * rows * piece,
             transcendentals=0,
         ),
         name="finish",
-    )(near(arrived, keep), near(columns, keep))
+    )(index, *blocks, columns)
 
 
 def exchange(blocks, axes):
@@ -543,13 +588,17 @@
         grams = [gram, after(swap(gram, "fsdp", 1), slopes[-1])]
     else:
         grams = [lax.psum(gram, "fsdp")]
-    loss, dembed, parts = backward(
+    loss, dembed, *parts = backward(
         index, all_embed, unit_gram(grams), final_gain, pooled, w_out, slopes, turns,
         mates, dp_size, per_image,
     )
-    arrived = exchange(parts, "dp")
-    columns = own_columns(index, dembed, dembed.shape[1] // dp_size)
-    grad_in, grad_out = finish(arrived, columns, mates, hidden)
+    out_rows = dembed.shape[1] // dp_size
+    parts = [parts[0]] + [swap(part, "dp", (k + 1) * mates) for k, part in enumerate(parts[1:])]
+    columns = own_columns(index, dembed, out_rows)
+    extra = teacher.shape[0] * hidden // parts[0].shape[1]
+    shares = sum_groups(index, parts, mates, out_rows, extra)
+    shares = [shares[0]] + [swap(part, "dp", j + 1) for j, part in enumerate(shares[1:])]
+    grad_in, grad_out = finish(index, shares, columns, hidden, teacher.shape[0])
     return (loss[0, 0], grad_in, grad_out)
 
 

time: 72.8 us -> 73.3 us (level)
  the two profiles are of different devices: /device:TPU:11 before, /device:TPU:9 now
where the time goes in v1:
time: 73.3 us; the launch traced here: 72.8 us
  waiting for transfers between devices  29.7 us (41%)
  starting transfers between devices  21.3 us (29%)
  Pallas kernels  21.1 us (29%)
  between operations  0.76 us (1%)
    ppermute x10, waiting for transfers between devices, swap(): lax.ppermute(value, axis, [(i, i ^ step) for i in range(lax.axis_size(axi...  28 us
    all_to_all x2, starting transfers between devices, exchange(): return lax.all_to_all(blocks, axes, split_axis=0, concat_axis=0, tiled=True)  11.3 us
    ppermute x10, starting transfers between devices, swap(): lax.ppermute(value, axis, [(i, i ^ step) for i in range(lax.axis_size(axi...  10 us
    pallas_call x1, Pallas kernels, forward(): pl.pallas_call(kernel, in_specs=[pl.BlockSpec(memory_space=pltpu.SMEM)] +...  6.41 us
    pallas_call x1, Pallas kernels, mate_slopes(): pl.pallas_call(kernel, grid_spec=pltpu.PrefetchScalarGridSpec(num_scalar_...  5.69 us
    pallas_call x1, Pallas kernels, backward(): pl.pallas_call(kernel, in_specs=[smem, whole, whole, whole, whole, in_hbm...  5.32 us
    all_to_all x2, waiting for transfers between devices, exchange(): return lax.all_to_all(blocks, axes, split_axis=0, concat_axis=0, tiled=True)  1.74 us
  transfers between devices with their start and end apart: 12, of which 6 were waited for; matrix products, arithmetic and copies ran while one was open for 0% of the time, Pallas kernels for 20%

profile of v1, /device:TPU:9, one launch (start us, length us, event | category | flops | bytes accessed | tf_op | source)
XLA Modules:
  0.0 72.8 jit_solution(5764447490627112424)
XLA Ops:
  0.6 0.7 %collective-permute-start = (bf16[256,1024]{1,0:T(8,128)(2,1)}, bf16[256,1024]{1,0:T(8,128)(2,1)S(1)}, u32[]{:S(2)}, u32[]{:S(2)}) collective-permute-start(bf16[256,1024]{1,0:T(8,128)(2,1)} %refs_0_.1), channel_id=1, source_target_pairs={{0,2},{2,0},{4,6},{6,4},{8,10},{10,8},{12,14},{14,12},{16,18},{18,... | collective-permute-start | bytes 1572872 | tf_op jit(solution)/shard_map/ppermute | solution.py:543
  1.4 1.2 %collective-permute-start.2 = (bf16[256,1024]{1,0:T(8,128)(2,1)}, bf16[256,1024]{1,0:T(8,128)(2,1)S(1)}, u32[]{:S(2)}, u32[]{:S(2)}) collective-permute-start(bf16[256,1024]{1,0:T(8,128)(2,1)} %refs_0_.1), channel_id=1, source_target_pairs={{0,4},{2,6},{4,0},{6,2},{8,12},{10,14},{12,8},{14,10},{16,20},{18,... | collective-permute-start | bytes 1572872 | tf_op jit(solution)/shard_map/ppermute | solution.py:543
  2.6 1.4 %teacher_payload.1 = bf16[16,16,384]{2,1,0:T(8,128)(2,1)} custom-call(s32[1]{0:T(128)} %bitcast.1.first_ref, bf16[2,6144]{1,0:T(2,128)(2,1)} %teacher_ref.1), custom_call_target="tpu_custom_call" | custom-call | flops 98304 | bytes 196608 | tf_op jit(solution)/shard_map/teacher_payload/pallas_call | solution.py:83
  4.0 5.3 %all-to-all-start.1 = ((bf16[16,16,384]{2,1,0:T(8,128)(2,1)}), bf16[16,16,384]{2,1,0:T(8,128)(2,1)S(1)}, u32[]{:S(2)}, u32[]{:S(2)}) async-start(bf16[16,16,384]{2,1,0:T(8,128)(2,1)} %teacher_payload.1), calls=%async_computation.1 | async-start | bytes 393216 | tf_op jit(solution)/shard_map/all_to_all | solution.py:532
  9.4 6.4 %forward.1 = (bf16[2,2048]{1,0:T(2,128)(2,1)S(1)}, bf16[32,16,128]{2,1,0:T(8,128)(2,1)}) custom-call(s32[1]{0:T(128)} %bitcast.1.first_ref, f32[1,1024]{1,0:T(1,128)} %bitcast.9, f32[1,2048]{1,0:T(1,128)} %bitcast.7, f32[1,1024]{1,0:T(1,128)} %bitcast.11, bf16[256,1024]{1,0:T(8,128)(2,1)} %refs_0_.1, bf16[1024,2048]{1,0:T(8,128)(2,1)} %refs_6_.1, ...), custom_call_target="tpu_custom_call" | custom-call | flops 1073741824 | bytes 8388608 | tf_op jit(solution)/shard_map/forward/pallas_call | solution.py:142
  15.8 1.7 %all-to-all-done.1.arrived_ref = bf16[16,16,384]{2,1,0:T(8,128)(2,1)S(1)} async-done(((bf16[16,16,384]{2,1,0:T(8,128)(2,1)}), bf16[16,16,384]{2,1,0:T(8,128)(2,1)S(1)}, u32[]{:S(2)}, u32[]{:S(2)}) %all-to-all-start.1) | async-done | bytes 196640 | tf_op jit(solution)/shard_map/all_to_all | solution.py:532
  17.5 0.0 collective-permute-done.refs_1_
  17.5 0.0 copy-start
  17.5 0.5 target_gram.1.refs_0_
  18.1 0.0 collective-permute-done.2.refs_2_
  18.1 0.0 copy-start.1
  18.1 0.5 collective-permute-start.3
  18.5 5.9 %all-to-all-start = ((bf16[32,16,128]{2,1,0:T(8,128)(2,1)}), bf16[32,16,128]{2,1,0:T(8,128)(2,1)S(1)}, u32[]{:S(2)}, u32[]{:S(2)}) async-start(bf16[32,16,128]{2,1,0:T(8,128)(2,1)} %get-tuple-element.22), calls=%async_computation | async-start | bytes 262144 | tf_op jit(solution)/shard_map/all_to_all | solution.py:532
  24.5 1.2 %collective-permute-start.1 = (f32[32,32]{1,0:T(8,128)S(1)}, f32[32,32]{1,0:T(8,128)S(1)}, u32[]{:S(2)}, u32[]{:S(2)}) collective-permute-start(f32[32,32]{1,0:T(8,128)S(1)} %target_gram.1.refs_0_), channel_id=1, source_target_pairs={{0,1},{1,0},{2,3},{3,2},{4,5},{5,4},{6,7},{7,6},{8,9},{9,8},{10,11... | collective-permute-start | bytes 12296 | tf_op jit(solution)/shard_map/ppermute | solution.py:543
  25.8 0.0 copy-done
  25.8 0.0 copy-done.1
  25.8 0.0 collective-permute-done.3.refs_3_
  25.8 5.7 %mate_slopes.1 = (bf16[1024,512]{1,0:T(8,128)(2,1)S(1)}, bf16[1024,1024]{1,0:T(8,128)(2,1)S(1)}) custom-call(s32[1]{0:T(128)S(6)} %select_n.7.index_ref, bf16[256,1024]{1,0:T(8,128)(2,1)} %refs_0_.1, bf16[256,1024]{1,0:T(8,128)(2,1)} %copy-done, bf16[256,1024]{1,0:T(8,128)(2,1)} %copy-done.1, bf16[256,1024]{1,0:T(8,128)(2,1)} %collective-permute-done.3.refs_3_, ...), custom_call_target="tpu_custom_call" | custom-call | flops 1073741824 | bytes 4194304 | tf_op jit(solution)/shard_map/mate_slopes/pallas_call | solution.py:201
  31.5 0.0 collective-permute-done.1.refs_1_
  31.5 0.1 unit_gram.1.gram_ref
  31.6 0.0 all-to-all-done.arrived_ref
  31.6 5.3 %backward.1 = (f32[1,1]{1,0:T(1,128)}, bf16[32,1024]{1,0:T(8,128)(2,1)S(1)}, bf16[528,256]{1,0:T(8,128)(2,1)S(1)}, bf16[528,256]{1,0:T(8,128)(2,1)}, bf16[528,256]{1,0:T(8,128)(2,1)}, /*index=5*/bf16[528,256]{1,0:T(8,128)(2,1)}) custom-call(s32[1]{0:T(128)} %bitcast.index_ref, bf16[32,16,128]{2,1,0:T(8,128)(2,1)S(1)} %all-to-all-done.arrived_ref, ...), custom_call_target="tpu_custom_call" | custom-call | flops 1073741824 | bytes 3145728 | tf_op jit(solution)/shard_map/backward/pallas_call | solution.py:393
  36.9 1.0 %collective-permute-start.4 = (bf16[528,256]{1,0:T(8,128)(2,1)}, bf16[528,256]{1,0:T(8,128)(2,1)S(1)}, u32[]{:S(2)}, u32[]{:S(2)}) collective-permute-start(bf16[528,256]{1,0:T(8,128)(2,1)} %get-tuple-element.31), channel_id=1, source_target_pairs={{0,8},{2,10},{4,12},{6,14},{8,0},{10,2},{12,4},{14,6},{16,24},{18,... | collective-permute-start | bytes 811016 | tf_op jit(solution)/shard_map/ppermute | solution.py:543
  37.9 1.5 %collective-permute-start.5 = (bf16[528,256]{1,0:T(8,128)(2,1)}, bf16[528,256]{1,0:T(8,128)(2,1)S(1)}, u32[]{:S(2)}, u32[]{:S(2)}) collective-permute-start(bf16[528,256]{1,0:T(8,128)(2,1)} %get-tuple-element.32), channel_id=1, source_target_pairs={{0,16},{2,18},{4,20},{6,22},{8,24},{10,26},{12,28},{14,30},{16,0},... | collective-permute-start | bytes 811016 | tf_op jit(solution)/shard_map/ppermute | solution.py:543
  39.4 0.3 collective-permute-start.6
  39.6 8.4 %collective-permute-done.4.refs_1_ = bf16[528,256]{1,0:T(8,128)(2,1)S(1)} collective-permute-done((bf16[528,256]{1,0:T(8,128)(2,1)}, bf16[528,256]{1,0:T(8,128)(2,1)S(1)}, u32[]{:S(2)}, u32[]{:S(2)}) %collective-permute-start.4) | collective-permute-done | bytes 270368 | tf_op jit(solution)/shard_map/ppermute | solution.py:543
  48.0 3.3 %collective-permute-done.5.refs_2_ = bf16[528,256]{1,0:T(8,128)(2,1)S(1)} collective-permute-done((bf16[528,256]{1,0:T(8,128)(2,1)}, bf16[528,256]{1,0:T(8,128)(2,1)S(1)}, u32[]{:S(2)}, u32[]{:S(2)}) %collective-permute-start.5) | collective-permute-done | bytes 270368 | tf_op jit(solution)/shard_map/ppermute | solution.py:543
  51.3 11.6 %collective-permute-done.6.refs_3_ = bf16[528,256]{1,0:T(8,128)(2,1)S(1)} collective-permute-done((bf16[528,256]{1,0:T(8,128)(2,1)}, bf16[528,256]{1,0:T(8,128)(2,1)S(1)}, u32[]{:S(2)}, u32[]{:S(2)}) %collective-permute-start.6) | collective-permute-done | bytes 270368 | tf_op jit(solution)/shard_map/ppermute | solution.py:543
  62.8 0.2 sum_groups.1
  63.1 1.9 %collective-permute-start.7 = (bf16[192,256]{1,0:T(8,128)(2,1)S(1)}, bf16[192,256]{1,0:T(8,128)(2,1)S(1)}, u32[]{:S(2)}, u32[]{:S(2)}) collective-permute-start(bf16[192,256]{1,0:T(8,128)(2,1)S(1)} %get-tuple-element.35), channel_id=1, source_target_pairs={{0,2},{2,0},{4,6},{6,4},{8,10},{10,8},{12,14},{14,12},{16,18},{18,... | collective-permute-start | bytes 294920 | tf_op jit(solution)/shard_map/ppermute | solution.py:543
  65.0 1.2 %collective-permute-start.8 = (bf16[192,256]{1,0:T(8,128)(2,1)S(1)}, bf16[192,256]{1,0:T(8,128)(2,1)S(1)}, u32[]{:S(2)}, u32[]{:S(2)}) collective-permute-start(bf16[192,256]{1,0:T(8,128)(2,1)S(1)} %get-tuple-element.36), channel_id=1, source_target_pairs={{0,4},{2,6},{4,0},{6,2},{8,12},{10,14},{12,8},{14,10},{16,20},{18,... | collective-permute-start | bytes 294920 | tf_op jit(solution)/shard_map/ppermute | solution.py:543
  66.2 0.5 collective-permute-start.9
  66.7 0.2 own_columns.1.refs_4_
  66.9 0.0 collective-permute-done.7.refs_1_
  66.9 2.5 %collective-permute-done.8.refs_2_ = bf16[192,256]{1,0:T(8,128)(2,1)S(1)} collective-permute-done((bf16[192,256]{1,0:T(8,128)(2,1)S(1)}, bf16[192,256]{1,0:T(8,128)(2,1)S(1)}, u32[]{:S(2)}, u32[]{:S(2)}) %collective-permute-start.8) | collective-permute-done | bytes 98336 | tf_op jit(solution)/shard_map/ppermute | solution.py:543
  69.4 2.3 %collective-permute-done.9.refs_3_ = bf16[192,256]{1,0:T(8,128)(2,1)S(1)} collective-permute-done((bf16[192,256]{1,0:T(8,128)(2,1)S(1)}, bf16[192,256]{1,0:T(8,128)(2,1)S(1)}, u32[]{:S(2)}, u32[]{:S(2)}) %collective-permute-start.9) | collective-permute-done | bytes 98336 | tf_op jit(solution)/shard_map/ppermute | solution.py:543
  71.6 1.2 %finish.1 = (bf16[64,2048]{1,0:T(8,128)(2,1)}, bf16[64,2048]{1,0:T(8,128)(2,1)}) custom-call(s32[1]{0:T(128)} %bitcast.index_ref, bf16[192,256]{1,0:T(8,128)(2,1)S(1)} %get-tuple-element.34.refs_0_, bf16[192,256]{1,0:T(8,128)(2,1)S(1)} %collective-permute-done.7.refs_1_, bf16[192,256]{1,0:T(8,128)(2,1)S(1)} %collective-permute-done.8.refs_2_, ...), custom_call_target="tpu_custom_call" | custom-call | flops 8388608 | bytes 393216 | tf_op jit(solution)/shard_map/finish/pallas_call | solution.py:515
Async XLA Ops:
  0.6 16.9 %collective-permute-start = (bf16[256,1024]{1,0:T(8,128)(2,1)}, bf16[256,1024]{1,0:T(8,128)(2,1)S(1)}, u32[]{:S(2)}, u32[]{:S(2)}) collective-permute-start(bf16[256,1024]{1,0:T(8,128)(2,1)} %refs_0_.1), channel_id=1, source_target_pairs={{0,2},{2,0},{4,6},{6,4},{8,10},{10,8},{12,14},{14,12},{16,18},{18,... | collective-permute-start | bytes 1572872 | tf_op jit(solution)/shard_map/ppermute | solution.py:543
  1.4 16.7 %collective-permute-start.2 = (bf16[256,1024]{1,0:T(8,128)(2,1)}, bf16[256,1024]{1,0:T(8,128)(2,1)S(1)}, u32[]{:S(2)}, u32[]{:S(2)}) collective-permute-start(bf16[256,1024]{1,0:T(8,128)(2,1)} %refs_0_.1), channel_id=1, source_target_pairs={{0,4},{2,6},{4,0},{6,2},{8,12},{10,14},{12,8},{14,10},{16,20},{18,... | collective-permute-start | bytes 1572872 | tf_op jit(solution)/shard_map/ppermute | solution.py:543
  4.0 13.5 %all-to-all-start.1 = ((bf16[16,16,384]{2,1,0:T(8,128)(2,1)}), bf16[16,16,384]{2,1,0:T(8,128)(2,1)S(1)}, u32[]{:S(2)}, u32[]{:S(2)}) async-start(bf16[16,16,384]{2,1,0:T(8,128)(2,1)} %teacher_payload.1), calls=%async_computation.1 | async-start | bytes 393216 | tf_op jit(solution)/shard_map/all_to_all | solution.py:532
  17.5 8.2 %copy-start = (bf16[256,1024]{1,0:T(8,128)(2,1)}, bf16[256,1024]{1,0:T(8,128)(2,1)S(1)}, u32[]{:S(2)}) copy-start(bf16[256,1024]{1,0:T(8,128)(2,1)S(1)} %collective-permute-done.refs_1_) | copy-start | bytes 1572868
  18.1 7.7 %copy-start.1 = (bf16[256,1024]{1,0:T(8,128)(2,1)}, bf16[256,1024]{1,0:T(8,128)(2,1)S(1)}, u32[]{:S(2)}) copy-start(bf16[256,1024]{1,0:T(8,128)(2,1)S(1)} %collective-permute-done.2.refs_2_) | copy-start | bytes 1572868
  18.1 7.7 %collective-permute-start.3 = (bf16[256,1024]{1,0:T(8,128)(2,1)S(1)}, bf16[256,1024]{1,0:T(8,128)(2,1)}, u32[]{:S(2)}, u32[]{:S(2)}) collective-permute-start(bf16[256,1024]{1,0:T(8,128)(2,1)S(1)} %collective-permute-done.2.refs_2_), channel_id=1, source_target_pairs={{0,2},{2,0},{4,6},{6,4},{8,10},{10,8},{12,14},{14,12},{16,18},{18,... | collective-permute-start | bytes 1572872 | tf_op jit(solution)/shard_map/ppermute | solution.py:543
  18.5 13.0 %all-to-all-start = ((bf16[32,16,128]{2,1,0:T(8,128)(2,1)}), bf16[32,16,128]{2,1,0:T(8,128)(2,1)S(1)}, u32[]{:S(2)}, u32[]{:S(2)}) async-start(bf16[32,16,128]{2,1,0:T(8,128)(2,1)} %get-tuple-element.22), calls=%async_computation | async-start | bytes 262144 | tf_op jit(solution)/shard_map/all_to_all | solution.py:532
  24.5 7.0 %collective-permute-start.1 = (f32[32,32]{1,0:T(8,128)S(1)}, f32[32,32]{1,0:T(8,128)S(1)}, u32[]{:S(2)}, u32[]{:S(2)}) collective-permute-start(f32[32,32]{1,0:T(8,128)S(1)} %target_gram.1.refs_0_), channel_id=1, source_target_pairs={{0,1},{1,0},{2,3},{3,2},{4,5},{5,4},{6,7},{7,6},{8,9},{9,8},{10,11... | collective-permute-start | bytes 12296 | tf_op jit(solution)/shard_map/ppermute | solution.py:543
  36.9 11.1 %collective-permute-start.4 = (bf16[528,256]{1,0:T(8,128)(2,1)}, bf16[528,256]{1,0:T(8,128)(2,1)S(1)}, u32[]{:S(2)}, u32[]{:S(2)}) collective-permute-start(bf16[528,256]{1,0:T(8,128)(2,1)} %get-tuple-element.31), channel_id=1, source_target_pairs={{0,8},{2,10},{4,12},{6,14},{8,0},{10,2},{12,4},{14,6},{16,24},{18,... | collective-permute-start | bytes 811016 | tf_op jit(solution)/shard_map/ppermute | solution.py:543
  37.9 13.4 %collective-permute-start.5 = (bf16[528,256]{1,0:T(8,128)(2,1)}, bf16[528,256]{1,0:T(8,128)(2,1)S(1)}, u32[]{:S(2)}, u32[]{:S(2)}) collective-permute-start(bf16[528,256]{1,0:T(8,128)(2,1)} %get-tuple-element.32), channel_id=1, source_target_pairs={{0,16},{2,18},{4,20},{6,22},{8,24},{10,26},{12,28},{14,30},{16,0},... | collective-permute-start | bytes 811016 | tf_op jit(solution)/shard_map/ppermute | solution.py:543
  39.4 23.5 %collective-permute-start.6 = (bf16[528,256]{1,0:T(8,128)(2,1)}, bf16[528,256]{1,0:T(8,128)(2,1)S(1)}, u32[]{:S(2)}, u32[]{:S(2)}) collective-permute-start(bf16[528,256]{1,0:T(8,128)(2,1)} %get-tuple-element.33), channel_id=1, source_target_pairs={{0,24},{2,26},{4,28},{6,30},{8,16},{10,18},{12,20},{14,22},{16,8},... | collective-permute-start | bytes 811016 | tf_op jit(solution)/shard_map/ppermute | solution.py:543
  63.1 3.8 %collective-permute-start.7 = (bf16[192,256]{1,0:T(8,128)(2,1)S(1)}, bf16[192,256]{1,0:T(8,128)(2,1)S(1)}, u32[]{:S(2)}, u32[]{:S(2)}) collective-permute-start(bf16[192,256]{1,0:T(8,128)(2,1)S(1)} %get-tuple-element.35), channel_id=1, source_target_pairs={{0,2},{2,0},{4,6},{6,4},{8,10},{10,8},{12,14},{14,12},{16,18},{18,... | collective-permute-start | bytes 294920 | tf_op jit(solution)/shard_map/ppermute | solution.py:543
  65.0 4.4 %collective-permute-start.8 = (bf16[192,256]{1,0:T(8,128)(2,1)S(1)}, bf16[192,256]{1,0:T(8,128)(2,1)S(1)}, u32[]{:S(2)}, u32[]{:S(2)}) collective-permute-start(bf16[192,256]{1,0:T(8,128)(2,1)S(1)} %get-tuple-element.36), channel_id=1, source_target_pairs={{0,4},{2,6},{4,0},{6,2},{8,12},{10,14},{12,8},{14,10},{16,20},{18,... | collective-permute-start | bytes 294920 | tf_op jit(solution)/shard_map/ppermute | solution.py:543
  66.2 5.4 %collective-permute-start.9 = (bf16[192,256]{1,0:T(8,128)(2,1)S(1)}, bf16[192,256]{1,0:T(8,128)(2,1)S(1)}, u32[]{:S(2)}, u32[]{:S(2)}) collective-permute-start(bf16[192,256]{1,0:T(8,128)(2,1)S(1)} %get-tuple-element.37), channel_id=1, source_target_pairs={{0,6},{2,4},{4,2},{6,0},{8,14},{10,12},{12,10},{14,8},{16,22},{18,... | collective-permute-start | bytes 294920 | tf_op jit(solution)/shard_map/ppermute | solution.py:543

commit v2 on v1

--- a/solution.py
+++ b/solution.py
@@ -288,7 +288,7 @@
 
 
 def backward(
-    index, arrived, gram, final_gain, pooled, w_out, slopes, turns, mates, dp_size, per_image
+    index, arrived, gram, final_gain, pooled, w_out, slopes, turns, sends, mates, dp_size, per_image
 ):
     senders, folded, _ = arrived.shape
     width = w_out.shape[0]
@@ -306,14 +306,18 @@
     extra = own_images * hidden // piece
     groups = dp_size // mates
     group_rows = mates * out_rows
-    part_shape = (pieces * group_rows + extra, piece)
+    shapes = [
+        (len(send) * group_rows + (extra if i < groups else 0), piece)
+        for i, send in enumerate(sends)
+    ]
     keep = images <= 64
 
     def kernel(index_ref, arrived_ref, gram_ref, gain_ref, pooled_ref, out_w_any, *refs):
         slope_refs, turned_refs, refs = refs[:parts], refs[parts : 2 * parts], refs[2 * parts :]
         loss_ref, dembed_ref, refs = refs[0], refs[1], refs[2:]
-        part_refs, refs = refs[:groups], refs[groups:]
-        wide_ref, hidden_ref, out_w_ref, payload_ref, sems = refs
+        part_refs, refs = refs[: len(sends)], refs[len(sends) :]
+        wide_ref, hidden_ref, out_w_ref, sems = refs[:4]
+        payload_refs = refs[4:]
         first_unit = pl.multiple_of(lax.rem(index_ref[0], mates) * share, share)
         load = pltpu.make_async_copy(
             out_w_any.at[:, pl.ds(first_unit, share)], out_w_ref, sems.at[0]
@@ -378,12 +382,16 @@
                     preferred_element_type=f32,
                 )
             term = term.astype(bf16)
-            for j in range(pieces):
-                payload_ref[k, j * group_rows : (j + 1) * group_rows] = term[
-                    :, j * piece : (j + 1) * piece
-                ]
-            payload_ref[k, pieces * group_rows :] = folded_pooled
-            stores.append(pltpu.make_async_copy(payload_ref.at[k], part_refs[k], sems.at[k]))
+            for i, send in enumerate(sends):
+                for at, (group, j) in enumerate(send):
+                    if group == k:
+                        payload_refs[i][at * group_rows : (at + 1) * group_rows] = term[
+                            :, j * piece : (j + 1) * piece
+                        ]
+        for i, send in enumerate(sends):
+            if i < groups:
+                payload_refs[i][len(send) * group_rows :] = folded_pooled
+            stores.append(pltpu.make_async_copy(payload_refs[i], part_refs[i], sems.at[i]))
             stores[-1].start()
         for store in stores:
             store.wait()
@@ -393,20 +401,22 @@
     return pl.pallas_call(
         kernel,
         in_specs=[smem, whole, whole, whole, whole, in_hbm] + [whole] * (2 * parts),
-        out_specs=[smem, whole, in_any] + [in_hbm] * (groups - 1),
+        out_specs=[smem, whole] + [in_any] * len(sends),
         out_shape=[
             jax.ShapeDtypeStruct((1, 1), f32),
             jax.ShapeDtypeStruct((images, width), bf16),
-            near_shape(part_shape, bf16, keep),
         ]
-        + [pltpu.HBM(part_shape, bf16)] * (groups - 1),
+        + [
+            near_shape(shape, bf16, keep) if i in (0, groups) else pltpu.HBM(shape, bf16)
+            for i, shape in enumerate(shapes)
+        ],
         scratch_shapes=[
             pltpu.VMEM((images, folds, lanes), f32),
             pltpu.VMEM((mate_rows, share), bf16),
             pltpu.VMEM((width, share), bf16),
-            pltpu.VMEM((groups,) + part_shape, bf16),
-            pltpu.SemaphoreType.DMA((groups,)),
-        ],
+            pltpu.SemaphoreType.DMA((len(sends),)),
+        ]
+        + [pltpu.VMEM(shape, bf16) for shape in shapes],
         compiler_params=vmem_params(mate_rows * (width + share) // 2 + arrived.size),
         cost_estimate=pl.CostEstimate(
             flops=2 * mate_rows * width * share,
@@ -447,19 +457,39 @@
     )(index, dembed)
 
 
-def sum_groups(index, parts, mates, out_rows, extra):
-    groups = len(parts)
-    rows, piece = parts[0].shape
+def add_pair(kept, arrived, start):
+    rows, _ = kept.shape
+
+    def kernel(kept_ref, arrived_ref, sum_ref):
+        sum_ref[...] = (
+            kept_ref[...].astype(f32) + arrived_ref[start : start + rows].astype(f32)
+        ).astype(bf16)
+
+    return pl.pallas_call(
+        kernel,
+        out_shape=jax.ShapeDtypeStruct(kept.shape, bf16),
+        compiler_params=vmem_params(kept.size + arrived.size),
+        cost_estimate=pl.CostEstimate(
+            flops=kept.size, bytes_accessed=6 * kept.size, transcendentals=0
+        ),
+        name="add_pair",
+    )(kept, arrived)
+
+
+def sum_groups(index, parts, sources, pooled_at, mates, out_rows, extra):
+    piece = parts[0].shape[1]
     group_rows = mates * out_rows
-    pieces = (rows - extra) // group_rows
-    block = (pieces * out_rows + groups * extra, piece)
+    pieces = len(sources)
+    block = (pieces * out_rows + len(pooled_at) * extra, piece)
 
     def kernel(index_ref, *refs):
-        part_refs, block_refs, total_ref = refs[:groups], refs[groups:-1], refs[-1]
-        total = part_refs[0][: rows - extra].astype(f32)
-        for part_ref in part_refs[1:]:
-            total += part_ref[: rows - extra].astype(f32)
-        total_ref[...] = total.astype(bf16)
+        part_refs, refs = refs[: len(parts)], refs[len(parts) :]
+        block_refs, total_ref = refs[:-1], refs[-1]
+        for j in range(pieces):
+            total = 0.0
+            for at, start in sources[j]:
+                total += part_refs[at][start : start + group_rows].astype(f32)
+            total_ref[j * group_rows : (j + 1) * group_rows] = total.astype(bf16)
         for j in range(mates):
             mate = lax.rem(index_ref[0], mates) ^ j
             for k in range(pieces):
@@ -467,19 +497,21 @@
                 block_refs[j][k * out_rows : (k + 1) * out_rows] = total_ref[
                     pl.ds(start, out_rows)
                 ]
-            for k in range(groups):
+            for k, (at, first) in enumerate(pooled_at):
                 start = pieces * out_rows + k * extra
-                block_refs[j][start : start + extra] = part_refs[k][rows - extra :]
+                block_refs[j][start : start + extra] = part_refs[at][first : first + extra]
 
     return pl.pallas_call(
         kernel,
         in_specs=[pl.BlockSpec(memory_space=pltpu.SMEM)]
-        + [pl.BlockSpec(memory_space=pltpu.VMEM)] * groups,
+        + [pl.BlockSpec(memory_space=pltpu.VMEM)] * len(parts),
         out_shape=[jax.ShapeDtypeStruct(block, bf16)] * mates,
-        scratch_shapes=[pltpu.VMEM((rows - extra, piece), bf16)],
-        compiler_params=vmem_params(groups * rows * piece),
-        cost_estimate=pl.CostEstimate(
-            flops=groups * rows * piece, bytes_accessed=4 * groups * rows * piece, transcendentals=0
+        scratch_shapes=[pltpu.VMEM((pieces * group_rows, piece), bf16)],
+        compiler_params=vmem_params(sum(part.size for part in parts)),
+        cost_estimate=pl.CostEstimate(
+            flops=sum(part.size for part in parts),
+            bytes_accessed=4 * sum(part.size for part in parts),
+            transcendentals=0,
         ),
         name="sum_groups",
     )(index, *parts)
@@ -588,15 +620,41 @@
         grams = [gram, after(swap(gram, "fsdp", 1), slopes[-1])]
     else:
         grams = [lax.psum(gram, "fsdp")]
+    groups = dp_size // mates
+    share = hidden // mates
+    pieces = share // min(share, 256)
+    out_rows = w_out.shape[0] // dp_size
+    group_rows = mates * out_rows
+    half = pieces // 2
+    paired = groups == 4 and half > 0
+    if paired:
+        sends = [
+            [(0, j) for j in range(pieces)],
+            [(1, j) for j in range(pieces)] + [(3, j) for j in range(half)],
+            [(2, j) for j in range(half, pieces)],
+            [(3, j) for j in range(half, pieces)],
+            [(2, j) for j in range(half)],
+        ]
+    else:
+        sends = [[(k, j) for j in range(pieces)] for k in range(groups)]
+    pooled_at = [(k, len(sends[k]) * group_rows) for k in range(groups)]
     loss, dembed, *parts = backward(
-        index, all_embed, unit_gram(grams), final_gain, pooled, w_out, slopes, turns,
+        index, all_embed, unit_gram(grams), final_gain, pooled, w_out, slopes, turns, sends,
         mates, dp_size, per_image,
     )
-    out_rows = dembed.shape[1] // dp_size
-    parts = [parts[0]] + [swap(part, "dp", (k + 1) * mates) for k, part in enumerate(parts[1:])]
+    swapped = [parts[0]] + [swap(parts[k], "dp", k * mates) for k in range(1, groups)]
+    sources = [[(0, j * group_rows), (1, j * group_rows)] for j in range(pieces)]
+    if paired:
+        pair = add_pair(parts[groups], swapped[1], pieces * group_rows)
+        swapped.append(swap(pair, "dp", 2 * mates))
+        for j in range(pieces):
+            arrays, first = ((4,), 0) if j < half else ((2, 3), half)
+            sources[j] += [(k, (j - first) * group_rows) for k in arrays]
+    else:
+        sources = [[(k, j * group_rows) for k in range(groups)] for j in range(pieces)]
     columns = own_columns(index, dembed, out_rows)
     extra = teacher.shape[0] * hidden // parts[0].shape[1]
-    shares = sum_groups(index, parts, mates, out_rows, extra)
+    shares = sum_groups(index, swapped, sources, pooled_at, mates, out_rows, extra)
     shares = [shares[0]] + [swap(part, "dp", j + 1) for j, part in enumerate(shares[1:])]
     grad_in, grad_out = finish(index, shares, columns, hidden, teacher.shape[0])
     return (loss[0, 0], grad_in, grad_out)

time: 73.3 us -> 72.8 us (level)
  the two profiles are of different devices: /device:TPU:9 before, /device:TPU:0 now
where the time goes in v2:
time: 72.8 us; the launch traced here: 72.3 us
  waiting for transfers between devices  25.6 us (35%)
  starting transfers between devices  24.3 us (33%)
  Pallas kernels  21.5 us (30%)
  between operations  0.76 us (1%)
    ppermute x11, waiting for transfers between devices, swap(): lax.ppermute(value, axis, [(i, i ^ step) for i in range(lax.axis_size(axi...  22.1 us
    ppermute x11, starting transfers between devices, swap(): lax.ppermute(value, axis, [(i, i ^ step) for i in range(lax.axis_size(axi...  13.7 us
    all_to_all x2, starting transfers between devices, exchange(): return lax.all_to_all(blocks, axes, split_axis=0, concat_axis=0, tiled=True)  10.6 us
    pallas_call x1, Pallas kernels, forward(): pl.pallas_call(kernel, in_specs=[pl.BlockSpec(memory_space=pltpu.SMEM)] +...  6.41 us
    pallas_call x1, Pallas kernels, backward(): pl.pallas_call(kernel, in_specs=[smem, whole, whole, whole, whole, in_hbm...  5.8 us
    pallas_call x1, Pallas kernels, mate_slopes(): pl.pallas_call(kernel, grid_spec=pltpu.PrefetchScalarGridSpec(num_scalar_...  5.69 us
    all_to_all x2, waiting for transfers between devices, exchange(): return lax.all_to_all(blocks, axes, split_axis=0, concat_axis=0, tiled=True)  3.53 us
  transfers between devices with their start and end apart: 13, of which 7 were waited for; matrix products, arithmetic and copies ran while one was open for 0% of the time, Pallas kernels for 20%

profile of v2, /device:TPU:0, one launch (start us, length us, event | category | flops | bytes accessed | tf_op | source)
XLA Modules:
  0.0 72.3 jit_solution(12123801846897304434)
XLA Ops:
  0.6 0.5 collective-permute-start
  1.1 2.6 %collective-permute-start.2 = (bf16[256,1024]{1,0:T(8,128)(2,1)}, bf16[256,1024]{1,0:T(8,128)(2,1)S(1)}, u32[]{:S(2)}, u32[]{:S(2)}) collective-permute-start(bf16[256,1024]{1,0:T(8,128)(2,1)} %refs_0_.1), channel_id=1, source_target_pairs={{0,4},{2,6},{4,0},{6,2},{8,12},{10,14},{12,8},{14,10},{16,20},{18,... | collective-permute-start | bytes 1572872 | tf_op jit(solution)/shard_map/ppermute | solution.py:575
  3.7 1.4 %teacher_payload.1 = bf16[16,16,384]{2,1,0:T(8,128)(2,1)} custom-call(s32[1]{0:T(128)} %bitcast.1.first_ref, bf16[2,6144]{1,0:T(2,128)(2,1)} %teacher_ref.1), custom_call_target="tpu_custom_call" | custom-call | flops 98304 | bytes 196608 | tf_op jit(solution)/shard_map/teacher_payload/pallas_call | solution.py:83
  5.2 5.0 %all-to-all-start.1 = ((bf16[16,16,384]{2,1,0:T(8,128)(2,1)}), bf16[16,16,384]{2,1,0:T(8,128)(2,1)S(1)}, u32[]{:S(2)}, u32[]{:S(2)}) async-start(bf16[16,16,384]{2,1,0:T(8,128)(2,1)} %teacher_payload.1), calls=%async_computation.1 | async-start | bytes 393216 | tf_op jit(solution)/shard_map/all_to_all | solution.py:564
  10.1 6.4 %forward.1 = (bf16[2,2048]{1,0:T(2,128)(2,1)S(1)}, bf16[32,16,128]{2,1,0:T(8,128)(2,1)}) custom-call(s32[1]{0:T(128)} %bitcast.1.first_ref, f32[1,1024]{1,0:T(1,128)} %bitcast.9, f32[1,2048]{1,0:T(1,128)} %bitcast.7, f32[1,1024]{1,0:T(1,128)} %bitcast.11, bf16[256,1024]{1,0:T(8,128)(2,1)} %refs_0_.1, bf16[1024,2048]{1,0:T(8,128)(2,1)} %refs_6_.1, ...), custom_call_target="tpu_custom_call" | custom-call | flops 1073741824 | bytes 8388608 | tf_op jit(solution)/shard_map/forward/pallas_call | solution.py:142
  16.6 2.6 %all-to-all-done.1.arrived_ref = bf16[16,16,384]{2,1,0:T(8,128)(2,1)S(1)} async-done(((bf16[16,16,384]{2,1,0:T(8,128)(2,1)}), bf16[16,16,384]{2,1,0:T(8,128)(2,1)S(1)}, u32[]{:S(2)}, u32[]{:S(2)}) %all-to-all-start.1) | async-done | bytes 196640 | tf_op jit(solution)/shard_map/all_to_all | solution.py:564
  19.1 0.0 collective-permute-done.refs_1_
  19.1 0.0 copy-start
  19.1 0.5 target_gram.1.refs_0_
  19.7 0.0 collective-permute-done.2.refs_2_
  19.7 0.0 copy-start.1
  19.7 0.1 collective-permute-start.3
  19.8 5.6 %all-to-all-start = ((bf16[32,16,128]{2,1,0:T(8,128)(2,1)}), bf16[32,16,128]{2,1,0:T(8,128)(2,1)S(1)}, u32[]{:S(2)}, u32[]{:S(2)}) async-start(bf16[32,16,128]{2,1,0:T(8,128)(2,1)} %get-tuple-element.23), calls=%async_computation | async-start | bytes 262144 | tf_op jit(solution)/shard_map/all_to_all | solution.py:564
  25.4 1.8 %collective-permute-start.1 = (f32[32,32]{1,0:T(8,128)S(1)}, f32[32,32]{1,0:T(8,128)S(1)}, u32[]{:S(2)}, u32[]{:S(2)}) collective-permute-start(f32[32,32]{1,0:T(8,128)S(1)} %target_gram.1.refs_0_), channel_id=1, source_target_pairs={{0,1},{1,0},{2,3},{3,2},{4,5},{5,4},{6,7},{7,6},{8,9},{9,8},{10,11... | collective-permute-start | bytes 12296 | tf_op jit(solution)/shard_map/ppermute | solution.py:575
  27.3 0.0 copy-done
  27.3 0.0 copy-done.1
  27.3 0.0 collective-permute-done.3.refs_3_
  27.3 5.7 %mate_slopes.1 = (bf16[1024,512]{1,0:T(8,128)(2,1)S(1)}, bf16[1024,1024]{1,0:T(8,128)(2,1)S(1)}) custom-call(s32[1]{0:T(128)S(6)} %select_n.7.index_ref, bf16[256,1024]{1,0:T(8,128)(2,1)} %refs_0_.1, bf16[256,1024]{1,0:T(8,128)(2,1)} %copy-done, bf16[256,1024]{1,0:T(8,128)(2,1)} %copy-done.1, bf16[256,1024]{1,0:T(8,128)(2,1)} %collective-permute-done.3.refs_3_, ...), custom_call_target="tpu_custom_call" | custom-call | flops 1073741824 | bytes 4194304 | tf_op jit(solution)/shard_map/mate_slopes/pallas_call | solution.py:201
  33.0 0.0 collective-permute-done.1.refs_1_
  33.0 0.1 unit_gram.1.gram_ref
  33.1 1.0 %all-to-all-done.arrived_ref = bf16[32,16,128]{2,1,0:T(8,128)(2,1)S(1)} async-done(((bf16[32,16,128]{2,1,0:T(8,128)(2,1)}), bf16[32,16,128]{2,1,0:T(8,128)(2,1)S(1)}, u32[]{:S(2)}, u32[]{:S(2)}) %all-to-all-start) | async-done | bytes 131104 | tf_op jit(solution)/shard_map/all_to_all | solution.py:564
  34.0 5.8 %backward.1 = (f32[1,1]{1,0:T(1,128)}, bf16[32,1024]{1,0:T(8,128)(2,1)S(1)}, bf16[528,256]{1,0:T(8,128)(2,1)S(1)}, bf16[784,256]{1,0:T(8,128)(2,1)}, bf16[272,25...) custom-call(s32[1]{0:T(128)} %bitcast.index_ref, ...), custom_call_target="tpu_custom_call" | custom-call | flops 1073741824 | bytes 3145728 | tf_op jit(solution)/shard_map/backward/pallas_call | solution.py:401
  39.9 0.6 collective-permute-start.4
  40.4 2.4 %collective-permute-start.5 = (bf16[272,256]{1,0:T(8,128)(2,1)}, bf16[272,256]{1,0:T(8,128)(2,1)S(1)}, u32[]{:S(2)}, u32[]{:S(2)}) collective-permute-start(bf16[272,256]{1,0:T(8,128)(2,1)} %get-tuple-element.33), channel_id=1, source_target_pairs={{0,16},{2,18},{4,20},{6,22},{8,24},{10,26},{12,28},{14,30},{16,0},... | collective-permute-start | bytes 417800 | tf_op jit(solution)/shard_map/ppermute | solution.py:575
  42.9 1.4 %collective-permute-start.6 = (bf16[272,256]{1,0:T(8,128)(2,1)}, bf16[272,256]{1,0:T(8,128)(2,1)S(1)}, u32[]{:S(2)}, u32[]{:S(2)}) collective-permute-start(bf16[272,256]{1,0:T(8,128)(2,1)} %get-tuple-element.34), channel_id=1, source_target_pairs={{0,24},{2,26},{4,28},{6,30},{8,16},{10,18},{12,20},{14,22},{16,8},... | collective-permute-start | bytes 417800 | tf_op jit(solution)/shard_map/ppermute | solution.py:575
  44.3 9.5 %collective-permute-done.4.arrived_ref.refs_1_ = bf16[784,256]{1,0:T(8,128)(2,1)S(1)} collective-permute-done((bf16[784,256]{1,0:T(8,128)(2,1)}, bf16[784,256]{1,0:T(8,128)(2,1)S(1)}, u32[]{:S(2)}, u32[]{:S(2)}) %collective-permute-start.4) | collective-permute-done | bytes 401440 | tf_op jit(solution)/shard_map/ppermute | solution.py:575
  53.9 2.1 %collective-permute-start.7 = (bf16[256,256]{1,0:T(8,128)(2,1)S(1)}, bf16[256,256]{1,0:T(8,128)(2,1)S(1)}, u32[]{:S(2)}, u32[]{:S(2)}) collective-permute-start(bf16[256,256]{1,0:T(8,128)(2,1)S(1)} %add_pair.1), channel_id=1, source_target_pairs={{0,16},{2,18},{4,20},{6,22},{8,24},{10,26},{12,28},{14,30},{16,0},... | collective-permute-start | bytes 393224 | tf_op jit(solution)/shard_map/ppermute | solution.py:575
  55.9 0.0 collective-permute-done.5.refs_2_
  55.9 3.3 %collective-permute-done.6.refs_3_ = bf16[272,256]{1,0:T(8,128)(2,1)S(1)} collective-permute-done((bf16[272,256]{1,0:T(8,128)(2,1)}, bf16[272,256]{1,0:T(8,128)(2,1)S(1)}, u32[]{:S(2)}, u32[]{:S(2)}) %collective-permute-start.6) | collective-permute-done | bytes 139296 | tf_op jit(solution)/shard_map/ppermute | solution.py:575
  59.2 4.4 %collective-permute-done.7.refs_4_ = bf16[256,256]{1,0:T(8,128)(2,1)S(1)} collective-permute-done((bf16[256,256]{1,0:T(8,128)(2,1)S(1)}, bf16[256,256]{1,0:T(8,128)(2,1)S(1)}, u32[]{:S(2)}, u32[]{:S(2)}) %collective-permute-start.7) | collective-permute-done | bytes 131104 | tf_op jit(solution)/shard_map/ppermute | solution.py:575
  63.6 0.2 sum_groups.1
  63.8 1.2 %collective-permute-start.10 = (bf16[192,256]{1,0:T(8,128)(2,1)S(1)}, bf16[192,256]{1,0:T(8,128)(2,1)S(1)}, u32[]{:S(2)}, u32[]{:S(2)}) collective-permute-start(bf16[192,256]{1,0:T(8,128)(2,1)S(1)} %get-tuple-element.39), channel_id=1, source_target_pairs={{0,6},{2,4},{4,2},{6,0},{8,14},{10,12},{12,10},{14,8},{16,22},{18,... | collective-permute-start | bytes 294920 | tf_op jit(solution)/shard_map/ppermute | solution.py:575
  65.0 0.5 collective-permute-start.8
  65.5 0.5 collective-permute-start.9
  66.0 0.2 own_columns.1.refs_4_
  66.2 2.6 %collective-permute-done.10.refs_3_ = bf16[192,256]{1,0:T(8,128)(2,1)S(1)} collective-permute-done((bf16[192,256]{1,0:T(8,128)(2,1)S(1)}, bf16[192,256]{1,0:T(8,128)(2,1)S(1)}, u32[]{:S(2)}, u32[]{:S(2)}) %collective-permute-start.10) | collective-permute-done | bytes 98336 | tf_op jit(solution)/shard_map/ppermute | solution.py:575
  68.8 0.0 collective-permute-done.8.refs_1_
  68.8 2.3 %collective-permute-done.9.refs_2_ = bf16[192,256]{1,0:T(8,128)(2,1)S(1)} collective-permute-done((bf16[192,256]{1,0:T(8,128)(2,1)S(1)}, bf16[192,256]{1,0:T(8,128)(2,1)S(1)}, u32[]{:S(2)}, u32[]{:S(2)}) %collective-permute-start.9) | collective-permute-done | bytes 98336 | tf_op jit(solution)/shard_map/ppermute | solution.py:575
  71.1 1.2 %finish.1 = (bf16[64,2048]{1,0:T(8,128)(2,1)}, bf16[64,2048]{1,0:T(8,128)(2,1)}) custom-call(s32[1]{0:T(128)} %bitcast.index_ref, bf16[192,256]{1,0:T(8,128)(2,1)S(1)} %get-tuple-element.36.refs_0_, bf16[192,256]{1,0:T(8,128)(2,1)S(1)} %collective-permute-done.8.refs_1_, bf16[192,256]{1,0:T(8,128)(2,1)S(1)} %collective-permute-done.9.refs_2_, ...), custom_call_target="tpu_custom_call" | custom-call | flops 8388608 | bytes 393216 | tf_op jit(solution)/shard_map/finish/pallas_call | solution.py:547
  (1 shorter events, 0.0 us)
Async XLA Ops:
  0.6 18.5 %collective-permute-start = (bf16[256,1024]{1,0:T(8,128)(2,1)}, bf16[256,1024]{1,0:T(8,128)(2,1)S(1)}, u32[]{:S(2)}, u32[]{:S(2)}) collective-permute-start(bf16[256,1024]{1,0:T(8,128)(2,1)} %refs_0_.1), channel_id=1, source_target_pairs={{0,2},{2,0},{4,6},{6,4},{8,10},{10,8},{12,14},{14,12},{16,18},{18,... | collective-permute-start | bytes 1572872 | tf_op jit(solution)/shard_map/ppermute | solution.py:575
  1.1 18.5 %collective-permute-start.2 = (bf16[256,1024]{1,0:T(8,128)(2,1)}, bf16[256,1024]{1,0:T(8,128)(2,1)S(1)}, u32[]{:S(2)}, u32[]{:S(2)}) collective-permute-start(bf16[256,1024]{1,0:T(8,128)(2,1)} %refs_0_.1), channel_id=1, source_target_pairs={{0,4},{2,6},{4,0},{6,2},{8,12},{10,14},{12,8},{14,10},{16,20},{18,... | collective-permute-start | bytes 1572872 | tf_op jit(solution)/shard_map/ppermute | solution.py:575
  5.2 14.0 %all-to-all-start.1 = ((bf16[16,16,384]{2,1,0:T(8,128)(2,1)}), bf16[16,16,384]{2,1,0:T(8,128)(2,1)S(1)}, u32[]{:S(2)}, u32[]{:S(2)}) async-start(bf16[16,16,384]{2,1,0:T(8,128)(2,1)} %teacher_payload.1), calls=%async_computation.1 | async-start | bytes 393216 | tf_op jit(solution)/shard_map/all_to_all | solution.py:564
  19.1 8.1 %copy-start = (bf16[256,1024]{1,0:T(8,128)(2,1)}, bf16[256,1024]{1,0:T(8,128)(2,1)S(1)}, u32[]{:S(2)}) copy-start(bf16[256,1024]{1,0:T(8,128)(2,1)S(1)} %collective-permute-done.refs_1_) | copy-start | bytes 1572868
  19.7 7.6 %copy-start.1 = (bf16[256,1024]{1,0:T(8,128)(2,1)}, bf16[256,1024]{1,0:T(8,128)(2,1)S(1)}, u32[]{:S(2)}) copy-start(bf16[256,1024]{1,0:T(8,128)(2,1)S(1)} %collective-permute-done.2.refs_2_) | copy-start | bytes 1572868
  19.7 7.6 %collective-permute-start.3 = (bf16[256,1024]{1,0:T(8,128)(2,1)S(1)}, bf16[256,1024]{1,0:T(8,128)(2,1)}, u32[]{:S(2)}, u32[]{:S(2)}) collective-permute-start(bf16[256,1024]{1,0:T(8,128)(2,1)S(1)} %collective-permute-done.2.refs_2_), channel_id=1, source_target_pairs={{0,2},{2,0},{4,6},{6,4},{8,10},{10,8},{12,14},{14,12},{16,18},{18,... | collective-permute-start | bytes 1572872 | tf_op jit(solution)/shard_map/ppermute | solution.py:575
  19.8 14.3 %all-to-all-start = ((bf16[32,16,128]{2,1,0:T(8,128)(2,1)}), bf16[32,16,128]{2,1,0:T(8,128)(2,1)S(1)}, u32[]{:S(2)}, u32[]{:S(2)}) async-start(bf16[32,16,128]{2,1,0:T(8,128)(2,1)} %get-tuple-element.23), calls=%async_computation | async-start | bytes 262144 | tf_op jit(solution)/shard_map/all_to_all | solution.py:564
  25.4 7.6 %collective-permute-start.1 = (f32[32,32]{1,0:T(8,128)S(1)}, f32[32,32]{1,0:T(8,128)S(1)}, u32[]{:S(2)}, u32[]{:S(2)}) collective-permute-start(f32[32,32]{1,0:T(8,128)S(1)} %target_gram.1.refs_0_), channel_id=1, source_target_pairs={{0,1},{1,0},{2,3},{3,2},{4,5},{5,4},{6,7},{7,6},{8,9},{9,8},{10,11... | collective-permute-start | bytes 12296 | tf_op jit(solution)/shard_map/ppermute | solution.py:575
  39.9 14.0 %collective-permute-start.4 = (bf16[784,256]{1,0:T(8,128)(2,1)}, bf16[784,256]{1,0:T(8,128)(2,1)S(1)}, u32[]{:S(2)}, u32[]{:S(2)}) collective-permute-start(bf16[784,256]{1,0:T(8,128)(2,1)} %get-tuple-element.32), channel_id=1, source_target_pairs={{0,8},{2,10},{4,12},{6,14},{8,0},{10,2},{12,4},{14,6},{16,24},{18,... | collective-permute-start | bytes 1204232 | tf_op jit(solution)/shard_map/ppermute | solution.py:575
  40.4 15.5 %collective-permute-start.5 = (bf16[272,256]{1,0:T(8,128)(2,1)}, bf16[272,256]{1,0:T(8,128)(2,1)S(1)}, u32[]{:S(2)}, u32[]{:S(2)}) collective-permute-start(bf16[272,256]{1,0:T(8,128)(2,1)} %get-tuple-element.33), channel_id=1, source_target_pairs={{0,16},{2,18},{4,20},{6,22},{8,24},{10,26},{12,28},{14,30},{16,0},... | collective-permute-start | bytes 417800 | tf_op jit(solution)/shard_map/ppermute | solution.py:575
  42.9 16.4 %collective-permute-start.6 = (bf16[272,256]{1,0:T(8,128)(2,1)}, bf16[272,256]{1,0:T(8,128)(2,1)S(1)}, u32[]{:S(2)}, u32[]{:S(2)}) collective-permute-start(bf16[272,256]{1,0:T(8,128)(2,1)} %get-tuple-element.34), channel_id=1, source_target_pairs={{0,24},{2,26},{4,28},{6,30},{8,16},{10,18},{12,20},{14,22},{16,8},... | collective-permute-start | bytes 417800 | tf_op jit(solution)/shard_map/ppermute | solution.py:575
  53.9 9.7 %collective-permute-start.7 = (bf16[256,256]{1,0:T(8,128)(2,1)S(1)}, bf16[256,256]{1,0:T(8,128)(2,1)S(1)}, u32[]{:S(2)}, u32[]{:S(2)}) collective-permute-start(bf16[256,256]{1,0:T(8,128)(2,1)S(1)} %add_pair.1), channel_id=1, source_target_pairs={{0,16},{2,18},{4,20},{6,22},{8,24},{10,26},{12,28},{14,30},{16,0},... | collective-permute-start | bytes 393224 | tf_op jit(solution)/shard_map/ppermute | solution.py:575
  63.8 5.0 %collective-permute-start.10 = (bf16[192,256]{1,0:T(8,128)(2,1)S(1)}, bf16[192,256]{1,0:T(8,128)(2,1)S(1)}, u32[]{:S(2)}, u32[]{:S(2)}) collective-permute-start(bf16[192,256]{1,0:T(8,128)(2,1)S(1)} %get-tuple-element.39), channel_id=1, source_target_pairs={{0,6},{2,4},{4,2},{6,0},{8,14},{10,12},{12,10},{14,8},{16,22},{18,... | collective-permute-start | bytes 294920 | tf_op jit(solution)/shard_map/ppermute | solution.py:575
  65.0 3.8 %collective-permute-start.8 = (bf16[192,256]{1,0:T(8,128)(2,1)S(1)}, bf16[192,256]{1,0:T(8,128)(2,1)S(1)}, u32[]{:S(2)}, u32[]{:S(2)}) collective-permute-start(bf16[192,256]{1,0:T(8,128)(2,1)S(1)} %get-tuple-element.37), channel_id=1, source_target_pairs={{0,2},{2,0},{4,6},{6,4},{8,10},{10,8},{12,14},{14,12},{16,18},{18,... | collective-permute-start | bytes 294920 | tf_op jit(solution)/shard_map/ppermute | solution.py:575
  65.5 5.6 %collective-permute-start.9 = (bf16[192,256]{1,0:T(8,128)(2,1)S(1)}, bf16[192,256]{1,0:T(8,128)(2,1)S(1)}, u32[]{:S(2)}, u32[]{:S(2)}) collective-permute-start(bf16[192,256]{1,0:T(8,128)(2,1)S(1)} %get-tuple-element.38), channel_id=1, source_target_pairs={{0,4},{2,6},{4,0},{6,2},{8,12},{10,14},{12,8},{14,10},{16,20},{18,... | collective-permute-start | bytes 294920 | tf_op jit(solution)/shard_map/ppermute | solution.py:575

commit v3 on v2

--- a/solution.py
+++ b/solution.py
@@ -457,13 +457,10 @@
     )(index, dembed)
 
 
-def add_pair(kept, arrived, start):
-    rows, _ = kept.shape
+def add_pair(kept, arrived):
 
     def kernel(kept_ref, arrived_ref, sum_ref):
-        sum_ref[...] = (
-            kept_ref[...].astype(f32) + arrived_ref[start : start + rows].astype(f32)
-        ).astype(bf16)
+        sum_ref[...] = (kept_ref[...].astype(f32) + arrived_ref[...].astype(f32)).astype(bf16)
 
     return pl.pallas_call(
         kernel,
@@ -630,10 +627,11 @@
     if paired:
         sends = [
             [(0, j) for j in range(pieces)],
-            [(1, j) for j in range(pieces)] + [(3, j) for j in range(half)],
+            [(1, j) for j in range(pieces)],
             [(2, j) for j in range(half, pieces)],
             [(3, j) for j in range(half, pieces)],
             [(2, j) for j in range(half)],
+            [(3, j) for j in range(half)],
         ]
     else:
         sends = [[(k, j) for j in range(pieces)] for k in range(groups)]
@@ -642,10 +640,15 @@
         index, all_embed, unit_gram(grams), final_gain, pooled, w_out, slopes, turns, sends,
         mates, dp_size, per_image,
     )
-    swapped = [parts[0]] + [swap(parts[k], "dp", k * mates) for k in range(1, groups)]
+    if paired:
+        pair = add_pair(parts[groups], swap(parts[groups + 1], "dp", mates))
+    swapped = [parts[0]] + [
+        swap(parts[k], "dp", k * mates) for k in list(range(2, groups)) + [1] if k < groups
+    ]
+    if groups > 1:
+        swapped.insert(1, swapped.pop())
     sources = [[(0, j * group_rows), (1, j * group_rows)] for j in range(pieces)]
     if paired:
-        pair = add_pair(parts[groups], swapped[1], pieces * group_rows)
         swapped.append(swap(pair, "dp", 2 * mates))
         for j in range(pieces):
             arrays, first = ((4,), 0) if j < half else ((2, 3), half)

time: 72.8 us -> 71.7 us (0.985)
  waiting for transfers between devices: 25.6 us -> 24.5 us
    ppermute x11 -> x12, waiting for transfers between devices: 22.1 us -> 21 us  [swap(): lax.ppermute(value, axis, [(i, i ^ step) for i in range(lax.axis_size(axi...]
    ppermute x11 -> x12, starting transfers between devices: 13.7 us -> 14.2 us  [swap(): lax.ppermute(value, axis, [(i, i ^ step) for i in range(lax.axis_size(axi...]
  transfers between devices with their start and end apart: 13 -> 14, of which waited for: 7 -> 7; matrix products, arithmetic and copies ran while one was open for 0% -> 0% of each run, Pallas kernels for 20% -> 20%
where the time goes in v3:
time: 71.7 us; the launch traced here: 71.2 us
  starting transfers between devices  24.8 us (35%)
  waiting for transfers between devices  24.5 us (34%)
  Pallas kernels  21.1 us (29%)
  between operations  0.76 us (1%)
    ppermute x12, waiting for transfers between devices, swap(): lax.ppermute(value, axis, [(i, i ^ step) for i in range(lax.axis_size(axi...  21 us
    ppermute x12, starting transfers between devices, swap(): lax.ppermute(value, axis, [(i, i ^ step) for i in range(lax.axis_size(axi...  14.2 us
    all_to_all x2, starting transfers between devices, exchange(): return lax.all_to_all(blocks, axes, split_axis=0, concat_axis=0, tiled=True)  10.6 us
    pallas_call x1, Pallas kernels, forward(): pl.pallas_call(kernel, in_specs=[pl.BlockSpec(memory_space=pltpu.SMEM)] +...  6.41 us
    pallas_call x1, Pallas kernels, mate_slopes(): pl.pallas_call(kernel, grid_spec=pltpu.PrefetchScalarGridSpec(num_scalar_...  5.69 us
    pallas_call x1, Pallas kernels, backward(): pl.pallas_call(kernel, in_specs=[smem, whole, whole, whole, whole, in_hbm...  5.42 us
    all_to_all x2, waiting for transfers between devices, exchange(): return lax.all_to_all(blocks, axes, split_axis=0, concat_axis=0, tiled=True)  3.53 us
    pallas_call x1, Pallas kernels, teacher_payload(): pl.pallas_call(kernel, in_specs=[pl.BlockSpec(memory_space=pltpu.SMEM), p...  1.44 us
  transfers between devices with their start and end apart: 14, of which 7 were waited for; matrix products, arithmetic and copies ran while one was open for 0% of the time, Pallas kernels for 20%

profile of v3, /device:TPU:0, one launch (start us, length us, event | category | flops | bytes accessed | tf_op | source)
XLA Modules:
  0.0 71.2 jit_solution(16184960689128550882)
XLA Ops:
  0.6 0.5 collective-permute-start
  1.1 2.6 %collective-permute-start.2 = (bf16[256,1024]{1,0:T(8,128)(2,1)}, bf16[256,1024]{1,0:T(8,128)(2,1)S(1)}, u32[]{:S(2)}, u32[]{:S(2)}) collective-permute-start(bf16[256,1024]{1,0:T(8,128)(2,1)} %refs_0_.1), channel_id=1, source_target_pairs={{0,4},{2,6},{4,0},{6,2},{8,12},{10,14},{12,8},{14,10},{16,20},{18,... | collective-permute-start | bytes 1572872 | tf_op jit(solution)/shard_map/ppermute | solution.py:572
  3.7 1.4 %teacher_payload.1 = bf16[16,16,384]{2,1,0:T(8,128)(2,1)} custom-call(s32[1]{0:T(128)} %bitcast.1.first_ref, bf16[2,6144]{1,0:T(2,128)(2,1)} %teacher_ref.1), custom_call_target="tpu_custom_call" | custom-call | flops 98304 | bytes 196608 | tf_op jit(solution)/shard_map/teacher_payload/pallas_call | solution.py:83
  5.2 5.0 %all-to-all-start.1 = ((bf16[16,16,384]{2,1,0:T(8,128)(2,1)}), bf16[16,16,384]{2,1,0:T(8,128)(2,1)S(1)}, u32[]{:S(2)}, u32[]{:S(2)}) async-start(bf16[16,16,384]{2,1,0:T(8,128)(2,1)} %teacher_payload.1), calls=%async_computation.1 | async-start | bytes 393216 | tf_op jit(solution)/shard_map/all_to_all | solution.py:561
  10.1 6.4 %forward.1 = (bf16[2,2048]{1,0:T(2,128)(2,1)S(1)}, bf16[32,16,128]{2,1,0:T(8,128)(2,1)}) custom-call(s32[1]{0:T(128)} %bitcast.1.first_ref, f32[1,1024]{1,0:T(1,128)} %bitcast.9, f32[1,2048]{1,0:T(1,128)} %bitcast.7, f32[1,1024]{1,0:T(1,128)} %bitcast.11, bf16[256,1024]{1,0:T(8,128)(2,1)} %refs_0_.1, bf16[1024,2048]{1,0:T(8,128)(2,1)} %refs_6_.1, ...), custom_call_target="tpu_custom_call" | custom-call | flops 1073741824 | bytes 8388608 | tf_op jit(solution)/shard_map/forward/pallas_call | solution.py:142
  16.6 2.6 %all-to-all-done.1.arrived_ref = bf16[16,16,384]{2,1,0:T(8,128)(2,1)S(1)} async-done(((bf16[16,16,384]{2,1,0:T(8,128)(2,1)}), bf16[16,16,384]{2,1,0:T(8,128)(2,1)S(1)}, u32[]{:S(2)}, u32[]{:S(2)}) %all-to-all-start.1) | async-done | bytes 196640 | tf_op jit(solution)/shard_map/all_to_all | solution.py:561
  19.1 0.0 collective-permute-done.refs_1_
  19.1 0.0 copy-start
  19.1 0.5 target_gram.1.refs_0_
  19.7 0.0 collective-permute-done.2.refs_2_
  19.7 0.0 copy-start.1
  19.7 0.1 collective-permute-start.3
  19.8 5.6 %all-to-all-start = ((bf16[32,16,128]{2,1,0:T(8,128)(2,1)}), bf16[32,16,128]{2,1,0:T(8,128)(2,1)S(1)}, u32[]{:S(2)}, u32[]{:S(2)}) async-start(bf16[32,16,128]{2,1,0:T(8,128)(2,1)} %get-tuple-element.24), calls=%async_computation | async-start | bytes 262144 | tf_op jit(solution)/shard_map/all_to_all | solution.py:561
  25.4 1.8 %collective-permute-start.1 = (f32[32,32]{1,0:T(8,128)S(1)}, f32[32,32]{1,0:T(8,128)S(1)}, u32[]{:S(2)}, u32[]{:S(2)}) collective-permute-start(f32[32,32]{1,0:T(8,128)S(1)} %target_gram.1.refs_0_), channel_id=1, source_target_pairs={{0,1},{1,0},{2,3},{3,2},{4,5},{5,4},{6,7},{7,6},{8,9},{9,8},{10,11... | collective-permute-start | bytes 12296 | tf_op jit(solution)/shard_map/ppermute | solution.py:572
  27.3 0.0 copy-done
  27.3 0.0 copy-done.1
  27.3 0.0 collective-permute-done.3.refs_3_
  27.3 5.7 %mate_slopes.1 = (bf16[1024,512]{1,0:T(8,128)(2,1)S(1)}, bf16[1024,1024]{1,0:T(8,128)(2,1)S(1)}) custom-call(s32[1]{0:T(128)S(6)} %select_n.7.index_ref, bf16[256,1024]{1,0:T(8,128)(2,1)} %refs_0_.1, bf16[256,1024]{1,0:T(8,128)(2,1)} %copy-done, bf16[256,1024]{1,0:T(8,128)(2,1)} %copy-done.1, bf16[256,1024]{1,0:T(8,128)(2,1)} %collective-permute-done.3.refs_3_, ...), custom_call_target="tpu_custom_call" | custom-call | flops 1073741824 | bytes 4194304 | tf_op jit(solution)/shard_map/mate_slopes/pallas_call | solution.py:201
  33.0 0.0 collective-permute-done.1.refs_1_
  33.0 0.1 unit_gram.1.gram_ref
  33.1 1.0 %all-to-all-done.arrived_ref = bf16[32,16,128]{2,1,0:T(8,128)(2,1)S(1)} async-done(((bf16[32,16,128]{2,1,0:T(8,128)(2,1)}), bf16[32,16,128]{2,1,0:T(8,128)(2,1)S(1)}, u32[]{:S(2)}, u32[]{:S(2)}) %all-to-all-start) | async-done | bytes 131104 | tf_op jit(solution)/shard_map/all_to_all | solution.py:561
  34.0 5.4 %backward.1 = (f32[1,1]{1,0:T(1,128)}, bf16[32,1024]{1,0:T(8,128)(2,1)S(1)}, bf16[528,256]{1,0:T(8,128)(2,1)S(1)}, bf16[528,256]{1,0:T(8,128)(2,1)}, bf16[272,25...) custom-call(s32[1]{0:T(128)} %bitcast.index_ref, ...), custom_call_target="tpu_custom_call" | custom-call | flops 1073741824 | bytes 3145728 | tf_op jit(solution)/shard_map/backward/pallas_call | solution.py:401
  39.5 0.6 collective-permute-start.4
  40.1 1.5 %collective-permute-start.7 = (bf16[256,256]{1,0:T(8,128)(2,1)}, bf16[256,256]{1,0:T(8,128)(2,1)S(1)}, u32[]{:S(2)}, u32[]{:S(2)}) collective-permute-start(bf16[256,256]{1,0:T(8,128)(2,1)} %get-tuple-element.37), channel_id=1, source_target_pairs={{0,8},{2,10},{4,12},{6,14},{8,0},{10,2},{12,4},{14,6},{16,24},{18,... | collective-permute-start | bytes 393224 | tf_op jit(solution)/shard_map/ppermute | solution.py:572
  41.6 1.4 %collective-permute-start.5 = (bf16[272,256]{1,0:T(8,128)(2,1)}, bf16[272,256]{1,0:T(8,128)(2,1)S(1)}, u32[]{:S(2)}, u32[]{:S(2)}) collective-permute-start(bf16[272,256]{1,0:T(8,128)(2,1)} %get-tuple-element.34), channel_id=1, source_target_pairs={{0,16},{2,18},{4,20},{6,22},{8,24},{10,26},{12,28},{14,30},{16,0},... | collective-permute-start | bytes 417800 | tf_op jit(solution)/shard_map/ppermute | solution.py:572
  43.0 1.4 %collective-permute-start.6 = (bf16[272,256]{1,0:T(8,128)(2,1)}, bf16[272,256]{1,0:T(8,128)(2,1)S(1)}, u32[]{:S(2)}, u32[]{:S(2)}) collective-permute-start(bf16[272,256]{1,0:T(8,128)(2,1)} %get-tuple-element.35), channel_id=1, source_target_pairs={{0,24},{2,26},{4,28},{6,30},{8,16},{10,18},{12,20},{14,22},{16,8},... | collective-permute-start | bytes 417800 | tf_op jit(solution)/shard_map/ppermute | solution.py:572
  44.4 9.0 %collective-permute-done.7.arrived_ref = bf16[256,256]{1,0:T(8,128)(2,1)S(1)} collective-permute-done((bf16[256,256]{1,0:T(8,128)(2,1)}, bf16[256,256]{1,0:T(8,128)(2,1)S(1)}, u32[]{:S(2)}, u32[]{:S(2)}) %collective-permute-start.7) | collective-permute-done | bytes 131104 | tf_op jit(solution)/shard_map/ppermute | solution.py:572
  53.5 2.1 %collective-permute-start.8 = (bf16[256,256]{1,0:T(8,128)(2,1)S(1)}, bf16[256,256]{1,0:T(8,128)(2,1)S(1)}, u32[]{:S(2)}, u32[]{:S(2)}) collective-permute-start(bf16[256,256]{1,0:T(8,128)(2,1)S(1)} %add_pair.1), channel_id=1, source_target_pairs={{0,16},{2,18},{4,20},{6,22},{8,24},{10,26},{12,28},{14,30},{16,0},... | collective-permute-start | bytes 393224 | tf_op jit(solution)/shard_map/ppermute | solution.py:572
  55.5 0.0 collective-permute-done.5.refs_2_
  55.5 3.3 %collective-permute-done.6.refs_3_ = bf16[272,256]{1,0:T(8,128)(2,1)S(1)} collective-permute-done((bf16[272,256]{1,0:T(8,128)(2,1)}, bf16[272,256]{1,0:T(8,128)(2,1)S(1)}, u32[]{:S(2)}, u32[]{:S(2)}) %collective-permute-start.6) | collective-permute-done | bytes 139296 | tf_op jit(solution)/shard_map/ppermute | solution.py:572
  58.9 4.4 %collective-permute-done.8.refs_4_ = bf16[256,256]{1,0:T(8,128)(2,1)S(1)} collective-permute-done((bf16[256,256]{1,0:T(8,128)(2,1)S(1)}, bf16[256,256]{1,0:T(8,128)(2,1)S(1)}, u32[]{:S(2)}, u32[]{:S(2)}) %collective-permute-start.8) | collective-permute-done | bytes 131104 | tf_op jit(solution)/shard_map/ppermute | solution.py:572
  63.2 0.0 collective-permute-done.4.refs_1_
  63.2 0.2 sum_groups.1
  63.4 1.5 %collective-permute-start.10 = (bf16[192,256]{1,0:T(8,128)(2,1)S(1)}, bf16[192,256]{1,0:T(8,128)(2,1)S(1)}, u32[]{:S(2)}, u32[]{:S(2)}) collective-permute-start(bf16[192,256]{1,0:T(8,128)(2,1)S(1)} %get-tuple-element.40), channel_id=1, source_target_pairs={{0,4},{2,6},{4,0},{6,2},{8,12},{10,14},{12,8},{14,10},{16,20},{18,... | collective-permute-start | bytes 294920 | tf_op jit(solution)/shard_map/ppermute | solution.py:572
  65.0 0.0 collective-permute-start.11
  65.0 0.7 collective-permute-start.9
  65.6 0.2 own_columns.1.refs_4_
  65.8 2.7 %collective-permute-done.10.refs_2_ = bf16[192,256]{1,0:T(8,128)(2,1)S(1)} collective-permute-done((bf16[192,256]{1,0:T(8,128)(2,1)S(1)}, bf16[192,256]{1,0:T(8,128)(2,1)S(1)}, u32[]{:S(2)}, u32[]{:S(2)}) %collective-permute-start.10) | collective-permute-done | bytes 98336 | tf_op jit(solution)/shard_map/ppermute | solution.py:572
  68.5 1.6 %collective-permute-done.11.refs_3_ = bf16[192,256]{1,0:T(8,128)(2,1)S(1)} collective-permute-done((bf16[192,256]{1,0:T(8,128)(2,1)S(1)}, bf16[192,256]{1,0:T(8,128)(2,1)S(1)}, u32[]{:S(2)}, u32[]{:S(2)}) %collective-permute-start.11) | collective-permute-done | bytes 98336 | tf_op jit(solution)/shard_map/ppermute | solution.py:572
  70.0 0.0 collective-permute-done.9.refs_1_
  70.0 1.2 %finish.1 = (bf16[64,2048]{1,0:T(8,128)(2,1)}, bf16[64,2048]{1,0:T(8,128)(2,1)}) custom-call(s32[1]{0:T(128)} %bitcast.index_ref, bf16[192,256]{1,0:T(8,128)(2,1)S(1)} %get-tuple-element.38.refs_0_, bf16[192,256]{1,0:T(8,128)(2,1)S(1)} %collective-permute-done.9.refs_1_, bf16[192,256]{1,0:T(8,128)(2,1)S(1)} %collective-permute-done.10.refs_2_, ...), custom_call_target="tpu_custom_call" | custom-call | flops 8388608 | bytes 393216 | tf_op jit(solution)/shard_map/finish/pallas_call | solution.py:544
  (1 shorter events, 0.0 us)
Async XLA Ops:
  0.6 18.5 %collective-permute-start = (bf16[256,1024]{1,0:T(8,128)(2,1)}, bf16[256,1024]{1,0:T(8,128)(2,1)S(1)}, u32[]{:S(2)}, u32[]{:S(2)}) collective-permute-start(bf16[256,1024]{1,0:T(8,128)(2,1)} %refs_0_.1), channel_id=1, source_target_pairs={{0,2},{2,0},{4,6},{6,4},{8,10},{10,8},{12,14},{14,12},{16,18},{18,... | collective-permute-start | bytes 1572872 | tf_op jit(solution)/shard_map/ppermute | solution.py:572
  1.1 18.5 %collective-permute-start.2 = (bf16[256,1024]{1,0:T(8,128)(2,1)}, bf16[256,1024]{1,0:T(8,128)(2,1)S(1)}, u32[]{:S(2)}, u32[]{:S(2)}) collective-permute-start(bf16[256,1024]{1,0:T(8,128)(2,1)} %refs_0_.1), channel_id=1, source_target_pairs={{0,4},{2,6},{4,0},{6,2},{8,12},{10,14},{12,8},{14,10},{16,20},{18,... | collective-permute-start | bytes 1572872 | tf_op jit(solution)/shard_map/ppermute | solution.py:572
  5.2 14.0 %all-to-all-start.1 = ((bf16[16,16,384]{2,1,0:T(8,128)(2,1)}), bf16[16,16,384]{2,1,0:T(8,128)(2,1)S(1)}, u32[]{:S(2)}, u32[]{:S(2)}) async-start(bf16[16,16,384]{2,1,0:T(8,128)(2,1)} %teacher_payload.1), calls=%async_computation.1 | async-start | bytes 393216 | tf_op jit(solution)/shard_map/all_to_all | solution.py:561
  19.1 8.1 %copy-start = (bf16[256,1024]{1,0:T(8,128)(2,1)}, bf16[256,1024]{1,0:T(8,128)(2,1)S(1)}, u32[]{:S(2)}) copy-start(bf16[256,1024]{1,0:T(8,128)(2,1)S(1)} %collective-permute-done.refs_1_) | copy-start | bytes 1572868
  19.7 7.6 %copy-start.1 = (bf16[256,1024]{1,0:T(8,128)(2,1)}, bf16[256,1024]{1,0:T(8,128)(2,1)S(1)}, u32[]{:S(2)}) copy-start(bf16[256,1024]{1,0:T(8,128)(2,1)S(1)} %collective-permute-done.2.refs_2_) | copy-start | bytes 1572868
  19.7 7.6 %collective-permute-start.3 = (bf16[256,1024]{1,0:T(8,128)(2,1)S(1)}, bf16[256,1024]{1,0:T(8,128)(2,1)}, u32[]{:S(2)}, u32[]{:S(2)}) collective-permute-start(bf16[256,1024]{1,0:T(8,128)(2,1)S(1)} %collective-permute-done.2.refs_2_), channel_id=1, source_target_pairs={{0,2},{2,0},{4,6},{6,4},{8,10},{10,8},{12,14},{14,12},{16,18},{18,... | collective-permute-start | bytes 1572872 | tf_op jit(solution)/shard_map/ppermute | solution.py:572
  19.8 14.3 %all-to-all-start = ((bf16[32,16,128]{2,1,0:T(8,128)(2,1)}), bf16[32,16,128]{2,1,0:T(8,128)(2,1)S(1)}, u32[]{:S(2)}, u32[]{:S(2)}) async-start(bf16[32,16,128]{2,1,0:T(8,128)(2,1)} %get-tuple-element.24), calls=%async_computation | async-start | bytes 262144 | tf_op jit(solution)/shard_map/all_to_all | solution.py:561
  25.4 7.6 %collective-permute-start.1 = (f32[32,32]{1,0:T(8,128)S(1)}, f32[32,32]{1,0:T(8,128)S(1)}, u32[]{:S(2)}, u32[]{:S(2)}) collective-permute-start(f32[32,32]{1,0:T(8,128)S(1)} %target_gram.1.refs_0_), channel_id=1, source_target_pairs={{0,1},{1,0},{2,3},{3,2},{4,5},{5,4},{6,7},{7,6},{8,9},{9,8},{10,11... | collective-permute-start | bytes 12296 | tf_op jit(solution)/shard_map/ppermute | solution.py:572
  39.5 23.8 %collective-permute-start.4 = (bf16[528,256]{1,0:T(8,128)(2,1)}, bf16[528,256]{1,0:T(8,128)(2,1)S(1)}, u32[]{:S(2)}, u32[]{:S(2)}) collective-permute-start(bf16[528,256]{1,0:T(8,128)(2,1)} %get-tuple-element.33), channel_id=1, source_target_pairs={{0,8},{2,10},{4,12},{6,14},{8,0},{10,2},{12,4},{14,6},{16,24},{18,... | collective-permute-start | bytes 811016 | tf_op jit(solution)/shard_map/ppermute | solution.py:572
  40.1 13.4 %collective-permute-start.7 = (bf16[256,256]{1,0:T(8,128)(2,1)}, bf16[256,256]{1,0:T(8,128)(2,1)S(1)}, u32[]{:S(2)}, u32[]{:S(2)}) collective-permute-start(bf16[256,256]{1,0:T(8,128)(2,1)} %get-tuple-element.37), channel_id=1, source_target_pairs={{0,8},{2,10},{4,12},{6,14},{8,0},{10,2},{12,4},{14,6},{16,24},{18,... | collective-permute-start | bytes 393224 | tf_op jit(solution)/shard_map/ppermute | solution.py:572
  41.6 14.0 %collective-permute-start.5 = (bf16[272,256]{1,0:T(8,128)(2,1)}, bf16[272,256]{1,0:T(8,128)(2,1)S(1)}, u32[]{:S(2)}, u32[]{:S(2)}) collective-permute-start(bf16[272,256]{1,0:T(8,128)(2,1)} %get-tuple-element.34), channel_id=1, source_target_pairs={{0,16},{2,18},{4,20},{6,22},{8,24},{10,26},{12,28},{14,30},{16,0},... | collective-permute-start | bytes 417800 | tf_op jit(solution)/shard_map/ppermute | solution.py:572
  43.0 15.9 %collective-permute-start.6 = (bf16[272,256]{1,0:T(8,128)(2,1)}, bf16[272,256]{1,0:T(8,128)(2,1)S(1)}, u32[]{:S(2)}, u32[]{:S(2)}) collective-permute-start(bf16[272,256]{1,0:T(8,128)(2,1)} %get-tuple-element.35), channel_id=1, source_target_pairs={{0,24},{2,26},{4,28},{6,30},{8,16},{10,18},{12,20},{14,22},{16,8},... | collective-permute-start | bytes 417800 | tf_op jit(solution)/shard_map/ppermute | solution.py:572
  53.5 9.7 %collective-permute-start.8 = (bf16[256,256]{1,0:T(8,128)(2,1)S(1)}, bf16[256,256]{1,0:T(8,128)(2,1)S(1)}, u32[]{:S(2)}, u32[]{:S(2)}) collective-permute-start(bf16[256,256]{1,0:T(8,128)(2,1)S(1)} %add_pair.1), channel_id=1, source_target_pairs={{0,16},{2,18},{4,20},{6,22},{8,24},{10,26},{12,28},{14,30},{16,0},... | collective-permute-start | bytes 393224 | tf_op jit(solution)/shard_map/ppermute | solution.py:572
  63.4 5.0 %collective-permute-start.10 = (bf16[192,256]{1,0:T(8,128)(2,1)S(1)}, bf16[192,256]{1,0:T(8,128)(2,1)S(1)}, u32[]{:S(2)}, u32[]{:S(2)}) collective-permute-start(bf16[192,256]{1,0:T(8,128)(2,1)S(1)} %get-tuple-element.40), channel_id=1, source_target_pairs={{0,4},{2,6},{4,0},{6,2},{8,12},{10,14},{12,8},{14,10},{16,20},{18,... | collective-permute-start | bytes 294920 | tf_op jit(solution)/shard_map/ppermute | solution.py:572
  65.0 5.1 %collective-permute-start.11 = (bf16[192,256]{1,0:T(8,128)(2,1)S(1)}, bf16[192,256]{1,0:T(8,128)(2,1)S(1)}, u32[]{:S(2)}, u32[]{:S(2)}) collective-permute-start(bf16[192,256]{1,0:T(8,128)(2,1)S(1)} %get-tuple-element.41), channel_id=1, source_target_pairs={{0,6},{2,4},{4,2},{6,0},{8,14},{10,12},{12,10},{14,8},{16,22},{18,... | collective-permute-start | bytes 294920 | tf_op jit(solution)/shard_map/ppermute | solution.py:572
  65.0 5.1 %collective-permute-start.9 = (bf16[192,256]{1,0:T(8,128)(2,1)S(1)}, bf16[192,256]{1,0:T(8,128)(2,1)S(1)}, u32[]{:S(2)}, u32[]{:S(2)}) collective-permute-start(bf16[192,256]{1,0:T(8,128)(2,1)S(1)} %get-tuple-element.39), channel_id=1, source_target_pairs={{0,2},{2,0},{4,6},{6,4},{8,10},{10,8},{12,14},{14,12},{16,18},{18,... | collective-permute-start | bytes 294920 | tf_op jit(solution)/shard_map/ppermute | solution.py:572

commit v4 on v3

--- a/solution.py
+++ b/solution.py
@@ -627,11 +627,12 @@
     if paired:
         sends = [
             [(0, j) for j in range(pieces)],
-            [(1, j) for j in range(pieces)],
+            [(1, j) for j in range(half)],
             [(2, j) for j in range(half, pieces)],
             [(3, j) for j in range(half, pieces)],
             [(2, j) for j in range(half)],
             [(3, j) for j in range(half)],
+            [(1, j) for j in range(half, pieces)],
         ]
     else:
         sends = [[(k, j) for j in range(pieces)] for k in range(groups)]
@@ -647,12 +648,15 @@
     ]
     if groups > 1:
         swapped.insert(1, swapped.pop())
-    sources = [[(0, j * group_rows), (1, j * group_rows)] for j in range(pieces)]
     if paired:
         swapped.append(swap(pair, "dp", 2 * mates))
+        swapped.append(swap(parts[groups + 2], "dp", mates))
+        sources = []
         for j in range(pieces):
-            arrays, first = ((4,), 0) if j < half else ((2, 3), half)
-            sources[j] += [(k, (j - first) * group_rows) for k in arrays]
+            arrays, first = ((1, 4), 0) if j < half else ((5, 2, 3), half)
+            sources.append(
+                [(0, j * group_rows)] + [(k, (j - first) * group_rows) for k in arrays]
+            )
     else:
         sources = [[(k, j * group_rows) for k in range(groups)] for j in range(pieces)]
     columns = own_columns(index, dembed, out_rows)

time: 71.7 us -> 71.1 us (level)
  starting transfers between devices: 24.8 us -> 23.2 us
    ppermute x12 -> x13, starting transfers between devices: 14.2 us -> 12.6 us  [swap(): lax.ppermute(value, axis, [(i, i ^ step) for i in range(lax.axis_size(axi...]
    ppermute x12 -> x13, waiting for transfers between devices: 21 us -> 21.5 us  [swap(): lax.ppermute(value, axis, [(i, i ^ step) for i in range(lax.axis_size(axi...]
  transfers between devices with their start and end apart: 14 -> 15, of which waited for: 7 -> 7; matrix products, arithmetic and copies ran while one was open for 0% -> 0% of each run, Pallas kernels for 20% -> 20%
where the time goes in v4:
time: 71.1 us; the launch traced here: 70.6 us
  waiting for transfers between devices  25.1 us (35%)
  starting transfers between devices  23.2 us (33%)
  Pallas kernels  21.6 us (30%)
  between operations  0.79 us (1%)
    ppermute x13, waiting for transfers between devices, swap(): lax.ppermute(value, axis, [(i, i ^ step) for i in range(lax.axis_size(axi...  21.5 us
    ppermute x13, starting transfers between devices, swap(): lax.ppermute(value, axis, [(i, i ^ step) for i in range(lax.axis_size(axi...  12.6 us
    all_to_all x2, starting transfers between devices, exchange(): return lax.all_to_all(blocks, axes, split_axis=0, concat_axis=0, tiled=True)  10.6 us
    pallas_call x1, Pallas kernels, forward(): pl.pallas_call(kernel, in_specs=[pl.BlockSpec(memory_space=pltpu.SMEM)] +...  6.41 us
    pallas_call x1, Pallas kernels, backward(): pl.pallas_call(kernel, in_specs=[smem, whole, whole, whole, whole, in_hbm...  5.85 us
    pallas_call x1, Pallas kernels, mate_slopes(): pl.pallas_call(kernel, grid_spec=pltpu.PrefetchScalarGridSpec(num_scalar_...  5.69 us
    all_to_all x2, waiting for transfers between devices, exchange(): return lax.all_to_all(blocks, axes, split_axis=0, concat_axis=0, tiled=True)  3.53 us
    pallas_call x1, Pallas kernels, teacher_payload(): pl.pallas_call(kernel, in_specs=[pl.BlockSpec(memory_space=pltpu.SMEM), p...  1.44 us
  transfers between devices with their start and end apart: 15, of which 7 were waited for; matrix products, arithmetic and copies ran while one was open for 0% of the time, Pallas kernels for 20%

profile of v4, /device:TPU:0, one launch (start us, length us, event | category | flops | bytes accessed | tf_op | source)
XLA Modules:
  0.0 70.6 jit_solution(14937377512754160327)
XLA Ops:
  0.6 0.5 collective-permute-start
  1.1 2.6 %collective-permute-start.2 = (bf16[256,1024]{1,0:T(8,128)(2,1)}, bf16[256,1024]{1,0:T(8,128)(2,1)S(1)}, u32[]{:S(2)}, u32[]{:S(2)}) collective-permute-start(bf16[256,1024]{1,0:T(8,128)(2,1)} %refs_0_.1), channel_id=1, source_target_pairs={{0,4},{2,6},{4,0},{6,2},{8,12},{10,14},{12,8},{14,10},{16,20},{18,... | collective-permute-start | bytes 1572872 | tf_op jit(solution)/shard_map/ppermute | solution.py:572
  3.7 1.4 %teacher_payload.1 = bf16[16,16,384]{2,1,0:T(8,128)(2,1)} custom-call(s32[1]{0:T(128)} %bitcast.1.first_ref, bf16[2,6144]{1,0:T(2,128)(2,1)} %teacher_ref.1), custom_call_target="tpu_custom_call" | custom-call | flops 98304 | bytes 196608 | tf_op jit(solution)/shard_map/teacher_payload/pallas_call | solution.py:83
  5.2 5.0 %all-to-all-start.1 = ((bf16[16,16,384]{2,1,0:T(8,128)(2,1)}), bf16[16,16,384]{2,1,0:T(8,128)(2,1)S(1)}, u32[]{:S(2)}, u32[]{:S(2)}) async-start(bf16[16,16,384]{2,1,0:T(8,128)(2,1)} %teacher_payload.1), calls=%async_computation.1 | async-start | bytes 393216 | tf_op jit(solution)/shard_map/all_to_all | solution.py:561
  10.1 6.4 %forward.1 = (bf16[2,2048]{1,0:T(2,128)(2,1)S(1)}, bf16[32,16,128]{2,1,0:T(8,128)(2,1)}) custom-call(s32[1]{0:T(128)} %bitcast.1.first_ref, f32[1,1024]{1,0:T(1,128)} %bitcast.9, f32[1,2048]{1,0:T(1,128)} %bitcast.7, f32[1,1024]{1,0:T(1,128)} %bitcast.11, bf16[256,1024]{1,0:T(8,128)(2,1)} %refs_0_.1, bf16[1024,2048]{1,0:T(8,128)(2,1)} %refs_6_.1, ...), custom_call_target="tpu_custom_call" | custom-call | flops 1073741824 | bytes 8388608 | tf_op jit(solution)/shard_map/forward/pallas_call | solution.py:142
  16.6 2.6 %all-to-all-done.1.arrived_ref = bf16[16,16,384]{2,1,0:T(8,128)(2,1)S(1)} async-done(((bf16[16,16,384]{2,1,0:T(8,128)(2,1)}), bf16[16,16,384]{2,1,0:T(8,128)(2,1)S(1)}, u32[]{:S(2)}, u32[]{:S(2)}) %all-to-all-start.1) | async-done | bytes 196640 | tf_op jit(solution)/shard_map/all_to_all | solution.py:561
  19.1 0.0 collective-permute-done.refs_1_
  19.1 0.0 copy-start
  19.1 0.5 target_gram.1.refs_0_
  19.7 0.0 collective-permute-done.2.refs_2_
  19.7 0.0 copy-start.1
  19.7 0.1 collective-permute-start.3
  19.8 5.6 %all-to-all-start = ((bf16[32,16,128]{2,1,0:T(8,128)(2,1)}), bf16[32,16,128]{2,1,0:T(8,128)(2,1)S(1)}, u32[]{:S(2)}, u32[]{:S(2)}) async-start(bf16[32,16,128]{2,1,0:T(8,128)(2,1)} %get-tuple-element.25), calls=%async_computation | async-start | bytes 262144 | tf_op jit(solution)/shard_map/all_to_all | solution.py:561
  25.4 1.8 %collective-permute-start.1 = (f32[32,32]{1,0:T(8,128)S(1)}, f32[32,32]{1,0:T(8,128)S(1)}, u32[]{:S(2)}, u32[]{:S(2)}) collective-permute-start(f32[32,32]{1,0:T(8,128)S(1)} %target_gram.1.refs_0_), channel_id=1, source_target_pairs={{0,1},{1,0},{2,3},{3,2},{4,5},{5,4},{6,7},{7,6},{8,9},{9,8},{10,11... | collective-permute-start | bytes 12296 | tf_op jit(solution)/shard_map/ppermute | solution.py:572
  27.3 0.0 copy-done
  27.3 0.0 copy-done.1
  27.3 0.0 collective-permute-done.3.refs_3_
  27.3 5.7 %mate_slopes.1 = (bf16[1024,512]{1,0:T(8,128)(2,1)S(1)}, bf16[1024,1024]{1,0:T(8,128)(2,1)S(1)}) custom-call(s32[1]{0:T(128)S(6)} %select_n.7.index_ref, bf16[256,1024]{1,0:T(8,128)(2,1)} %refs_0_.1, bf16[256,1024]{1,0:T(8,128)(2,1)} %copy-done, bf16[256,1024]{1,0:T(8,128)(2,1)} %copy-done.1, bf16[256,1024]{1,0:T(8,128)(2,1)} %collective-permute-done.3.refs_3_, ...), custom_call_target="tpu_custom_call" | custom-call | flops 1073741824 | bytes 4194304 | tf_op jit(solution)/shard_map/mate_slopes/pallas_call | solution.py:201
  33.0 0.0 collective-permute-done.1.refs_1_
  33.0 0.1 unit_gram.1.gram_ref
  33.1 1.0 %all-to-all-done.arrived_ref = bf16[32,16,128]{2,1,0:T(8,128)(2,1)S(1)} async-done(((bf16[32,16,128]{2,1,0:T(8,128)(2,1)}), bf16[32,16,128]{2,1,0:T(8,128)(2,1)S(1)}, u32[]{:S(2)}, u32[]{:S(2)}) %all-to-all-start) | async-done | bytes 131104 | tf_op jit(solution)/shard_map/all_to_all | solution.py:561
  34.0 5.9 %backward.1 = (f32[1,1]{1,0:T(1,128)}, bf16[32,1024]{1,0:T(8,128)(2,1)S(1)}, bf16[528,256]{1,0:T(8,128)(2,1)S(1)}, bf16[272,256]{1,0:T(8,128)(2,1)}, bf16[272,25...) custom-call(s32[1]{0:T(128)} %bitcast.index_ref, ...), custom_call_target="tpu_custom_call" | custom-call | flops 1073741824 | bytes 3145728 | tf_op jit(solution)/shard_map/backward/pallas_call | solution.py:401
  39.9 0.6 collective-permute-start.7
  40.5 1.5 %collective-permute-start.4 = (bf16[272,256]{1,0:T(8,128)(2,1)}, bf16[272,256]{1,0:T(8,128)(2,1)S(1)}, u32[]{:S(2)}, u32[]{:S(2)}) collective-permute-start(bf16[272,256]{1,0:T(8,128)(2,1)} %get-tuple-element.34), channel_id=1, source_target_pairs={{0,8},{2,10},{4,12},{6,14},{8,0},{10,2},{12,4},{14,6},{16,24},{18,... | collective-permute-start | bytes 417800 | tf_op jit(solution)/shard_map/ppermute | solution.py:572
  42.0 1.4 %collective-permute-start.5 = (bf16[272,256]{1,0:T(8,128)(2,1)}, bf16[272,256]{1,0:T(8,128)(2,1)S(1)}, u32[]{:S(2)}, u32[]{:S(2)}) collective-permute-start(bf16[272,256]{1,0:T(8,128)(2,1)} %get-tuple-element.35), channel_id=1, source_target_pairs={{0,16},{2,18},{4,20},{6,22},{8,24},{10,26},{12,28},{14,30},{16,0},... | collective-permute-start | bytes 417800 | tf_op jit(solution)/shard_map/ppermute | solution.py:572
  43.4 1.4 %collective-permute-start.6 = (bf16[272,256]{1,0:T(8,128)(2,1)}, bf16[272,256]{1,0:T(8,128)(2,1)S(1)}, u32[]{:S(2)}, u32[]{:S(2)}) collective-permute-start(bf16[272,256]{1,0:T(8,128)(2,1)} %get-tuple-element.36), channel_id=1, source_target_pairs={{0,24},{2,26},{4,28},{6,30},{8,16},{10,18},{12,20},{14,22},{16,8},... | collective-permute-start | bytes 417800 | tf_op jit(solution)/shard_map/ppermute | solution.py:572
  44.9 0.6 collective-permute-start.9
  45.5 3.5 %collective-permute-done.7.arrived_ref = bf16[256,256]{1,0:T(8,128)(2,1)S(1)} collective-permute-done((bf16[256,256]{1,0:T(8,128)(2,1)}, bf16[256,256]{1,0:T(8,128)(2,1)S(1)}, u32[]{:S(2)}, u32[]{:S(2)}) %collective-permute-start.7) | collective-permute-done | bytes 131104 | tf_op jit(solution)/shard_map/ppermute | solution.py:572
  49.1 0.1 collective-permute-start.8
  49.1 9.1 %collective-permute-done.9.refs_5_ = bf16[256,256]{1,0:T(8,128)(2,1)S(1)} collective-permute-done((bf16[256,256]{1,0:T(8,128)(2,1)}, bf16[256,256]{1,0:T(8,128)(2,1)S(1)}, u32[]{:S(2)}, u32[]{:S(2)}) %collective-permute-start.9) | collective-permute-done | bytes 131104 | tf_op jit(solution)/shard_map/ppermute | solution.py:572
  58.3 0.0 collective-permute-done.4.refs_1_
  58.3 0.0 collective-permute-done.5.refs_2_
  58.3 0.0 collective-permute-done.6.refs_3_
  58.3 4.0 %collective-permute-done.8.refs_4_ = bf16[256,256]{1,0:T(8,128)(2,1)S(1)} collective-permute-done((bf16[256,256]{1,0:T(8,128)(2,1)S(1)}, bf16[256,256]{1,0:T(8,128)(2,1)S(1)}, u32[]{:S(2)}, u32[]{:S(2)}) %collective-permute-start.8) | collective-permute-done | bytes 131104 | tf_op jit(solution)/shard_map/ppermute | solution.py:572
  62.3 0.2 sum_groups.1
  62.5 0.1 collective-permute-start.10
  62.6 1.0 %collective-permute-start.11 = (bf16[192,256]{1,0:T(8,128)(2,1)S(1)}, bf16[192,256]{1,0:T(8,128)(2,1)S(1)}, u32[]{:S(2)}, u32[]{:S(2)}) collective-permute-start(bf16[192,256]{1,0:T(8,128)(2,1)S(1)} %get-tuple-element.42), channel_id=1, source_target_pairs={{0,4},{2,6},{4,0},{6,2},{8,12},{10,14},{12,8},{14,10},{16,20},{18,... | collective-permute-start | bytes 294920 | tf_op jit(solution)/shard_map/ppermute | solution.py:572
  63.6 0.9 %collective-permute-start.12 = (bf16[192,256]{1,0:T(8,128)(2,1)S(1)}, bf16[192,256]{1,0:T(8,128)(2,1)S(1)}, u32[]{:S(2)}, u32[]{:S(2)}) collective-permute-start(bf16[192,256]{1,0:T(8,128)(2,1)S(1)} %get-tuple-element.43), channel_id=1, source_target_pairs={{0,6},{2,4},{4,2},{6,0},{8,14},{10,12},{12,10},{14,8},{16,22},{18,... | collective-permute-start | bytes 294920 | tf_op jit(solution)/shard_map/ppermute | solution.py:572
  64.4 0.2 own_columns.1.refs_4_
  64.6 0.0 collective-permute-done.10.refs_1_
  64.6 3.6 %collective-permute-done.11.refs_2_ = bf16[192,256]{1,0:T(8,128)(2,1)S(1)} collective-permute-done((bf16[192,256]{1,0:T(8,128)(2,1)S(1)}, bf16[192,256]{1,0:T(8,128)(2,1)S(1)}, u32[]{:S(2)}, u32[]{:S(2)}) %collective-permute-start.11) | collective-permute-done | bytes 98336 | tf_op jit(solution)/shard_map/ppermute | solution.py:572
  68.2 1.2 %collective-permute-done.12.refs_3_ = bf16[192,256]{1,0:T(8,128)(2,1)S(1)} collective-permute-done((bf16[192,256]{1,0:T(8,128)(2,1)S(1)}, bf16[192,256]{1,0:T(8,128)(2,1)S(1)}, u32[]{:S(2)}, u32[]{:S(2)}) %collective-permute-start.12) | collective-permute-done | bytes 98336 | tf_op jit(solution)/shard_map/ppermute | solution.py:572
  69.4 1.2 %finish.1 = (bf16[64,2048]{1,0:T(8,128)(2,1)}, bf16[64,2048]{1,0:T(8,128)(2,1)}) custom-call(s32[1]{0:T(128)} %bitcast.index_ref, bf16[192,256]{1,0:T(8,128)(2,1)S(1)} %get-tuple-element.40.refs_0_, bf16[192,256]{1,0:T(8,128)(2,1)S(1)} %collective-permute-done.10.refs_1_, bf16[192,256]{1,0:T(8,128)(2,1)S(1)} %collective-permute-done.11.refs_2_, ...), custom_call_target="tpu_custom_call" | custom-call | flops 8388608 | bytes 393216 | tf_op jit(solution)/shard_map/finish/pallas_call | solution.py:544
  (1 shorter events, 0.0 us)
Async XLA Ops:
  0.6 18.5 %collective-permute-start = (bf16[256,1024]{1,0:T(8,128)(2,1)}, bf16[256,1024]{1,0:T(8,128)(2,1)S(1)}, u32[]{:S(2)}, u32[]{:S(2)}) collective-permute-start(bf16[256,1024]{1,0:T(8,128)(2,1)} %refs_0_.1), channel_id=1, source_target_pairs={{0,2},{2,0},{4,6},{6,4},{8,10},{10,8},{12,14},{14,12},{16,18},{18,... | collective-permute-start | bytes 1572872 | tf_op jit(solution)/shard_map/ppermute | solution.py:572
  1.1 18.5 %collective-permute-start.2 = (bf16[256,1024]{1,0:T(8,128)(2,1)}, bf16[256,1024]{1,0:T(8,128)(2,1)S(1)}, u32[]{:S(2)}, u32[]{:S(2)}) collective-permute-start(bf16[256,1024]{1,0:T(8,128)(2,1)} %refs_0_.1), channel_id=1, source_target_pairs={{0,4},{2,6},{4,0},{6,2},{8,12},{10,14},{12,8},{14,10},{16,20},{18,... | collective-permute-start | bytes 1572872 | tf_op jit(solution)/shard_map/ppermute | solution.py:572
  5.2 14.0 %all-to-all-start.1 = ((bf16[16,16,384]{2,1,0:T(8,128)(2,1)}), bf16[16,16,384]{2,1,0:T(8,128)(2,1)S(1)}, u32[]{:S(2)}, u32[]{:S(2)}) async-start(bf16[16,16,384]{2,1,0:T(8,128)(2,1)} %teacher_payload.1), calls=%async_computation.1 | async-start | bytes 393216 | tf_op jit(solution)/shard_map/all_to_all | solution.py:561
  19.1 8.1 %copy-start = (bf16[256,1024]{1,0:T(8,128)(2,1)}, bf16[256,1024]{1,0:T(8,128)(2,1)S(1)}, u32[]{:S(2)}) copy-start(bf16[256,1024]{1,0:T(8,128)(2,1)S(1)} %collective-permute-done.refs_1_) | copy-start | bytes 1572868
  19.7 7.6 %copy-start.1 = (bf16[256,1024]{1,0:T(8,128)(2,1)}, bf16[256,1024]{1,0:T(8,128)(2,1)S(1)}, u32[]{:S(2)}) copy-start(bf16[256,1024]{1,0:T(8,128)(2,1)S(1)} %collective-permute-done.2.refs_2_) | copy-start | bytes 1572868
  19.7 7.6 %collective-permute-start.3 = (bf16[256,1024]{1,0:T(8,128)(2,1)S(1)}, bf16[256,1024]{1,0:T(8,128)(2,1)}, u32[]{:S(2)}, u32[]{:S(2)}) collective-permute-start(bf16[256,1024]{1,0:T(8,128)(2,1)S(1)} %collective-permute-done.2.refs_2_), channel_id=1, source_target_pairs={{0,2},{2,0},{4,6},{6,4},{8,10},{10,8},{12,14},{14,12},{16,18},{18,... | collective-permute-start | bytes 1572872 | tf_op jit(solution)/shard_map/ppermute | solution.py:572
  19.8 14.3 %all-to-all-start = ((bf16[32,16,128]{2,1,0:T(8,128)(2,1)}), bf16[32,16,128]{2,1,0:T(8,128)(2,1)S(1)}, u32[]{:S(2)}, u32[]{:S(2)}) async-start(bf16[32,16,128]{2,1,0:T(8,128)(2,1)} %get-tuple-element.25), calls=%async_computation | async-start | bytes 262144 | tf_op jit(solution)/shard_map/all_to_all | solution.py:561
  25.4 7.6 %collective-permute-start.1 = (f32[32,32]{1,0:T(8,128)S(1)}, f32[32,32]{1,0:T(8,128)S(1)}, u32[]{:S(2)}, u32[]{:S(2)}) collective-permute-start(f32[32,32]{1,0:T(8,128)S(1)} %target_gram.1.refs_0_), channel_id=1, source_target_pairs={{0,1},{1,0},{2,3},{3,2},{4,5},{5,4},{6,7},{7,6},{8,9},{9,8},{10,11... | collective-permute-start | bytes 12296 | tf_op jit(solution)/shard_map/ppermute | solution.py:572
  39.9 9.1 %collective-permute-start.7 = (bf16[256,256]{1,0:T(8,128)(2,1)}, bf16[256,256]{1,0:T(8,128)(2,1)S(1)}, u32[]{:S(2)}, u32[]{:S(2)}) collective-permute-start(bf16[256,256]{1,0:T(8,128)(2,1)} %get-tuple-element.38), channel_id=1, source_target_pairs={{0,8},{2,10},{4,12},{6,14},{8,0},{10,2},{12,4},{14,6},{16,24},{18,... | collective-permute-start | bytes 393224 | tf_op jit(solution)/shard_map/ppermute | solution.py:572
  40.5 17.8 %collective-permute-start.4 = (bf16[272,256]{1,0:T(8,128)(2,1)}, bf16[272,256]{1,0:T(8,128)(2,1)S(1)}, u32[]{:S(2)}, u32[]{:S(2)}) collective-permute-start(bf16[272,256]{1,0:T(8,128)(2,1)} %get-tuple-element.34), channel_id=1, source_target_pairs={{0,8},{2,10},{4,12},{6,14},{8,0},{10,2},{12,4},{14,6},{16,24},{18,... | collective-permute-start | bytes 417800 | tf_op jit(solution)/shard_map/ppermute | solution.py:572
  42.0 16.3 %collective-permute-start.5 = (bf16[272,256]{1,0:T(8,128)(2,1)}, bf16[272,256]{1,0:T(8,128)(2,1)S(1)}, u32[]{:S(2)}, u32[]{:S(2)}) collective-permute-start(bf16[272,256]{1,0:T(8,128)(2,1)} %get-tuple-element.35), channel_id=1, source_target_pairs={{0,16},{2,18},{4,20},{6,22},{8,24},{10,26},{12,28},{14,30},{16,0},... | collective-permute-start | bytes 417800 | tf_op jit(solution)/shard_map/ppermute | solution.py:572
  43.4 14.8 %collective-permute-start.6 = (bf16[272,256]{1,0:T(8,128)(2,1)}, bf16[272,256]{1,0:T(8,128)(2,1)S(1)}, u32[]{:S(2)}, u32[]{:S(2)}) collective-permute-start(bf16[272,256]{1,0:T(8,128)(2,1)} %get-tuple-element.36), channel_id=1, source_target_pairs={{0,24},{2,26},{4,28},{6,30},{8,16},{10,18},{12,20},{14,22},{16,8},... | collective-permute-start | bytes 417800 | tf_op jit(solution)/shard_map/ppermute | solution.py:572
  44.9 13.4 %collective-permute-start.9 = (bf16[256,256]{1,0:T(8,128)(2,1)}, bf16[256,256]{1,0:T(8,128)(2,1)S(1)}, u32[]{:S(2)}, u32[]{:S(2)}) collective-permute-start(bf16[256,256]{1,0:T(8,128)(2,1)} %get-tuple-element.39), channel_id=1, source_target_pairs={{0,8},{2,10},{4,12},{6,14},{8,0},{10,2},{12,4},{14,6},{16,24},{18,... | collective-permute-start | bytes 393224 | tf_op jit(solution)/shard_map/ppermute | solution.py:572
  49.1 13.2 %collective-permute-start.8 = (bf16[256,256]{1,0:T(8,128)(2,1)S(1)}, bf16[256,256]{1,0:T(8,128)(2,1)S(1)}, u32[]{:S(2)}, u32[]{:S(2)}) collective-permute-start(bf16[256,256]{1,0:T(8,128)(2,1)S(1)} %add_pair.1), channel_id=1, source_target_pairs={{0,16},{2,18},{4,20},{6,22},{8,24},{10,26},{12,28},{14,30},{16,0},... | collective-permute-start | bytes 393224 | tf_op jit(solution)/shard_map/ppermute | solution.py:572
  62.5 2.1 %collective-permute-start.10 = (bf16[192,256]{1,0:T(8,128)(2,1)S(1)}, bf16[192,256]{1,0:T(8,128)(2,1)S(1)}, u32[]{:S(2)}, u32[]{:S(2)}) collective-permute-start(bf16[192,256]{1,0:T(8,128)(2,1)S(1)} %get-tuple-element.41), channel_id=1, source_target_pairs={{0,2},{2,0},{4,6},{6,4},{8,10},{10,8},{12,14},{14,12},{16,18},{18,... | collective-permute-start | bytes 294920 | tf_op jit(solution)/shard_map/ppermute | solution.py:572
  62.6 5.7 %collective-permute-start.11 = (bf16[192,256]{1,0:T(8,128)(2,1)S(1)}, bf16[192,256]{1,0:T(8,128)(2,1)S(1)}, u32[]{:S(2)}, u32[]{:S(2)}) collective-permute-start(bf16[192,256]{1,0:T(8,128)(2,1)S(1)} %get-tuple-element.42), channel_id=1, source_target_pairs={{0,4},{2,6},{4,0},{6,2},{8,12},{10,14},{12,8},{14,10},{16,20},{18,... | collective-permute-start | bytes 294920 | tf_op jit(solution)/shard_map/ppermute | solution.py:572
  63.6 5.9 %collective-permute-start.12 = (bf16[192,256]{1,0:T(8,128)(2,1)S(1)}, bf16[192,256]{1,0:T(8,128)(2,1)S(1)}, u32[]{:S(2)}, u32[]{:S(2)}) collective-permute-start(bf16[192,256]{1,0:T(8,128)(2,1)S(1)} %get-tuple-element.43), channel_id=1, source_target_pairs={{0,6},{2,4},{4,2},{6,0},{8,14},{10,12},{12,10},{14,8},{16,22},{18,... | collective-permute-start | bytes 294920 | tf_op jit(solution)/shard_map/ppermute | solution.py:572

commit v5 on v4

--- a/solution.py
+++ b/solution.py
@@ -650,7 +650,7 @@
         swapped.insert(1, swapped.pop())
     if paired:
         swapped.append(swap(pair, "dp", 2 * mates))
-        swapped.append(swap(parts[groups + 2], "dp", mates))
+        swapped.append(swap(after(parts[groups + 2], swapped[1]), "dp", mates))
         sources = []
         for j in range(pieces):
             arrays, first = ((1, 4), 0) if j < half else ((5, 2, 3), half)

time: 71.1 us -> 71.1 us (level)
  waiting for transfers between devices: 25.1 us -> 22.5 us
  starting transfers between devices: 23.2 us -> 25.7 us
    ppermute x13, waiting for transfers between devices: 21.5 us -> 19 us  [swap(): lax.ppermute(value, axis, [(i, i ^ step) for i in range(lax.axis_size(axi...]
    ppermute x13, starting transfers between devices: 12.6 us -> 15.1 us  [swap(): lax.ppermute(value, axis, [(i, i ^ step) for i in range(lax.axis_size(axi...]
where the time goes in v5:
time: 71.1 us; the launch traced here: 70.6 us
  starting transfers between devices  25.7 us (36%)
  waiting for transfers between devices  22.5 us (32%)
  Pallas kernels  21.6 us (30%)
  between operations  0.78 us (1%)
    ppermute x13, waiting for transfers between devices, swap(): lax.ppermute(value, axis, [(i, i ^ step) for i in range(lax.axis_size(axi...  19 us
    ppermute x13, starting transfers between devices, swap(): lax.ppermute(value, axis, [(i, i ^ step) for i in range(lax.axis_size(axi...  15.1 us
    all_to_all x2, starting transfers between devices, exchange(): return lax.all_to_all(blocks, axes, split_axis=0, concat_axis=0, tiled=True)  10.6 us
    pallas_call x1, Pallas kernels, forward(): pl.pallas_call(kernel, in_specs=[pl.BlockSpec(memory_space=pltpu.SMEM)] +...  6.41 us
    pallas_call x1, Pallas kernels, backward(): pl.pallas_call(kernel, in_specs=[smem, whole, whole, whole, whole, in_hbm...  5.85 us
    pallas_call x1, Pallas kernels, mate_slopes(): pl.pallas_call(kernel, grid_spec=pltpu.PrefetchScalarGridSpec(num_scalar_...  5.69 us
    all_to_all x2, waiting for transfers between devices, exchange(): return lax.all_to_all(blocks, axes, split_axis=0, concat_axis=0, tiled=True)  3.53 us
    pallas_call x1, Pallas kernels, teacher_payload(): pl.pallas_call(kernel, in_specs=[pl.BlockSpec(memory_space=pltpu.SMEM), p...  1.44 us
  transfers between devices with their start and end apart: 15, of which 7 were waited for; matrix products, arithmetic and copies ran while one was open for 0% of the time, Pallas kernels for 20%

profile of v5, /device:TPU:0, one launch (start us, length us, event | category | flops | bytes accessed | tf_op | source)
XLA Modules:
  0.0 70.6 jit_solution(3253269523525729457)
XLA Ops:
  0.6 0.5 collective-permute-start
  1.1 2.6 %collective-permute-start.2 = (bf16[256,1024]{1,0:T(8,128)(2,1)}, bf16[256,1024]{1,0:T(8,128)(2,1)S(1)}, u32[]{:S(2)}, u32[]{:S(2)}) collective-permute-start(bf16[256,1024]{1,0:T(8,128)(2,1)} %refs_0_.1), channel_id=1, source_target_pairs={{0,4},{2,6},{4,0},{6,2},{8,12},{10,14},{12,8},{14,10},{16,20},{18,... | collective-permute-start | bytes 1572872 | tf_op jit(solution)/shard_map/ppermute | solution.py:572
  3.7 1.4 %teacher_payload.1 = bf16[16,16,384]{2,1,0:T(8,128)(2,1)} custom-call(s32[1]{0:T(128)} %bitcast.1.first_ref, bf16[2,6144]{1,0:T(2,128)(2,1)} %teacher_ref.1), custom_call_target="tpu_custom_call" | custom-call | flops 98304 | bytes 196608 | tf_op jit(solution)/shard_map/teacher_payload/pallas_call | solution.py:83
  5.2 5.0 %all-to-all-start.1 = ((bf16[16,16,384]{2,1,0:T(8,128)(2,1)}), bf16[16,16,384]{2,1,0:T(8,128)(2,1)S(1)}, u32[]{:S(2)}, u32[]{:S(2)}) async-start(bf16[16,16,384]{2,1,0:T(8,128)(2,1)} %teacher_payload.1), calls=%async_computation.1 | async-start | bytes 393216 | tf_op jit(solution)/shard_map/all_to_all | solution.py:561
  10.1 6.4 %forward.1 = (bf16[2,2048]{1,0:T(2,128)(2,1)S(1)}, bf16[32,16,128]{2,1,0:T(8,128)(2,1)}) custom-call(s32[1]{0:T(128)} %bitcast.1.first_ref, f32[1,1024]{1,0:T(1,128)} %bitcast.9, f32[1,2048]{1,0:T(1,128)} %bitcast.7, f32[1,1024]{1,0:T(1,128)} %bitcast.11, bf16[256,1024]{1,0:T(8,128)(2,1)} %refs_0_.1, bf16[1024,2048]{1,0:T(8,128)(2,1)} %refs_6_.1, ...), custom_call_target="tpu_custom_call" | custom-call | flops 1073741824 | bytes 8388608 | tf_op jit(solution)/shard_map/forward/pallas_call | solution.py:142
  16.6 2.6 %all-to-all-done.1.arrived_ref = bf16[16,16,384]{2,1,0:T(8,128)(2,1)S(1)} async-done(((bf16[16,16,384]{2,1,0:T(8,128)(2,1)}), bf16[16,16,384]{2,1,0:T(8,128)(2,1)S(1)}, u32[]{:S(2)}, u32[]{:S(2)}) %all-to-all-start.1) | async-done | bytes 196640 | tf_op jit(solution)/shard_map/all_to_all | solution.py:561
  19.1 0.0 collective-permute-done.refs_1_
  19.1 0.0 copy-start
  19.1 0.5 target_gram.1.refs_0_
  19.7 0.0 collective-permute-done.2.refs_2_
  19.7 0.0 copy-start.1
  19.7 0.1 collective-permute-start.3
  19.8 5.6 %all-to-all-start = ((bf16[32,16,128]{2,1,0:T(8,128)(2,1)}), bf16[32,16,128]{2,1,0:T(8,128)(2,1)S(1)}, u32[]{:S(2)}, u32[]{:S(2)}) async-start(bf16[32,16,128]{2,1,0:T(8,128)(2,1)} %get-tuple-element.26), calls=%async_computation | async-start | bytes 262144 | tf_op jit(solution)/shard_map/all_to_all | solution.py:561
  25.4 1.8 %collective-permute-start.1 = (f32[32,32]{1,0:T(8,128)S(1)}, f32[32,32]{1,0:T(8,128)S(1)}, u32[]{:S(2)}, u32[]{:S(2)}) collective-permute-start(f32[32,32]{1,0:T(8,128)S(1)} %target_gram.1.refs_0_), channel_id=1, source_target_pairs={{0,1},{1,0},{2,3},{3,2},{4,5},{5,4},{6,7},{7,6},{8,9},{9,8},{10,11... | collective-permute-start | bytes 12296 | tf_op jit(solution)/shard_map/ppermute | solution.py:572
  27.3 0.0 copy-done
  27.3 0.0 copy-done.1
  27.3 0.0 collective-permute-done.3.refs_3_
  27.3 5.7 %mate_slopes.1 = (bf16[1024,512]{1,0:T(8,128)(2,1)S(1)}, bf16[1024,1024]{1,0:T(8,128)(2,1)S(1)}) custom-call(s32[1]{0:T(128)S(6)} %select_n.7.index_ref, bf16[256,1024]{1,0:T(8,128)(2,1)} %refs_0_.1, bf16[256,1024]{1,0:T(8,128)(2,1)} %copy-done, bf16[256,1024]{1,0:T(8,128)(2,1)} %copy-done.1, bf16[256,1024]{1,0:T(8,128)(2,1)} %collective-permute-done.3.refs_3_, ...), custom_call_target="tpu_custom_call" | custom-call | flops 1073741824 | bytes 4194304 | tf_op jit(solution)/shard_map/mate_slopes/pallas_call | solution.py:201
  33.0 0.0 collective-permute-done.1.refs_1_
  33.0 0.1 unit_gram.1.gram_ref
  33.1 1.0 %all-to-all-done.arrived_ref = bf16[32,16,128]{2,1,0:T(8,128)(2,1)S(1)} async-done(((bf16[32,16,128]{2,1,0:T(8,128)(2,1)}), bf16[32,16,128]{2,1,0:T(8,128)(2,1)S(1)}, u32[]{:S(2)}, u32[]{:S(2)}) %all-to-all-start) | async-done | bytes 131104 | tf_op jit(solution)/shard_map/all_to_all | solution.py:561
  34.0 5.9 %backward.1 = (f32[1,1]{1,0:T(1,128)}, bf16[32,1024]{1,0:T(8,128)(2,1)S(1)}, bf16[528,256]{1,0:T(8,128)(2,1)S(1)}, bf16[272,256]{1,0:T(8,128)(2,1)}, bf16[272,25...) custom-call(s32[1]{0:T(128)} %bitcast.index_ref, ...), custom_call_target="tpu_custom_call" | custom-call | flops 1073741824 | bytes 3145728 | tf_op jit(solution)/shard_map/backward/pallas_call | solution.py:401
  39.9 0.6 collective-permute-start.4
  40.5 1.5 %collective-permute-start.7 = (bf16[256,256]{1,0:T(8,128)(2,1)}, bf16[256,256]{1,0:T(8,128)(2,1)S(1)}, u32[]{:S(2)}, u32[]{:S(2)}) collective-permute-start(bf16[256,256]{1,0:T(8,128)(2,1)} %get-tuple-element.39), channel_id=1, source_target_pairs={{0,8},{2,10},{4,12},{6,14},{8,0},{10,2},{12,4},{14,6},{16,24},{18,... | collective-permute-start | bytes 393224 | tf_op jit(solution)/shard_map/ppermute | solution.py:572
  42.0 1.4 %collective-permute-start.5 = (bf16[272,256]{1,0:T(8,128)(2,1)}, bf16[272,256]{1,0:T(8,128)(2,1)S(1)}, u32[]{:S(2)}, u32[]{:S(2)}) collective-permute-start(bf16[272,256]{1,0:T(8,128)(2,1)} %get-tuple-element.36), channel_id=1, source_target_pairs={{0,16},{2,18},{4,20},{6,22},{8,24},{10,26},{12,28},{14,30},{16,0},... | collective-permute-start | bytes 417800 | tf_op jit(solution)/shard_map/ppermute | solution.py:572
  43.4 1.4 %collective-permute-start.6 = (bf16[272,256]{1,0:T(8,128)(2,1)}, bf16[272,256]{1,0:T(8,128)(2,1)S(1)}, u32[]{:S(2)}, u32[]{:S(2)}) collective-permute-start(bf16[272,256]{1,0:T(8,128)(2,1)} %get-tuple-element.37), channel_id=1, source_target_pairs={{0,24},{2,26},{4,28},{6,30},{8,16},{10,18},{12,20},{14,22},{16,8},... | collective-permute-start | bytes 417800 | tf_op jit(solution)/shard_map/ppermute | solution.py:572
  44.9 6.2 %collective-permute-done.7.arrived_ref = bf16[256,256]{1,0:T(8,128)(2,1)S(1)} collective-permute-done((bf16[256,256]{1,0:T(8,128)(2,1)}, bf16[256,256]{1,0:T(8,128)(2,1)S(1)}, u32[]{:S(2)}, u32[]{:S(2)}) %collective-permute-start.7) | collective-permute-done | bytes 131104 | tf_op jit(solution)/shard_map/ppermute | solution.py:572
  51.1 0.6 collective-permute-start.8
  51.8 0.0 collective-permute-done.4.refs_1_
  51.8 2.5 %collective-permute-start.9 = (bf16[256,256]{1,0:T(8,128)(2,1)}, bf16[256,256]{1,0:T(8,128)(2,1)S(1)}, u32[]{:S(2)}, u32[]{:S(2)}) collective-permute-start(bf16[256,256]{1,0:T(8,128)(2,1)} %get-tuple-element.41), channel_id=1, source_target_pairs={{0,8},{2,10},{4,12},{6,14},{8,0},{10,2},{12,4},{14,6},{16,24},{18,... | collective-permute-start | bytes 393224 | tf_op jit(solution)/shard_map/ppermute | solution.py:572
  54.3 0.0 collective-permute-done.5.refs_2_
  54.3 2.2 %collective-permute-done.6.refs_3_ = bf16[272,256]{1,0:T(8,128)(2,1)S(1)} collective-permute-done((bf16[272,256]{1,0:T(8,128)(2,1)}, bf16[272,256]{1,0:T(8,128)(2,1)S(1)}, u32[]{:S(2)}, u32[]{:S(2)}) %collective-permute-start.6) | collective-permute-done | bytes 139296 | tf_op jit(solution)/shard_map/ppermute | solution.py:572
  56.5 5.8 %collective-permute-done.8.refs_4_ = bf16[256,256]{1,0:T(8,128)(2,1)S(1)} collective-permute-done((bf16[256,256]{1,0:T(8,128)(2,1)S(1)}, bf16[256,256]{1,0:T(8,128)(2,1)S(1)}, u32[]{:S(2)}, u32[]{:S(2)}) %collective-permute-start.8) | collective-permute-done | bytes 131104 | tf_op jit(solution)/shard_map/ppermute | solution.py:572
  62.3 0.0 collective-permute-done.9.refs_5_
  62.3 0.2 sum_groups.1
  62.5 0.1 collective-permute-start.10
  62.5 1.0 %collective-permute-start.11 = (bf16[192,256]{1,0:T(8,128)(2,1)S(1)}, bf16[192,256]{1,0:T(8,128)(2,1)S(1)}, u32[]{:S(2)}, u32[]{:S(2)}) collective-permute-start(bf16[192,256]{1,0:T(8,128)(2,1)S(1)} %get-tuple-element.44), channel_id=1, source_target_pairs={{0,4},{2,6},{4,0},{6,2},{8,12},{10,14},{12,8},{14,10},{16,20},{18,... | collective-permute-start | bytes 294920 | tf_op jit(solution)/shard_map/ppermute | solution.py:572
  63.6 0.8 %collective-permute-start.12 = (bf16[192,256]{1,0:T(8,128)(2,1)S(1)}, bf16[192,256]{1,0:T(8,128)(2,1)S(1)}, u32[]{:S(2)}, u32[]{:S(2)}) collective-permute-start(bf16[192,256]{1,0:T(8,128)(2,1)S(1)} %get-tuple-element.45), channel_id=1, source_target_pairs={{0,6},{2,4},{4,2},{6,0},{8,14},{10,12},{12,10},{14,8},{16,22},{18,... | collective-permute-start | bytes 294920 | tf_op jit(solution)/shard_map/ppermute | solution.py:572
  64.4 0.2 own_columns.1.refs_4_
  64.6 0.0 collective-permute-done.10.refs_1_
  64.6 3.6 %collective-permute-done.11.refs_2_ = bf16[192,256]{1,0:T(8,128)(2,1)S(1)} collective-permute-done((bf16[192,256]{1,0:T(8,128)(2,1)S(1)}, bf16[192,256]{1,0:T(8,128)(2,1)S(1)}, u32[]{:S(2)}, u32[]{:S(2)}) %collective-permute-start.11) | collective-permute-done | bytes 98336 | tf_op jit(solution)/shard_map/ppermute | solution.py:572
  68.2 1.2 %collective-permute-done.12.refs_3_ = bf16[192,256]{1,0:T(8,128)(2,1)S(1)} collective-permute-done((bf16[192,256]{1,0:T(8,128)(2,1)S(1)}, bf16[192,256]{1,0:T(8,128)(2,1)S(1)}, u32[]{:S(2)}, u32[]{:S(2)}) %collective-permute-start.12) | collective-permute-done | bytes 98336 | tf_op jit(solution)/shard_map/ppermute | solution.py:572
  69.4 1.2 %finish.1 = (bf16[64,2048]{1,0:T(8,128)(2,1)}, bf16[64,2048]{1,0:T(8,128)(2,1)}) custom-call(s32[1]{0:T(128)} %bitcast.index_ref, bf16[192,256]{1,0:T(8,128)(2,1)S(1)} %get-tuple-element.42.refs_0_, bf16[192,256]{1,0:T(8,128)(2,1)S(1)} %collective-permute-done.10.refs_1_, bf16[192,256]{1,0:T(8,128)(2,1)S(1)} %collective-permute-done.11.refs_2_, ...), custom_call_target="tpu_custom_call" | custom-call | flops 8388608 | bytes 393216 | tf_op jit(solution)/shard_map/finish/pallas_call | solution.py:544
  (1 shorter events, 0.0 us)
Async XLA Ops:
  0.6 18.5 %collective-permute-start = (bf16[256,1024]{1,0:T(8,128)(2,1)}, bf16[256,1024]{1,0:T(8,128)(2,1)S(1)}, u32[]{:S(2)}, u32[]{:S(2)}) collective-permute-start(bf16[256,1024]{1,0:T(8,128)(2,1)} %refs_0_.1), channel_id=1, source_target_pairs={{0,2},{2,0},{4,6},{6,4},{8,10},{10,8},{12,14},{14,12},{16,18},{18,... | collective-permute-start | bytes 1572872 | tf_op jit(solution)/shard_map/ppermute | solution.py:572
  1.1 18.5 %collective-permute-start.2 = (bf16[256,1024]{1,0:T(8,128)(2,1)}, bf16[256,1024]{1,0:T(8,128)(2,1)S(1)}, u32[]{:S(2)}, u32[]{:S(2)}) collective-permute-start(bf16[256,1024]{1,0:T(8,128)(2,1)} %refs_0_.1), channel_id=1, source_target_pairs={{0,4},{2,6},{4,0},{6,2},{8,12},{10,14},{12,8},{14,10},{16,20},{18,... | collective-permute-start | bytes 1572872 | tf_op jit(solution)/shard_map/ppermute | solution.py:572
  5.2 14.0 %all-to-all-start.1 = ((bf16[16,16,384]{2,1,0:T(8,128)(2,1)}), bf16[16,16,384]{2,1,0:T(8,128)(2,1)S(1)}, u32[]{:S(2)}, u32[]{:S(2)}) async-start(bf16[16,16,384]{2,1,0:T(8,128)(2,1)} %teacher_payload.1), calls=%async_computation.1 | async-start | bytes 393216 | tf_op jit(solution)/shard_map/all_to_all | solution.py:561
  19.1 8.1 %copy-start = (bf16[256,1024]{1,0:T(8,128)(2,1)}, bf16[256,1024]{1,0:T(8,128)(2,1)S(1)}, u32[]{:S(2)}) copy-start(bf16[256,1024]{1,0:T(8,128)(2,1)S(1)} %collective-permute-done.refs_1_) | copy-start | bytes 1572868
  19.7 7.6 %copy-start.1 = (bf16[256,1024]{1,0:T(8,128)(2,1)}, bf16[256,1024]{1,0:T(8,128)(2,1)S(1)}, u32[]{:S(2)}) copy-start(bf16[256,1024]{1,0:T(8,128)(2,1)S(1)} %collective-permute-done.2.refs_2_) | copy-start | bytes 1572868
  19.7 7.6 %collective-permute-start.3 = (bf16[256,1024]{1,0:T(8,128)(2,1)S(1)}, bf16[256,1024]{1,0:T(8,128)(2,1)}, u32[]{:S(2)}, u32[]{:S(2)}) collective-permute-start(bf16[256,1024]{1,0:T(8,128)(2,1)S(1)} %collective-permute-done.2.refs_2_), channel_id=1, source_target_pairs={{0,2},{2,0},{4,6},{6,4},{8,10},{10,8},{12,14},{14,12},{16,18},{18,... | collective-permute-start | bytes 1572872 | tf_op jit(solution)/shard_map/ppermute | solution.py:572
  19.8 14.3 %all-to-all-start = ((bf16[32,16,128]{2,1,0:T(8,128)(2,1)}), bf16[32,16,128]{2,1,0:T(8,128)(2,1)S(1)}, u32[]{:S(2)}, u32[]{:S(2)}) async-start(bf16[32,16,128]{2,1,0:T(8,128)(2,1)} %get-tuple-element.26), calls=%async_computation | async-start | bytes 262144 | tf_op jit(solution)/shard_map/all_to_all | solution.py:561
  25.4 7.6 %collective-permute-start.1 = (f32[32,32]{1,0:T(8,128)S(1)}, f32[32,32]{1,0:T(8,128)S(1)}, u32[]{:S(2)}, u32[]{:S(2)}) collective-permute-start(f32[32,32]{1,0:T(8,128)S(1)} %target_gram.1.refs_0_), channel_id=1, source_target_pairs={{0,1},{1,0},{2,3},{3,2},{4,5},{5,4},{6,7},{7,6},{8,9},{9,8},{10,11... | collective-permute-start | bytes 12296 | tf_op jit(solution)/shard_map/ppermute | solution.py:572
  39.9 11.9 %collective-permute-start.4 = (bf16[272,256]{1,0:T(8,128)(2,1)}, bf16[272,256]{1,0:T(8,128)(2,1)S(1)}, u32[]{:S(2)}, u32[]{:S(2)}) collective-permute-start(bf16[272,256]{1,0:T(8,128)(2,1)} %get-tuple-element.35), channel_id=1, source_target_pairs={{0,8},{2,10},{4,12},{6,14},{8,0},{10,2},{12,4},{14,6},{16,24},{18,... | collective-permute-start | bytes 417800 | tf_op jit(solution)/shard_map/ppermute | solution.py:572
  40.5 10.6 %collective-permute-start.7 = (bf16[256,256]{1,0:T(8,128)(2,1)}, bf16[256,256]{1,0:T(8,128)(2,1)S(1)}, u32[]{:S(2)}, u32[]{:S(2)}) collective-permute-start(bf16[256,256]{1,0:T(8,128)(2,1)} %get-tuple-element.39), channel_id=1, source_target_pairs={{0,8},{2,10},{4,12},{6,14},{8,0},{10,2},{12,4},{14,6},{16,24},{18,... | collective-permute-start | bytes 393224 | tf_op jit(solution)/shard_map/ppermute | solution.py:572
  42.0 12.3 %collective-permute-start.5 = (bf16[272,256]{1,0:T(8,128)(2,1)}, bf16[272,256]{1,0:T(8,128)(2,1)S(1)}, u32[]{:S(2)}, u32[]{:S(2)}) collective-permute-start(bf16[272,256]{1,0:T(8,128)(2,1)} %get-tuple-element.36), channel_id=1, source_target_pairs={{0,16},{2,18},{4,20},{6,22},{8,24},{10,26},{12,28},{14,30},{16,0},... | collective-permute-start | bytes 417800 | tf_op jit(solution)/shard_map/ppermute | solution.py:572
  43.4 13.1 %collective-permute-start.6 = (bf16[272,256]{1,0:T(8,128)(2,1)}, bf16[272,256]{1,0:T(8,128)(2,1)S(1)}, u32[]{:S(2)}, u32[]{:S(2)}) collective-permute-start(bf16[272,256]{1,0:T(8,128)(2,1)} %get-tuple-element.37), channel_id=1, source_target_pairs={{0,24},{2,26},{4,28},{6,30},{8,16},{10,18},{12,20},{14,22},{16,8},... | collective-permute-start | bytes 417800 | tf_op jit(solution)/shard_map/ppermute | solution.py:572
  51.1 11.2 %collective-permute-start.8 = (bf16[256,256]{1,0:T(8,128)(2,1)S(1)}, bf16[256,256]{1,0:T(8,128)(2,1)S(1)}, u32[]{:S(2)}, u32[]{:S(2)}) collective-permute-start(bf16[256,256]{1,0:T(8,128)(2,1)S(1)} %add_pair.1), channel_id=1, source_target_pairs={{0,16},{2,18},{4,20},{6,22},{8,24},{10,26},{12,28},{14,30},{16,0},... | collective-permute-start | bytes 393224 | tf_op jit(solution)/shard_map/ppermute | solution.py:572
  51.8 10.5 %collective-permute-start.9 = (bf16[256,256]{1,0:T(8,128)(2,1)}, bf16[256,256]{1,0:T(8,128)(2,1)S(1)}, u32[]{:S(2)}, u32[]{:S(2)}) collective-permute-start(bf16[256,256]{1,0:T(8,128)(2,1)} %get-tuple-element.41), channel_id=1, source_target_pairs={{0,8},{2,10},{4,12},{6,14},{8,0},{10,2},{12,4},{14,6},{16,24},{18,... | collective-permute-start | bytes 393224 | tf_op jit(solution)/shard_map/ppermute | solution.py:572
  62.5 2.1 %collective-permute-start.10 = (bf16[192,256]{1,0:T(8,128)(2,1)S(1)}, bf16[192,256]{1,0:T(8,128)(2,1)S(1)}, u32[]{:S(2)}, u32[]{:S(2)}) collective-permute-start(bf16[192,256]{1,0:T(8,128)(2,1)S(1)} %get-tuple-element.43), channel_id=1, source_target_pairs={{0,2},{2,0},{4,6},{6,4},{8,10},{10,8},{12,14},{14,12},{16,18},{18,... | collective-permute-start | bytes 294920 | tf_op jit(solution)/shard_map/ppermute | solution.py:572
  62.5 5.7 %collective-permute-start.11 = (bf16[192,256]{1,0:T(8,128)(2,1)S(1)}, bf16[192,256]{1,0:T(8,128)(2,1)S(1)}, u32[]{:S(2)}, u32[]{:S(2)}) collective-permute-start(bf16[192,256]{1,0:T(8,128)(2,1)S(1)} %get-tuple-element.44), channel_id=1, source_target_pairs={{0,4},{2,6},{4,0},{6,2},{8,12},{10,14},{12,8},{14,10},{16,20},{18,... | collective-permute-start | bytes 294920 | tf_op jit(solution)/shard_map/ppermute | solution.py:572
  63.6 5.8 %collective-permute-start.12 = (bf16[192,256]{1,0:T(8,128)(2,1)S(1)}, bf16[192,256]{1,0:T(8,128)(2,1)S(1)}, u32[]{:S(2)}, u32[]{:S(2)}) collective-permute-start(bf16[192,256]{1,0:T(8,128)(2,1)S(1)} %get-tuple-element.45), channel_id=1, source_target_pairs={{0,6},{2,4},{4,2},{6,0},{8,14},{10,12},{12,10},{14,8},{16,22},{18,... | collective-permute-start | bytes 294920 | tf_op jit(solution)/shard_map/ppermute | solution.py:572

commit v6 on v5

--- a/solution.py
+++ b/solution.py
@@ -118,9 +118,10 @@
         loads.append(pltpu.make_async_copy(out_any_ref, out_w_ref, sems.at[steps]))
         loads.append(pltpu.make_async_copy(tokens_any, tokens_ref, sems.at[steps + 1]))
         loads[-1].start()
-        for load in loads[:-1]:
+        for load in loads[:steps]:
             load.start()
         loads[-1].wait()
+        loads[steps].start()
         values = tokens_ref[...].astype(f32)
         normed = normalize(values, gain_ref[...])
         token_mean = jnp.mean(values.reshape(images, per_image, width), axis=1)

time: 71.1 us -> 71.1 us (level)
  no operation moved by 1% of the time
where the time goes in v6:
time: 71.1 us; the launch traced here: 70.6 us
  starting transfers between devices  25.7 us (36%)
  waiting for transfers between devices  22.4 us (32%)
  Pallas kernels  21.7 us (31%)
  between operations  0.78 us (1%)
    ppermute x13, waiting for transfers between devices, swap(): lax.ppermute(value, axis, [(i, i ^ step) for i in range(lax.axis_size(axi...  19 us
    ppermute x13, starting transfers between devices, swap(): lax.ppermute(value, axis, [(i, i ^ step) for i in range(lax.axis_size(axi...  15.1 us
    all_to_all x2, starting transfers between devices, exchange(): return lax.all_to_all(blocks, axes, split_axis=0, concat_axis=0, tiled=True)  10.6 us
    pallas_call x1, Pallas kernels, forward(): pl.pallas_call(kernel, in_specs=[pl.BlockSpec(memory_space=pltpu.SMEM)] +...  6.52 us
    pallas_call x1, Pallas kernels, backward(): pl.pallas_call(kernel, in_specs=[smem, whole, whole, whole, whole, in_hbm...  5.85 us
    pallas_call x1, Pallas kernels, mate_slopes(): pl.pallas_call(kernel, grid_spec=pltpu.PrefetchScalarGridSpec(num_scalar_...  5.69 us
    all_to_all x2, waiting for transfers between devices, exchange(): return lax.all_to_all(blocks, axes, split_axis=0, concat_axis=0, tiled=True)  3.43 us
    pallas_call x1, Pallas kernels, teacher_payload(): pl.pallas_call(kernel, in_specs=[pl.BlockSpec(memory_space=pltpu.SMEM), p...  1.44 us
  transfers between devices with their start and end apart: 15, of which 7 were waited for; matrix products, arithmetic and copies ran while one was open for 0% of the time, Pallas kernels for 20%

profile of v6, /device:TPU:0, one launch (start us, length us, event | category | flops | bytes accessed | tf_op | source)
XLA Modules:
  0.0 70.6 jit_solution(3095372194778492893)
XLA Ops:
  0.6 0.5 collective-permute-start
  1.1 2.6 %collective-permute-start.2 = (bf16[256,1024]{1,0:T(8,128)(2,1)}, bf16[256,1024]{1,0:T(8,128)(2,1)S(1)}, u32[]{:S(2)}, u32[]{:S(2)}) collective-permute-start(bf16[256,1024]{1,0:T(8,128)(2,1)} %refs_0_.1), channel_id=1, source_target_pairs={{0,4},{2,6},{4,0},{6,2},{8,12},{10,14},{12,8},{14,10},{16,20},{18,... | collective-permute-start | bytes 1572872 | tf_op jit(solution)/shard_map/ppermute | solution.py:573
  3.7 1.4 %teacher_payload.1 = bf16[16,16,384]{2,1,0:T(8,128)(2,1)} custom-call(s32[1]{0:T(128)} %bitcast.1.first_ref, bf16[2,6144]{1,0:T(2,128)(2,1)} %teacher_ref.1), custom_call_target="tpu_custom_call" | custom-call | flops 98304 | bytes 196608 | tf_op jit(solution)/shard_map/teacher_payload/pallas_call | solution.py:83
  5.2 5.0 %all-to-all-start.1 = ((bf16[16,16,384]{2,1,0:T(8,128)(2,1)}), bf16[16,16,384]{2,1,0:T(8,128)(2,1)S(1)}, u32[]{:S(2)}, u32[]{:S(2)}) async-start(bf16[16,16,384]{2,1,0:T(8,128)(2,1)} %teacher_payload.1), calls=%async_computation.1 | async-start | bytes 393216 | tf_op jit(solution)/shard_map/all_to_all | solution.py:562
  10.1 6.5 %forward.1 = (bf16[2,2048]{1,0:T(2,128)(2,1)S(1)}, bf16[32,16,128]{2,1,0:T(8,128)(2,1)}) custom-call(s32[1]{0:T(128)} %bitcast.1.first_ref, f32[1,1024]{1,0:T(1,128)} %bitcast.9, f32[1,2048]{1,0:T(1,128)} %bitcast.7, f32[1,1024]{1,0:T(1,128)} %bitcast.11, bf16[256,1024]{1,0:T(8,128)(2,1)} %refs_0_.1, bf16[1024,2048]{1,0:T(8,128)(2,1)} %refs_6_.1, ...), custom_call_target="tpu_custom_call" | custom-call | flops 1073741824 | bytes 8388608 | tf_op jit(solution)/shard_map/forward/pallas_call | solution.py:143
  16.7 2.5 %all-to-all-done.1.arrived_ref = bf16[16,16,384]{2,1,0:T(8,128)(2,1)S(1)} async-done(((bf16[16,16,384]{2,1,0:T(8,128)(2,1)}), bf16[16,16,384]{2,1,0:T(8,128)(2,1)S(1)}, u32[]{:S(2)}, u32[]{:S(2)}) %all-to-all-start.1) | async-done | bytes 196640 | tf_op jit(solution)/shard_map/all_to_all | solution.py:562
  19.1 0.0 collective-permute-done.refs_1_
  19.1 0.0 copy-start
  19.1 0.5 target_gram.1.refs_0_
  19.7 0.0 collective-permute-done.2.refs_2_
  19.7 0.0 copy-start.1
  19.7 0.1 collective-permute-start.3
  19.8 5.6 %all-to-all-start = ((bf16[32,16,128]{2,1,0:T(8,128)(2,1)}), bf16[32,16,128]{2,1,0:T(8,128)(2,1)S(1)}, u32[]{:S(2)}, u32[]{:S(2)}) async-start(bf16[32,16,128]{2,1,0:T(8,128)(2,1)} %get-tuple-element.26), calls=%async_computation | async-start | bytes 262144 | tf_op jit(solution)/shard_map/all_to_all | solution.py:562
  25.4 1.8 %collective-permute-start.1 = (f32[32,32]{1,0:T(8,128)S(1)}, f32[32,32]{1,0:T(8,128)S(1)}, u32[]{:S(2)}, u32[]{:S(2)}) collective-permute-start(f32[32,32]{1,0:T(8,128)S(1)} %target_gram.1.refs_0_), channel_id=1, source_target_pairs={{0,1},{1,0},{2,3},{3,2},{4,5},{5,4},{6,7},{7,6},{8,9},{9,8},{10,11... | collective-permute-start | bytes 12296 | tf_op jit(solution)/shard_map/ppermute | solution.py:573
  27.3 0.0 copy-done
  27.3 0.0 copy-done.1
  27.3 0.0 collective-permute-done.3.refs_3_
  27.3 5.7 %mate_slopes.1 = (bf16[1024,512]{1,0:T(8,128)(2,1)S(1)}, bf16[1024,1024]{1,0:T(8,128)(2,1)S(1)}) custom-call(s32[1]{0:T(128)S(6)} %select_n.7.index_ref, bf16[256,1024]{1,0:T(8,128)(2,1)} %refs_0_.1, bf16[256,1024]{1,0:T(8,128)(2,1)} %copy-done, bf16[256,1024]{1,0:T(8,128)(2,1)} %copy-done.1, bf16[256,1024]{1,0:T(8,128)(2,1)} %collective-permute-done.3.refs_3_, ...), custom_call_target="tpu_custom_call" | custom-call | flops 1073741824 | bytes 4194304 | tf_op jit(solution)/shard_map/mate_slopes/pallas_call | solution.py:202
  33.0 0.0 collective-permute-done.1.refs_1_
  33.0 0.1 unit_gram.1.gram_ref
  33.1 1.0 %all-to-all-done.arrived_ref = bf16[32,16,128]{2,1,0:T(8,128)(2,1)S(1)} async-done(((bf16[32,16,128]{2,1,0:T(8,128)(2,1)}), bf16[32,16,128]{2,1,0:T(8,128)(2,1)S(1)}, u32[]{:S(2)}, u32[]{:S(2)}) %all-to-all-start) | async-done | bytes 131104 | tf_op jit(solution)/shard_map/all_to_all | solution.py:562
  34.0 5.9 %backward.1 = (f32[1,1]{1,0:T(1,128)}, bf16[32,1024]{1,0:T(8,128)(2,1)S(1)}, bf16[528,256]{1,0:T(8,128)(2,1)S(1)}, bf16[272,256]{1,0:T(8,128)(2,1)}, bf16[272,25...) custom-call(s32[1]{0:T(128)} %bitcast.index_ref, ...), custom_call_target="tpu_custom_call" | custom-call | flops 1073741824 | bytes 3145728 | tf_op jit(solution)/shard_map/backward/pallas_call | solution.py:402
  39.9 0.6 collective-permute-start.4
  40.5 1.5 %collective-permute-start.7 = (bf16[256,256]{1,0:T(8,128)(2,1)}, bf16[256,256]{1,0:T(8,128)(2,1)S(1)}, u32[]{:S(2)}, u32[]{:S(2)}) collective-permute-start(bf16[256,256]{1,0:T(8,128)(2,1)} %get-tuple-element.39), channel_id=1, source_target_pairs={{0,8},{2,10},{4,12},{6,14},{8,0},{10,2},{12,4},{14,6},{16,24},{18,... | collective-permute-start | bytes 393224 | tf_op jit(solution)/shard_map/ppermute | solution.py:573
  42.0 1.4 %collective-permute-start.5 = (bf16[272,256]{1,0:T(8,128)(2,1)}, bf16[272,256]{1,0:T(8,128)(2,1)S(1)}, u32[]{:S(2)}, u32[]{:S(2)}) collective-permute-start(bf16[272,256]{1,0:T(8,128)(2,1)} %get-tuple-element.36), channel_id=1, source_target_pairs={{0,16},{2,18},{4,20},{6,22},{8,24},{10,26},{12,28},{14,30},{16,0},... | collective-permute-start | bytes 417800 | tf_op jit(solution)/shard_map/ppermute | solution.py:573
  43.4 1.4 %collective-permute-start.6 = (bf16[272,256]{1,0:T(8,128)(2,1)}, bf16[272,256]{1,0:T(8,128)(2,1)S(1)}, u32[]{:S(2)}, u32[]{:S(2)}) collective-permute-start(bf16[272,256]{1,0:T(8,128)(2,1)} %get-tuple-element.37), channel_id=1, source_target_pairs={{0,24},{2,26},{4,28},{6,30},{8,16},{10,18},{12,20},{14,22},{16,8},... | collective-permute-start | bytes 417800 | tf_op jit(solution)/shard_map/ppermute | solution.py:573
  44.9 6.2 %collective-permute-done.7.arrived_ref = bf16[256,256]{1,0:T(8,128)(2,1)S(1)} collective-permute-done((bf16[256,256]{1,0:T(8,128)(2,1)}, bf16[256,256]{1,0:T(8,128)(2,1)S(1)}, u32[]{:S(2)}, u32[]{:S(2)}) %collective-permute-start.7) | collective-permute-done | bytes 131104 | tf_op jit(solution)/shard_map/ppermute | solution.py:573
  51.1 0.6 collective-permute-start.8
  51.8 0.0 collective-permute-done.4.refs_1_
  51.8 2.5 %collective-permute-start.9 = (bf16[256,256]{1,0:T(8,128)(2,1)}, bf16[256,256]{1,0:T(8,128)(2,1)S(1)}, u32[]{:S(2)}, u32[]{:S(2)}) collective-permute-start(bf16[256,256]{1,0:T(8,128)(2,1)} %get-tuple-element.41), channel_id=1, source_target_pairs={{0,8},{2,10},{4,12},{6,14},{8,0},{10,2},{12,4},{14,6},{16,24},{18,... | collective-permute-start | bytes 393224 | tf_op jit(solution)/shard_map/ppermute | solution.py:573
  54.3 0.0 collective-permute-done.5.refs_2_
  54.3 2.2 %collective-permute-done.6.refs_3_ = bf16[272,256]{1,0:T(8,128)(2,1)S(1)} collective-permute-done((bf16[272,256]{1,0:T(8,128)(2,1)}, bf16[272,256]{1,0:T(8,128)(2,1)S(1)}, u32[]{:S(2)}, u32[]{:S(2)}) %collective-permute-start.6) | collective-permute-done | bytes 139296 | tf_op jit(solution)/shard_map/ppermute | solution.py:573
  56.5 5.8 %collective-permute-done.8.refs_4_ = bf16[256,256]{1,0:T(8,128)(2,1)S(1)} collective-permute-done((bf16[256,256]{1,0:T(8,128)(2,1)S(1)}, bf16[256,256]{1,0:T(8,128)(2,1)S(1)}, u32[]{:S(2)}, u32[]{:S(2)}) %collective-permute-start.8) | collective-permute-done | bytes 131104 | tf_op jit(solution)/shard_map/ppermute | solution.py:573
  62.3 0.0 collective-permute-done.9.refs_5_
  62.3 0.2 sum_groups.1
  62.5 0.1 collective-permute-start.10
  62.5 1.0 %collective-permute-start.11 = (bf16[192,256]{1,0:T(8,128)(2,1)S(1)}, bf16[192,256]{1,0:T(8,128)(2,1)S(1)}, u32[]{:S(2)}, u32[]{:S(2)}) collective-permute-start(bf16[192,256]{1,0:T(8,128)(2,1)S(1)} %get-tuple-element.44), channel_id=1, source_target_pairs={{0,4},{2,6},{4,0},{6,2},{8,12},{10,14},{12,8},{14,10},{16,20},{18,... | collective-permute-start | bytes 294920 | tf_op jit(solution)/shard_map/ppermute | solution.py:573
  63.6 0.8 %collective-permute-start.12 = (bf16[192,256]{1,0:T(8,128)(2,1)S(1)}, bf16[192,256]{1,0:T(8,128)(2,1)S(1)}, u32[]{:S(2)}, u32[]{:S(2)}) collective-permute-start(bf16[192,256]{1,0:T(8,128)(2,1)S(1)} %get-tuple-element.45), channel_id=1, source_target_pairs={{0,6},{2,4},{4,2},{6,0},{8,14},{10,12},{12,10},{14,8},{16,22},{18,... | collective-permute-start | bytes 294920 | tf_op jit(solution)/shard_map/ppermute | solution.py:573
  64.4 0.2 own_columns.1.refs_4_
  64.6 0.0 collective-permute-done.10.refs_1_
  64.6 3.6 %collective-permute-done.11.refs_2_ = bf16[192,256]{1,0:T(8,128)(2,1)S(1)} collective-permute-done((bf16[192,256]{1,0:T(8,128)(2,1)S(1)}, bf16[192,256]{1,0:T(8,128)(2,1)S(1)}, u32[]{:S(2)}, u32[]{:S(2)}) %collective-permute-start.11) | collective-permute-done | bytes 98336 | tf_op jit(solution)/shard_map/ppermute | solution.py:573
  68.2 1.2 %collective-permute-done.12.refs_3_ = bf16[192,256]{1,0:T(8,128)(2,1)S(1)} collective-permute-done((bf16[192,256]{1,0:T(8,128)(2,1)S(1)}, bf16[192,256]{1,0:T(8,128)(2,1)S(1)}, u32[]{:S(2)}, u32[]{:S(2)}) %collective-permute-start.12) | collective-permute-done | bytes 98336 | tf_op jit(solution)/shard_map/ppermute | solution.py:573
  69.4 1.2 %finish.1 = (bf16[64,2048]{1,0:T(8,128)(2,1)}, bf16[64,2048]{1,0:T(8,128)(2,1)}) custom-call(s32[1]{0:T(128)} %bitcast.index_ref, bf16[192,256]{1,0:T(8,128)(2,1)S(1)} %get-tuple-element.42.refs_0_, bf16[192,256]{1,0:T(8,128)(2,1)S(1)} %collective-permute-done.10.refs_1_, bf16[192,256]{1,0:T(8,128)(2,1)S(1)} %collective-permute-done.11.refs_2_, ...), custom_call_target="tpu_custom_call" | custom-call | flops 8388608 | bytes 393216 | tf_op jit(solution)/shard_map/finish/pallas_call | solution.py:545
  (1 shorter events, 0.0 us)
Async XLA Ops:
  0.6 18.5 %collective-permute-start = (bf16[256,1024]{1,0:T(8,128)(2,1)}, bf16[256,1024]{1,0:T(8,128)(2,1)S(1)}, u32[]{:S(2)}, u32[]{:S(2)}) collective-permute-start(bf16[256,1024]{1,0:T(8,128)(2,1)} %refs_0_.1), channel_id=1, source_target_pairs={{0,2},{2,0},{4,6},{6,4},{8,10},{10,8},{12,14},{14,12},{16,18},{18,... | collective-permute-start | bytes 1572872 | tf_op jit(solution)/shard_map/ppermute | solution.py:573
  1.1 18.5 %collective-permute-start.2 = (bf16[256,1024]{1,0:T(8,128)(2,1)}, bf16[256,1024]{1,0:T(8,128)(2,1)S(1)}, u32[]{:S(2)}, u32[]{:S(2)}) collective-permute-start(bf16[256,1024]{1,0:T(8,128)(2,1)} %refs_0_.1), channel_id=1, source_target_pairs={{0,4},{2,6},{4,0},{6,2},{8,12},{10,14},{12,8},{14,10},{16,20},{18,... | collective-permute-start | bytes 1572872 | tf_op jit(solution)/shard_map/ppermute | solution.py:573
  5.2 14.0 %all-to-all-start.1 = ((bf16[16,16,384]{2,1,0:T(8,128)(2,1)}), bf16[16,16,384]{2,1,0:T(8,128)(2,1)S(1)}, u32[]{:S(2)}, u32[]{:S(2)}) async-start(bf16[16,16,384]{2,1,0:T(8,128)(2,1)} %teacher_payload.1), calls=%async_computation.1 | async-start | bytes 393216 | tf_op jit(solution)/shard_map/all_to_all | solution.py:562
  19.1 8.1 %copy-start = (bf16[256,1024]{1,0:T(8,128)(2,1)}, bf16[256,1024]{1,0:T(8,128)(2,1)S(1)}, u32[]{:S(2)}) copy-start(bf16[256,1024]{1,0:T(8,128)(2,1)S(1)} %collective-permute-done.refs_1_) | copy-start | bytes 1572868
  19.7 7.6 %copy-start.1 = (bf16[256,1024]{1,0:T(8,128)(2,1)}, bf16[256,1024]{1,0:T(8,128)(2,1)S(1)}, u32[]{:S(2)}) copy-start(bf16[256,1024]{1,0:T(8,128)(2,1)S(1)} %collective-permute-done.2.refs_2_) | copy-start | bytes 1572868
  19.7 7.6 %collective-permute-start.3 = (bf16[256,1024]{1,0:T(8,128)(2,1)S(1)}, bf16[256,1024]{1,0:T(8,128)(2,1)}, u32[]{:S(2)}, u32[]{:S(2)}) collective-permute-start(bf16[256,1024]{1,0:T(8,128)(2,1)S(1)} %collective-permute-done.2.refs_2_), channel_id=1, source_target_pairs={{0,2},{2,0},{4,6},{6,4},{8,10},{10,8},{12,14},{14,12},{16,18},{18,... | collective-permute-start | bytes 1572872 | tf_op jit(solution)/shard_map/ppermute | solution.py:573
  19.8 14.3 %all-to-all-start = ((bf16[32,16,128]{2,1,0:T(8,128)(2,1)}), bf16[32,16,128]{2,1,0:T(8,128)(2,1)S(1)}, u32[]{:S(2)}, u32[]{:S(2)}) async-start(bf16[32,16,128]{2,1,0:T(8,128)(2,1)} %get-tuple-element.26), calls=%async_computation | async-start | bytes 262144 | tf_op jit(solution)/shard_map/all_to_all | solution.py:562
  25.4 7.6 %collective-permute-start.1 = (f32[32,32]{1,0:T(8,128)S(1)}, f32[32,32]{1,0:T(8,128)S(1)}, u32[]{:S(2)}, u32[]{:S(2)}) collective-permute-start(f32[32,32]{1,0:T(8,128)S(1)} %target_gram.1.refs_0_), channel_id=1, source_target_pairs={{0,1},{1,0},{2,3},{3,2},{4,5},{5,4},{6,7},{7,6},{8,9},{9,8},{10,11... | collective-permute-start | bytes 12296 | tf_op jit(solution)/shard_map/ppermute | solution.py:573
  39.9 11.9 %collective-permute-start.4 = (bf16[272,256]{1,0:T(8,128)(2,1)}, bf16[272,256]{1,0:T(8,128)(2,1)S(1)}, u32[]{:S(2)}, u32[]{:S(2)}) collective-permute-start(bf16[272,256]{1,0:T(8,128)(2,1)} %get-tuple-element.35), channel_id=1, source_target_pairs={{0,8},{2,10},{4,12},{6,14},{8,0},{10,2},{12,4},{14,6},{16,24},{18,... | collective-permute-start | bytes 417800 | tf_op jit(solution)/shard_map/ppermute | solution.py:573
  40.5 10.6 %collective-permute-start.7 = (bf16[256,256]{1,0:T(8,128)(2,1)}, bf16[256,256]{1,0:T(8,128)(2,1)S(1)}, u32[]{:S(2)}, u32[]{:S(2)}) collective-permute-start(bf16[256,256]{1,0:T(8,128)(2,1)} %get-tuple-element.39), channel_id=1, source_target_pairs={{0,8},{2,10},{4,12},{6,14},{8,0},{10,2},{12,4},{14,6},{16,24},{18,... | collective-permute-start | bytes 393224 | tf_op jit(solution)/shard_map/ppermute | solution.py:573
  42.0 12.3 %collective-permute-start.5 = (bf16[272,256]{1,0:T(8,128)(2,1)}, bf16[272,256]{1,0:T(8,128)(2,1)S(1)}, u32[]{:S(2)}, u32[]{:S(2)}) collective-permute-start(bf16[272,256]{1,0:T(8,128)(2,1)} %get-tuple-element.36), channel_id=1, source_target_pairs={{0,16},{2,18},{4,20},{6,22},{8,24},{10,26},{12,28},{14,30},{16,0},... | collective-permute-start | bytes 417800 | tf_op jit(solution)/shard_map/ppermute | solution.py:573
  43.4 13.1 %collective-permute-start.6 = (bf16[272,256]{1,0:T(8,128)(2,1)}, bf16[272,256]{1,0:T(8,128)(2,1)S(1)}, u32[]{:S(2)}, u32[]{:S(2)}) collective-permute-start(bf16[272,256]{1,0:T(8,128)(2,1)} %get-tuple-element.37), channel_id=1, source_target_pairs={{0,24},{2,26},{4,28},{6,30},{8,16},{10,18},{12,20},{14,22},{16,8},... | collective-permute-start | bytes 417800 | tf_op jit(solution)/shard_map/ppermute | solution.py:573
  51.1 11.2 %collective-permute-start.8 = (bf16[256,256]{1,0:T(8,128)(2,1)S(1)}, bf16[256,256]{1,0:T(8,128)(2,1)S(1)}, u32[]{:S(2)}, u32[]{:S(2)}) collective-permute-start(bf16[256,256]{1,0:T(8,128)(2,1)S(1)} %add_pair.1), channel_id=1, source_target_pairs={{0,16},{2,18},{4,20},{6,22},{8,24},{10,26},{12,28},{14,30},{16,0},... | collective-permute-start | bytes 393224 | tf_op jit(solution)/shard_map/ppermute | solution.py:573
  51.8 10.5 %collective-permute-start.9 = (bf16[256,256]{1,0:T(8,128)(2,1)}, bf16[256,256]{1,0:T(8,128)(2,1)S(1)}, u32[]{:S(2)}, u32[]{:S(2)}) collective-permute-start(bf16[256,256]{1,0:T(8,128)(2,1)} %get-tuple-element.41), channel_id=1, source_target_pairs={{0,8},{2,10},{4,12},{6,14},{8,0},{10,2},{12,4},{14,6},{16,24},{18,... | collective-permute-start | bytes 393224 | tf_op jit(solution)/shard_map/ppermute | solution.py:573
  62.5 2.1 %collective-permute-start.10 = (bf16[192,256]{1,0:T(8,128)(2,1)S(1)}, bf16[192,256]{1,0:T(8,128)(2,1)S(1)}, u32[]{:S(2)}, u32[]{:S(2)}) collective-permute-start(bf16[192,256]{1,0:T(8,128)(2,1)S(1)} %get-tuple-element.43), channel_id=1, source_target_pairs={{0,2},{2,0},{4,6},{6,4},{8,10},{10,8},{12,14},{14,12},{16,18},{18,... | collective-permute-start | bytes 294920 | tf_op jit(solution)/shard_map/ppermute | solution.py:573
  62.5 5.7 %collective-permute-start.11 = (bf16[192,256]{1,0:T(8,128)(2,1)S(1)}, bf16[192,256]{1,0:T(8,128)(2,1)S(1)}, u32[]{:S(2)}, u32[]{:S(2)}) collective-permute-start(bf16[192,256]{1,0:T(8,128)(2,1)S(1)} %get-tuple-element.44), channel_id=1, source_target_pairs={{0,4},{2,6},{4,0},{6,2},{8,12},{10,14},{12,8},{14,10},{16,20},{18,... | collective-permute-start | bytes 294920 | tf_op jit(solution)/shard_map/ppermute | solution.py:573
  63.6 5.8 %collective-permute-start.12 = (bf16[192,256]{1,0:T(8,128)(2,1)S(1)}, bf16[192,256]{1,0:T(8,128)(2,1)S(1)}, u32[]{:S(2)}, u32[]{:S(2)}) collective-permute-start(bf16[192,256]{1,0:T(8,128)(2,1)S(1)} %get-tuple-element.45), channel_id=1, source_target_pairs={{0,6},{2,4},{4,2},{6,0},{8,14},{10,12},{12,10},{14,8},{16,22},{18,... | collective-permute-start | bytes 294920 | tf_op jit(solution)/shard_map/ppermute | solution.py:573
